TPU v7x, 32 devices: a whole 2x2x4 slice. The times are simulated.
32 devices in a mesh: seq: 16 (over z, y, core), head: 2 (over x).
Axes of the slice: x: 2, y: 2, z: 4, core: 2. Of those that a mesh axis runs over, the one named last changes fastest.
Arguments:
- queries: bfloat16 [2048, 6144], P('seq', 'head'), may hold values from -5 to 5
- key_rows: bfloat16 [2048, 6144], P('seq', 'head'), may hold values from -5 to 5
- value_rows: bfloat16 [2048, 6144], P('seq', 'head'), may hold values from -6 to 6
- out_grad: bfloat16 [2048, 6144], P('seq', 'head'), may hold values from -6 to 6
- partner: int32 [32, 48, 2], P('seq', 'head'), may hold values from 0 to 31, as said below
Outputs:
- query_gradient: bfloat16 [2048, 6144], P(('seq', 'head'))
- key_grad: bfloat16 [2048, 6144], P(('seq', 'head'))
- value_grad: bfloat16 [2048, 6144], P(('seq', 'head'))
Inputs may be any that keep to these rules, and one draw needn't show every extreme that they name: `partner`: each entry is o * 2 + j for an owner o of the seq axis and a block j of it. Among the 96 entries of the rows of one device (its query blocks and its heads), at most 9 have the same owner; in every draw one owner, the same for all devices of one index of head, gets exactly 9 entries from each of them.
All inputs are finite; a program needn't handle non-finite values.
Results may differ from a plain program's by a relative error of at most 0.012.
Values may be sent and summed in bfloat16 or wider, within the bound.
A program may use at most 128 MiB of HBM per device.

v0:
```python
import math

import jax
import jax.numpy as jnp
from jax import lax
from jax.sharding import PartitionSpec as P


def padded(x, sides, width):
    for axis, dim in sides:
        size, length = (lax.axis_size(axis), x.shape[dim])
        up = [(i, (i + 1) % size) for i in range(size - 1)]
        down = [(j, i) for i, j in up]
        last = lax.slice_in_dim(x, length - width, length, axis=dim)
        first = lax.slice_in_dim(x, 0, width, axis=dim)
        before = lax.ppermute(last, axis, up)
        after = lax.ppermute(first, axis, down)
        x = jnp.concatenate([before, x, after], axis=dim)
    return x


def shifted(value, axis, steps):
    count = lax.axis_size(axis)
    first, last = (max(0, -steps), min(count, count - steps))
    return lax.ppermute(value, axis, [(source, source + steps) for source in range(first, last)])


def block_items(matrix, block_count, block_size, head_count, head_size):
    shaped = matrix.reshape(block_count, block_size, head_count, head_size)
    return shaped.transpose(0, 2, 1, 3).reshape(block_count * head_count, block_size, head_size)


def local(queries, key_rows, value_rows, out_grad, partner):
    seq_devices = lax.axis_size("seq")
    seq_index = lax.axis_index("seq")
    token_count, row_width = queries.shape
    block_count, head_count, random_count = partner.shape
    block_size = token_count // block_count
    head_size = row_width // head_count
    similarity_multiplier = 1.0 / math.sqrt(head_size)
    item_count = block_count * head_count * random_count
    capacity = max(2, (3 * item_count + 2 * seq_devices - 1) // (2 * seq_devices))
    slot_count = seq_devices * capacity
    wanted_blocks = partner.reshape(item_count)
    owner_ids = wanted_blocks // block_count
    item_order = jnp.arange(item_count, dtype=jnp.int32)
    earlier = (owner_ids[None, :] == owner_ids[:, None]) & (
        item_order[None, :] < item_order[:, None]
    )
    item_rank = jnp.sum(earlier.astype(jnp.int32), axis=1)
    item_slot = owner_ids * capacity + item_rank
    head_ids = jnp.broadcast_to(
        jnp.arange(head_count, dtype=jnp.int32)[None, :, None],
        (block_count, head_count, random_count),
    ).reshape(item_count)
    item_code = wanted_blocks % block_count * head_count + head_ids
    wanted = jnp.full((slot_count,), -1, jnp.int32).at[item_slot].set(item_code)
    asked_codes = lax.all_to_all(
        wanted.reshape(seq_devices, capacity), "seq", split_axis=0, concat_axis=0, tiled=True
    ).reshape(slot_count)
    own_items = jnp.concatenate(
        [
            block_items(key_rows, block_count, block_size, head_count, head_size),
            block_items(value_rows, block_count, block_size, head_count, head_size),
        ],
        axis=2,
    )
    outgoing = own_items[jnp.maximum(asked_codes, 0)]
    fetched = lax.all_to_all(
        outgoing.reshape(seq_devices, capacity, block_size, 2 * head_size),
        "seq",
        split_axis=0,
        concat_axis=0,
        tiled=True,
    )
    fetched = fetched.reshape(slot_count, block_size, 2 * head_size)
    remote = fetched[item_slot].reshape(
        block_count, head_count, random_count * block_size, 2 * head_size
    )
    random_keys = remote[..., :head_size]
    random_values = remote[..., head_size:]
    key_value = jnp.concatenate([key_rows, value_rows], axis=1)
    extended = padded(key_value, (("seq", 0),), block_size)
    extended = extended.reshape(block_count + 2, block_size, 2, head_count, head_size)
    window = jnp.concatenate([extended[:-2], extended[1:-1], extended[2:]], axis=1)
    window_keys = window[:, :, 0]
    window_values = window[:, :, 1]
    window_size = 3 * block_size
    query_blocks = queries.reshape(block_count, block_size, head_count, head_size)
    grad_blocks = out_grad.reshape(block_count, block_size, head_count, head_size)
    logit_scores = jnp.concatenate(
        [
            jnp.einsum(
                "bqhd,bkhd->bhqk", query_blocks, window_keys, preferred_element_type=jnp.float32
            ),
            jnp.einsum(
                "bqhd,bhkd->bhqk", query_blocks, random_keys, preferred_element_type=jnp.float32
            ),
        ],
        axis=3,
    )
    logit_scores = similarity_multiplier * logit_scores
    block_ids = seq_index * block_count + jnp.arange(block_count, dtype=jnp.int32)
    total_blocks = block_count * seq_devices
    filled = jnp.ones((block_count, block_size), jnp.bool_)
    allowed = jnp.concatenate(
        [
            filled & (block_ids > 0)[:, None],
            filled,
            filled & (block_ids < total_blocks - 1)[:, None],
            jnp.ones((block_count, random_count * block_size), jnp.bool_),
        ],
        axis=1,
    )
    logit_scores = jnp.where(allowed[:, None, None, :], logit_scores, -jnp.inf)
    row_max = jnp.max(logit_scores, axis=3, keepdims=True)
    log_total = row_max + jnp.log(jnp.sum(jnp.exp(logit_scores - row_max), axis=3, keepdims=True))
    weights = jnp.exp(logit_scores - log_total)
    reduced_precision_probabilities = weights.astype(jnp.bfloat16)
    attended_output = jnp.einsum(
        "bhqk,bkhd->bqhd",
        reduced_precision_probabilities[..., :window_size],
        window_values,
        preferred_element_type=jnp.float32,
    )
    attended_output = attended_output + jnp.einsum(
        "bhqk,bhkd->bqhd",
        reduced_precision_probabilities[..., window_size:],
        random_values,
        preferred_element_type=jnp.float32,
    )
    attended_output = lax.optimization_barrier(attended_output.astype(jnp.bfloat16))
    row_delta = jnp.sum(
        grad_blocks.astype(jnp.float32) * attended_output.astype(jnp.float32), axis=3
    ).transpose(0, 2, 1)[..., None]
    weight_gradient = jnp.concatenate(
        [
            jnp.einsum(
                "bqhd,bkhd->bhqk", grad_blocks, window_values, preferred_element_type=jnp.float32
            ),
            jnp.einsum(
                "bqhd,bhkd->bhqk", grad_blocks, random_values, preferred_element_type=jnp.float32
            ),
        ],
        axis=3,
    )
    similarity_derivative = (weights * (weight_gradient - row_delta)).astype(jnp.bfloat16)
    query_gradient = jnp.einsum(
        "bhqk,bkhd->bqhd",
        similarity_derivative[..., :window_size],
        window_keys,
        preferred_element_type=jnp.float32,
    )
    query_gradient = similarity_multiplier * (
        query_gradient
        + jnp.einsum(
            "bhqk,bhkd->bqhd",
            similarity_derivative[..., window_size:],
            random_keys,
            preferred_element_type=jnp.float32,
        )
    )
    window_key_grad = similarity_multiplier * jnp.einsum(
        "bhqk,bqhd->bkhd",
        similarity_derivative[..., :window_size],
        query_blocks,
        preferred_element_type=jnp.float32,
    )
    window_value_grad = jnp.einsum(
        "bhqk,bqhd->bkhd",
        reduced_precision_probabilities[..., :window_size],
        grad_blocks,
        preferred_element_type=jnp.float32,
    )
    window_terms = jnp.stack([window_key_grad, window_value_grad], axis=2).reshape(
        block_count, 3, block_size, 2 * row_width
    )
    zero_rows = jnp.zeros((1, block_size, 2 * row_width), jnp.float32)
    spread = jnp.concatenate([window_terms[:, 0], zero_rows, zero_rows], axis=0)
    spread = spread + jnp.concatenate([zero_rows, window_terms[:, 1], zero_rows], axis=0)
    spread = spread + jnp.concatenate([zero_rows, zero_rows, window_terms[:, 2]], axis=0)
    from_below = shifted(spread[0].astype(jnp.bfloat16), "seq", -1).astype(jnp.float32)
    from_above = shifted(spread[-1].astype(jnp.bfloat16), "seq", 1).astype(jnp.float32)
    local_grads = spread[1:-1]
    local_grads = local_grads.at[0].add(from_above)
    local_grads = local_grads.at[-1].add(from_below)
    random_key_grad = similarity_multiplier * jnp.einsum(
        "bhqk,bqhd->bhkd",
        similarity_derivative[..., window_size:],
        query_blocks,
        preferred_element_type=jnp.float32,
    )
    random_value_grad = jnp.einsum(
        "bhqk,bqhd->bhkd",
        reduced_precision_probabilities[..., window_size:],
        grad_blocks,
        preferred_element_type=jnp.float32,
    )
    random_terms = jnp.concatenate([random_key_grad, random_value_grad], axis=3).reshape(
        item_count, block_size, 2 * head_size
    )
    outbound = (
        jnp.zeros((slot_count, block_size, 2 * head_size), jnp.float32)
        .at[item_slot]
        .set(random_terms)
    )
    inbound = lax.all_to_all(
        outbound.reshape(seq_devices, capacity, block_size, 2 * head_size).astype(jnp.bfloat16),
        "seq",
        split_axis=0,
        concat_axis=0,
        tiled=True,
    ).astype(jnp.float32)
    inbound = inbound.reshape(slot_count, block_size, 2 * head_size)
    segment_ids = jnp.where(asked_codes >= 0, asked_codes, block_count * head_count)
    summed = jax.ops.segment_sum(inbound, segment_ids, num_segments=block_count * head_count + 1)[
        :-1
    ]
    summed = (
        summed.reshape(block_count, head_count, block_size, 2, head_size)
        .transpose(0, 2, 3, 1, 4)
        .reshape(block_count, block_size, 2 * row_width)
    )
    joined_grads = local_grads + summed
    query_rows = query_gradient.reshape(token_count, row_width).astype(jnp.bfloat16)
    key_grad_rows = (
        joined_grads[:, :, :row_width].reshape(token_count, row_width).astype(jnp.bfloat16)
    )
    value_grad_rows = (
        joined_grads[:, :, row_width:].reshape(token_count, row_width).astype(jnp.bfloat16)
    )
    return (
        lax.all_to_all(query_rows, "head", split_axis=0, concat_axis=1, tiled=True),
        lax.all_to_all(key_grad_rows, "head", split_axis=0, concat_axis=1, tiled=True),
        lax.all_to_all(value_grad_rows, "head", split_axis=0, concat_axis=1, tiled=True),
    )


def solution(mesh):
    placed = (
        P("seq", "head"),
        P("seq", "head"),
        P("seq", "head"),
        P("seq", "head"),
        P("seq", "head", None),
    )
    return jax.shard_map(
        local,
        mesh=mesh,
        in_specs=placed,
        out_specs=(P(("seq", "head"), None), P(("seq", "head"), None), P(("seq", "head"), None)),
        check_vma=False,
    )
```

profile of v0, /device:TPU:16, one launch (start us, length us, event | category | flops | bytes accessed | tf_op | source)
XLA Modules:
  0.0 405.9 jit_solution(14961372682652943931)
XLA Ops:
  0.6 0.8 copy.93
  2.1 0.9 scatter_custom_fusion
  3.6 6.2 %all-to-all-start = ((s32[16,1,9]{2,1,0:T(1,128)}), s32[16,1,9]{2,1,0:T(1,128)S(1)}, u32[]{:S(2)}, u32[]{:S(2)}) async-start(s32[16,1,9]{2,1,0:T(1,128)} %bitcast.8), calls=%async_computation | async-start | bytes 16384 | tf_op jit(solution)/shard_map/all_to_all | solution.py:58
  9.8 1.3 copy.124
  12.1 1.8 all-to-all-done
  15.2 7.6 %gather_fusion = bf16[144,64,256]{2,1,0:T(8,128)(2,1)} fusion(bf16[48,64,256]{2,1,0:T(8,128)(2,1)S(1)} %pad_maximum_fusion.4, s32[1024]{0:T(1024)S(1)} %pad_clamp_fusion.1), kind=kCustom, calls=%fused_computation | custom fusion | bytes 9437760 | tf_op jit(solution)/shard_map/gather | solution.py:68
  22.7 6.9 %all-to-all-start.1 = ((bf16[16,9,64,256]{3,2,1,0:T(8,128)(2,1)}), bf16[16,9,64,256]{3,2,1,0:T(8,128)(2,1)}, u32[]{:S(2)}, u32[]{:S(2)}) async-start(bf16[16,9,64,256]{3,2,1,0:T(8,128)(2,1)} %bitcast.151), calls=%async_computation.1 | async-start | bytes 9437184 | tf_op jit(solution)/shard_map/all_to_all | solution.py:69
  29.8 1.2 fusion.56
  31.0 3.1 collective-permute-start.1
  34.1 2.4 collective-permute-start
  36.8 1.0 copy.122
  37.8 1.0 copy.125
  39.4 100.8 %collective-permute-done.1 = bf16[64,6144]{1,0:T(8,128)(2,1)} collective-permute-done((bf16[64,6144]{1,0:T(8,128)(2,1)}, bf16[64,6144]{1,0:T(8,128)(2,1)}, u32[]{:S(2)}, u32[]{:S(2)}) %collective-permute-start.1) | collective-permute-done | bytes 786464 | tf_op jit(solution)/shard_map/ppermute | solution.py:17
  140.2 1.8 collective-permute-done
  142.0 1.6 fusion.13
  145.9 1.6 fusion.10
  148.0 3.3 fusion.9
  151.3 4.9 %gather_fusion.1 = bf16[96,64,256]{2,1,0:T(8,128)(2,1)} fusion(bf16[144,64,256]{2,1,0:T(8,128)(2,1)} %bitcast.11, s32[1024]{0:T(1024)S(1)} %pad_clamp_fusion), kind=kCustom, calls=%fused_computation.1 | custom fusion | bytes 6291840 | tf_op jit(solution)/shard_map/gather | solution.py:77
  156.2 2.9 convolution_bitcast_fusion.2
  159.2 1.2 convolution_bitcast_fusion.1
  160.3 1.8 fusion.36
  162.1 2.7 exponential_reduce_fusion
  164.9 1.9 fusion.4
  167.4 0.9 fusion.33
  168.4 1.0 fusion.25
  170.3 3.2 fusion.3
  173.5 1.4 copy-done.8
  175.0 0.9 convolution_multiply_fusion
  175.9 3.0 pad_maximum_fusion.1
  178.9 6.6 %copy.109 = f32[2,24,128,256]{3,2,1,0:T(8,128)} copy(f32[2,24,128,256]{2,3,1,0:T(8,128)} %pad_maximum_fusion.1) | data formatting | bytes 12582912 | tf_op jit(solution)/shard_map/concatenate | solution.py:199
  185.5 4.9 %broadcast_in_dim.61 = f32[144,64,256]{2,1,0:T(8,128)} broadcast(f32[]{:T(128)} %constant.116.clone.1), dimensions={} | broadcast | bytes 9437188 | tf_op jit(solution)/shard_map/broadcast_in_dim | solution.py:203
  190.3 17.8 %scatter_fusion = f32[144,64,256]{2,1,0:T(8,128)} fusion(f32[144,64,256]{2,1,0:T(8,128)} %broadcast_in_dim.61, s32[96]{0:T(128)S(1)} %fusion.48, f32[96,64,256]{2,1,0:T(8,128)} %bitcast.144), kind=kCustom, calls=%fused_computation.3 | custom fusion | bytes 18874752 | tf_op jit(solution)/shard_map/scatter | solution.py:205
  208.1 6.5 %convert_element_type.64 = bf16[144,64,256]{2,1,0:T(8,128)(2,1)} convert(f32[144,64,256]{2,1,0:T(8,128)} %scatter_fusion) | non-fusion elementwise | flops 2359296 | bytes 14155776 | tf_op jit(solution)/shard_map/convert_element_type | solution.py:208
  214.6 4.9 %all-to-all-start.3 = ((bf16[16,9,64,256]{3,2,1,0:T(8,128)(2,1)}), bf16[16,9,64,256]{3,2,1,0:T(8,128)(2,1)}, u32[]{:S(2)}, u32[]{:S(2)}) async-start(bf16[16,9,64,256]{3,2,1,0:T(8,128)(2,1)} %bitcast.150), calls=%async_computation.3 | async-start | bytes 9437184 | tf_op jit(solution)/shard_map/all_to_all | solution.py:207
  219.6 0.9 convolution_bitcast_fusion
  221.5 0.9 multiply_bitcast_fusion
  222.3 1.2 pad_maximum_fusion
  223.5 9.1 %copy.104 = f32[2,192,2,24,128]{4,3,2,1,0:T(8,128)} copy(f32[2,192,2,24,128]{4,1,3,0,2:T(8,128)S(1)} %pad_maximum_fusion) | data formatting | bytes 18874368 | tf_op jit(solution)/shard_map/stack | solution.py:175
  232.6 9.9 %reshape.341 = f32[2,3,64,6144]{3,2,1,0:T(8,128)} reshape(f32[2,192,2,24,128]{4,3,2,1,0:T(8,128)} %copy.104) | data formatting | bytes 18874368 | tf_op jit(solution)/shard_map/reshape | solution.py:175
  242.5 4.8 %slice_bitcast_fusion.2 = (f32[2,64,6144]{2,1,0:T(8,128)S(1)}, f32[2,64,6144]{2,1,0:T(8,128)S(1)}, f32[2,64,6144]{2,1,0:T(8,128)S(1)}) fusion(f32[2,3,64,6144]{3,2,1,0:T(8,128)} %reshape.341), kind=kLoop, calls=%fused_computation.21 | loop fusion | bytes 18874368 | tf_op jit(solution)/shard_map/squeeze | solution.py:179
  247.5 1.0 fusion.53
  248.6 2.4 collective-permute-start.2
  251.8 1.0 fusion.28
  252.8 1.1 copy.147
  253.8 4.3 %collective-permute-start.3 = (bf16[64,6144]{1,0:T(8,128)(2,1)S(1)}, bf16[64,6144]{1,0:T(8,128)(2,1)S(1)}, u32[]{:S(2)}, u32[]{:S(2)}) collective-permute-start(bf16[64,6144]{1,0:T(8,128)(2,1)S(1)} %get-tuple-element.32), channel_id=1, source_target_pairs={{2,0},{4,2},{6,4},{8,6},{10,8},{12,10},{14,12},{16,14},{18,16},{20... | collective-permute-start | bytes 2359304 | tf_op jit(solution)/shard_map/ppermute | solution.py:25
  258.1 1.9 slice.171
  260.1 71.6 %collective-permute-done.2 = bf16[64,6144]{1,0:T(8,128)(2,1)S(1)} collective-permute-done((bf16[64,6144]{1,0:T(8,128)(2,1)S(1)}, bf16[64,6144]{1,0:T(8,128)(2,1)S(1)}, u32[]{:S(2)}, u32[]{:S(2)}) %collective-permute-start.2) | collective-permute-done | bytes 786464 | tf_op jit(solution)/shard_map/ppermute | solution.py:25
  331.6 1.3 fusion.12
  332.9 2.8 fusion.11
  335.7 4.6 %all-to-all-start.2 = ((bf16[2,64,3072]{2,1,0:T(8,128)(2,1)}), bf16[2,64,3072]{2,1,0:T(8,128)(2,1)}, u32[]{:S(2)}, u32[]{:S(2)}) async-start(bf16[2,64,3072]{2,1,0:T(8,128)(2,1)} %bitcast.126), calls=%async_computation.2 | async-start | bytes 1572864 | tf_op jit(solution)/shard_map/all_to_all | solution.py:233
  340.3 7.3 %bitcast_convert_fusion = f32[144,64,256]{2,1,0:T(8,128)} fusion(bf16[16,9,64,256]{3,2,1,0:T(8,128)(2,1)} %all-to-all-done.3), kind=kLoop, calls=%fused_computation.14 | loop fusion | flops 2359296 | bytes 14155776 | tf_op jit(solution)/shard_map/reshape | solution.py:214
  347.9 19.1 %scatter_fusion.1 = f32[49,64,256]{2,1,0:T(8,128)S(1)} fusion(f32[49,64,256]{2,1,0:T(8,128)S(1)} %broadcast_in_dim.60, s32[144]{0:T(256)S(1)} %bitcast.170, f32[144,64,256]{2,1,0:T(8,128)} %bitcast_convert_fusion), kind=kCustom, calls=%fused_computation.4 | custom fusion | flops 2359296 | bytes 28312128 | tf_op jit(solution)/shard_map/scatter-add | solution.py:216
  367.0 1.9 slice.176
  368.9 3.5 reshape.347
  372.4 3.5 copy.110
  375.9 2.8 reshape.348
  378.7 2.2 add_convert_fusion
  380.9 1.0 fusion.55
  381.8 11.4 %all_to_all.67 = bf16[2,64,3072]{2,1,0:T(8,128)(2,1)S(1)} all-to-all(bf16[2,64,3072]{2,1,0:T(8,128)(2,1)S(1)} %get-tuple-element.34), channel_id=1, replica_groups=mesh['seq'=16,'head'=2] {'head'}, dimensions={0} | all-to-all | bytes 1572864 | tf_op jit(solution)/shard_map/all_to_all | solution.py:235
  393.2 3.5 all-to-all-start.4
  396.8 2.1 copy.116
  398.8 0.9 copy.118
  399.7 5.0 %all-to-all-done.4 = bf16[2,64,3072]{2,1,0:T(8,128)(2,1)S(1)} async-done(((bf16[2,64,3072]{2,1,0:T(8,128)(2,1)}), bf16[2,64,3072]{2,1,0:T(8,128)(2,1)S(1)}, u32[]{:S(2)}, u32[]{:S(2)}) %all-to-all-start.4) | async-done | bytes 786464 | tf_op jit(solution)/shard_map/all_to_all | solution.py:234
  404.7 0.9 copy.117
  (94 shorter events, 10.9 us)
Async XLA Ops:
  0.6 10.8 %copy-start.15 = (bf16[128,3072]{1,0:T(8,128)(2,1)S(1)}, bf16[128,3072]{1,0:T(8,128)(2,1)}, u32[]{:S(2)}) copy-start(bf16[128,3072]{1,0:T(8,128)(2,1)} %param.10) | copy-start | bytes 2359300
  3.6 10.2 %all-to-all-start = ((s32[16,1,9]{2,1,0:T(1,128)}), s32[16,1,9]{2,1,0:T(1,128)S(1)}, u32[]{:S(2)}, u32[]{:S(2)}) async-start(s32[16,1,9]{2,1,0:T(1,128)} %bitcast.8), calls=%async_computation | async-start | bytes 16384 | tf_op jit(solution)/shard_map/all_to_all | solution.py:58
  22.7 7.0 %copy-start.16 = (bf16[128,3072]{1,0:T(8,128)(2,1)S(1)}, bf16[128,3072]{1,0:T(8,128)(2,1)}, u32[]{:S(2)}) copy-start(bf16[128,3072]{1,0:T(8,128)(2,1)} %param.11) | copy-start | bytes 2359300
  22.7 128.6 %all-to-all-start.1 = ((bf16[16,9,64,256]{3,2,1,0:T(8,128)(2,1)}), bf16[16,9,64,256]{3,2,1,0:T(8,128)(2,1)}, u32[]{:S(2)}, u32[]{:S(2)}) async-start(bf16[16,9,64,256]{3,2,1,0:T(8,128)(2,1)} %bitcast.151), calls=%async_computation.1 | async-start | bytes 9437184 | tf_op jit(solution)/shard_map/all_to_all | solution.py:69
  29.7 7.1 %copy-start.17 = (bf16[128,3072]{1,0:T(8,128)(2,1)S(1)}, bf16[128,3072]{1,0:T(8,128)(2,1)}, u32[]{:S(2)}) copy-start(bf16[128,3072]{1,0:T(8,128)(2,1)} %param.9) | copy-start | bytes 2359300
  29.8 8.0 %copy-start.18 = (bf16[128,3072]{1,0:T(8,128)(2,1)S(1)}, bf16[128,3072]{1,0:T(8,128)(2,1)}, u32[]{:S(2)}) copy-start(bf16[128,3072]{1,0:T(8,128)(2,1)} %param.12) | copy-start | bytes 2359300
  31.0 109.1 %collective-permute-start.1 = (bf16[64,6144]{1,0:T(8,128)(2,1)}, bf16[64,6144]{1,0:T(8,128)(2,1)}, u32[]{:S(2)}, u32[]{:S(2)}) collective-permute-start(bf16[64,6144]{1,0:T(8,128)(2,1)} %get-tuple-element.38), channel_id=1, source_target_pairs={{2,0},{4,2},{6,4},{8,6},{10,8},{12,10},{14,12},{16,14},{18,16},{20... | collective-permute-start | bytes 2359304 | tf_op jit(solution)/shard_map/ppermute | solution.py:17
  34.1 107.8 %collective-permute-start = (bf16[64,6144]{1,0:T(8,128)(2,1)}, bf16[64,6144]{1,0:T(8,128)(2,1)}, u32[]{:S(2)}, u32[]{:S(2)}) collective-permute-start(bf16[64,6144]{1,0:T(8,128)(2,1)} %get-tuple-element.39), channel_id=1, source_target_pairs={{0,2},{2,4},{4,6},{6,8},{8,10},{10,12},{12,14},{14,16},{16,18},{18... | collective-permute-start | bytes 2359304 | tf_op jit(solution)/shard_map/ppermute | solution.py:16
  144.8 1.1 copy-start.11
  145.8 2.2 copy-start.5
  145.9 2.1 copy-start
  156.2 2.9 copy-start.1
  156.2 2.9 copy-start.3
  164.9 3.5 slice-start
  166.8 1.5 copy-start.6
  166.8 1.5 slice-start.1
  168.4 1.9 copy-start.14
  170.3 4.7 %copy-start.12 = (bf16[16,8,24,128]{3,2,1,0:T(8,128)(2,1)S(1)}, bf16[16,8,24,128]{3,2,1,0:T(8,128)(2,1)}, u32[]{:S(2)}) copy-start(bf16[16,8,24,128]{3,2,1,0:T(8,128)(2,1)} %copy.122) | copy-start | bytes 2359300
  173.5 1.5 copy-start.8
  214.6 5.0 %copy-start.2 = (bf16[16,8,24,128]{3,2,1,0:T(8,128)(2,1)S(1)}, bf16[16,8,24,128]{3,2,1,0:T(8,128)(2,1)}, u32[]{:S(2)}) copy-start(bf16[16,8,24,128]{3,2,1,0:T(8,128)(2,1)} %copy.125) | copy-start | bytes 2359300
  214.6 5.0 %copy-start.7 = (bf16[2,24,64,320]{3,2,1,0:T(8,128)(2,1)S(1)}, bf16[2,24,64,320]{3,2,1,0:T(8,128)(2,1)}, u32[]{:S(2)}) copy-start(bf16[2,24,64,320]{3,2,1,0:T(8,128)(2,1)} %copy-done.6) | copy-start | bytes 5898244
  214.6 121.0 %all-to-all-start.3 = ((bf16[16,9,64,256]{3,2,1,0:T(8,128)(2,1)}), bf16[16,9,64,256]{3,2,1,0:T(8,128)(2,1)}, u32[]{:S(2)}, u32[]{:S(2)}) async-start(bf16[16,9,64,256]{3,2,1,0:T(8,128)(2,1)} %bitcast.150), calls=%async_computation.3 | async-start | bytes 9437184 | tf_op jit(solution)/shard_map/all_to_all | solution.py:207
  219.6 1.7 copy-start.9
  219.6 1.8 copy-start.13
  247.4 4.4 %slice-start.2 = ((s8[4718592]{0:T(1024)(128)(4,1)}), s8[4194304]{0:T(1024)(128)(4,1)S(1)}, s32[]{:S(2)}) async-start(s8[4718592]{0:T(1024)(128)(4,1)} %bitcast.142), calls=%async_computation.8 | async-start | bytes 8388608
  247.5 3.5 copy-start.10
  247.5 4.3 %slice-start.3 = ((s8[4718592]{0:T(1024)(128)(4,1)}), s8[524288]{0:T(1024)(128)(4,1)S(1)}, s32[]{:S(2)}) async-start(s8[4718592]{0:T(1024)(128)(4,1)} %bitcast.142), calls=%async_computation.9 | async-start | bytes 1048576
  248.5 2.6 copy-start.4
  248.6 83.0 %collective-permute-start.2 = (bf16[64,6144]{1,0:T(8,128)(2,1)S(1)}, bf16[64,6144]{1,0:T(8,128)(2,1)S(1)}, u32[]{:S(2)}, u32[]{:S(2)}) collective-permute-start(bf16[64,6144]{1,0:T(8,128)(2,1)S(1)} %get-tuple-element.33), channel_id=1, source_target_pairs={{0,2},{2,4},{4,6},{6,8},{8,10},{10,12},{12,14},{14,16},{16,18},{18... | collective-permute-start | bytes 2359304 | tf_op jit(solution)/shard_map/ppermute | solution.py:25
  253.8 79.1 %collective-permute-start.3 = (bf16[64,6144]{1,0:T(8,128)(2,1)S(1)}, bf16[64,6144]{1,0:T(8,128)(2,1)S(1)}, u32[]{:S(2)}, u32[]{:S(2)}) collective-permute-start(bf16[64,6144]{1,0:T(8,128)(2,1)S(1)} %get-tuple-element.32), channel_id=1, source_target_pairs={{2,0},{4,2},{6,4},{8,6},{10,8},{12,10},{14,12},{16,14},{18,16},{20... | collective-permute-start | bytes 2359304 | tf_op jit(solution)/shard_map/ppermute | solution.py:25
  335.7 46.2 %all-to-all-start.2 = ((bf16[2,64,3072]{2,1,0:T(8,128)(2,1)}), bf16[2,64,3072]{2,1,0:T(8,128)(2,1)}, u32[]{:S(2)}, u32[]{:S(2)}) async-start(bf16[2,64,3072]{2,1,0:T(8,128)(2,1)} %bitcast.126), calls=%async_computation.2 | async-start | bytes 1572864 | tf_op jit(solution)/shard_map/all_to_all | solution.py:233
  393.2 11.5 %all-to-all-start.4 = ((bf16[2,64,3072]{2,1,0:T(8,128)(2,1)}), bf16[2,64,3072]{2,1,0:T(8,128)(2,1)S(1)}, u32[]{:S(2)}, u32[]{:S(2)}) async-start(bf16[2,64,3072]{2,1,0:T(8,128)(2,1)} %get-tuple-element.35), calls=%async_computation.4 | async-start | bytes 1572864 | tf_op jit(solution)/shard_map/all_to_all | solution.py:234
where the time goes:
time: 412 us; the launch traced here: 406 us
  waiting for transfers between devices  181 us (44%)
  local copies, waits for them, and re-layouts  101 us (25%)
  other arithmetic  57.3 us (14%)
  starting transfers between devices  38.3 us (9%)
  matrix products  15.8 us (4%)
  blocking collectives  11.4 us (3%)
    ppermute x1, waiting for transfers between devices, padded(): after = lax.ppermute(first, axis, down)  101 us
    ppermute x2, waiting for transfers between devices, shifted(): lax.ppermute(value, axis, [(source, source + steps) for source in range(f...  71.6 us
    scatter-add x1, other arithmetic, local(): jax.ops.segment_sum(inbound, segment_ids, num_segments=block_count * head...  19.1 us
    scatter x1, local copies, waits for them, and re-layouts, local(): outbound = jnp.zeros((slot_count, block_size, 2 * head_size), jnp.float32...  17.8 us
    all_to_all x1, blocking collectives, local(): lax.all_to_all(value_grad_rows, 'head', split_axis=0, concat_axis=1, tile...  11.4 us
    unnamed x57, local copies, waits for them, and re-layouts  9.95 us
    reshape x1, local copies, waits for them, and re-layouts, local(): jnp.stack([window_key_grad, window_value_grad], axis=2)  9.91 us
    another operation x1, local copies, waits for them, and re-layouts, local(): jnp.stack([window_key_grad, window_value_grad], axis=2)  9.13 us
  transfers between devices with their start and end apart: 9, of which 5 were waited for; matrix products, arithmetic and copies ran while one was open for 24% of the time, Pallas kernels for 0%

commit v1 on v0

v1 whole, which is shorter than its diff:
```python
import functools
import math

import jax
import jax.numpy as jnp
from jax import lax
from jax.experimental import pallas as pl
from jax.experimental.pallas import tpu as pltpu
from jax.sharding import PartitionSpec as P

F32 = jnp.float32
BF16 = jnp.bfloat16
VMEM = pltpu.VMEM
LIMIT = 48 * 1024 * 1024


def dot(a, b, ca, cb):
    return lax.dot_general(a, b, (((ca,), (cb,)), ((), ())), preferred_element_type=F32)


def gather_kernel(block, dim, heads, cap, codes, k_ref, v_ref, o_ref):
    peer = pl.program_id(0)
    for j in range(cap):
        code = jnp.maximum(codes[peer * cap + j], 0)
        rows = pl.ds(pl.multiple_of(code // heads * block, block), block)
        cols = pl.ds(pl.multiple_of(code % heads * dim, dim), dim)
        o_ref[j, :, :dim] = k_ref[rows, cols]
        o_ref[j, :, dim:] = v_ref[rows, cols]


def attend_kernel(
    blocks, block, dim, heads, rand, step, scale,
    slots, edge, q_ref, k_ref, v_ref, g_ref, up_ref, down_ref, far_ref,
    dq_ref, dk_ref, dv_ref, tok_ref, tov_ref, tnk_ref, tnv_ref, out_ref,
):
    group = pl.program_id(0)
    for j in range(step):
        head = group * step + j
        cols = slice(j * dim, (j + 1) * dim)
        ks = [up_ref[0, :, cols]] + [k_ref[b * block:(b + 1) * block, cols] for b in range(blocks)]
        ks.append(down_ref[0, :, cols])
        vs = [up_ref[1, :, cols]] + [v_ref[b * block:(b + 1) * block, cols] for b in range(blocks)]
        vs.append(down_ref[1, :, cols])
        gk = [None] * (blocks + 2)
        gv = [None] * (blocks + 2)
        for b in range(blocks):
            rows = slice(b * block, (b + 1) * block)
            q = q_ref[rows, cols]
            g = g_ref[rows, cols]
            at = [slots[(b * heads + head) * rand + r] for r in range(rand)]
            keys = jnp.concatenate(ks[b:b + 3] + [far_ref[s, :, :dim] for s in at], axis=0)
            vals = jnp.concatenate(vs[b:b + 3] + [far_ref[s, :, dim:] for s in at], axis=0)
            s = scale * dot(q, keys, 1, 1)
            place = lax.broadcasted_iota(jnp.int32, s.shape, 1)
            if b == 0:
                s = jnp.where((place < block) & (edge[0] == 0), -jnp.inf, s)
            if b == blocks - 1:
                s = jnp.where(
                    (place >= 2 * block) & (place < 3 * block) & (edge[1] == 0), -jnp.inf, s
                )
            top = jnp.max(s, axis=1, keepdims=True)
            e = jnp.exp(s - top)
            w = e * (1.0 / jnp.sum(e, axis=1, keepdims=True))
            p = w.astype(BF16)
            o = dot(p, vals, 1, 0).astype(BF16).astype(F32)
            delta = jnp.sum(o * g.astype(F32), axis=1, keepdims=True)
            ds = (w * (dot(g, vals, 1, 1) - delta)).astype(BF16)
            dq_ref[rows, cols] = (scale * dot(ds, keys, 1, 0)).astype(BF16)
            dk = scale * dot(ds, q, 0, 0)
            dv = dot(p, g, 0, 0)
            for i in range(3):
                part = slice(i * block, (i + 1) * block)
                gk[b + i] = dk[part] if gk[b + i] is None else gk[b + i] + dk[part]
                gv[b + i] = dv[part] if gv[b + i] is None else gv[b + i] + dv[part]
            for r in range(rand):
                part = slice((3 + r) * block, (4 + r) * block)
                out_ref[at[r], :, :dim] = dk[part].astype(BF16)
                out_ref[at[r], :, dim:] = dv[part].astype(BF16)
        tok_ref[:, cols] = gk[0].astype(BF16)
        tov_ref[:, cols] = gv[0].astype(BF16)
        tnk_ref[:, cols] = gk[-1].astype(BF16)
        tnv_ref[:, cols] = gv[-1].astype(BF16)
        for b in range(blocks):
            rows = slice(b * block, (b + 1) * block)
            dk_ref[rows, cols] = gk[b + 1]
            dv_ref[rows, cols] = gv[b + 1]


def collect_kernel(
    blocks, block, dim, heads, count, codes, dk_ref, dv_ref, ak_ref, av_ref, bk_ref, bv_ref,
    in_ref, ok_ref, ov_ref, k_acc, v_acc,
):
    last = slice((blocks - 1) * block, blocks * block)
    k_acc[...] = dk_ref[...]
    v_acc[...] = dv_ref[...]
    k_acc[:block] += ak_ref[...].astype(F32)
    v_acc[:block] += av_ref[...].astype(F32)
    k_acc[last] += bk_ref[...].astype(F32)
    v_acc[last] += bv_ref[...].astype(F32)

    @pl.loop(0, count)
    def _(s):
        code = codes[s]

        @pl.when(code >= 0)
        def _():
            rows = pl.ds(pl.multiple_of(code // heads * block, block), block)
            cols = pl.ds(pl.multiple_of(code % heads * dim, dim), dim)
            k_acc[rows, cols] += in_ref[s, :, :dim].astype(F32)
            v_acc[rows, cols] += in_ref[s, :, dim:].astype(F32)

    ok_ref[...] = k_acc[...].astype(BF16)
    ov_ref[...] = v_acc[...].astype(BF16)


def shifted(value, axis, steps):
    count = lax.axis_size(axis)
    first, last = (max(0, -steps), min(count, count - steps))
    return lax.ppermute(value, axis, [(source, source + steps) for source in range(first, last)])


def local(queries, key_rows, value_rows, out_grad, partner):
    peers = lax.axis_size("seq")
    me = lax.axis_index("seq")
    tokens, width = queries.shape
    blocks, heads, rand = partner.shape
    block = tokens // blocks
    dim = width // heads
    scale = 1.0 / math.sqrt(dim)
    items = blocks * heads * rand
    cap = max(2, (3 * items + 2 * peers - 1) // (2 * peers))
    count = peers * cap
    wanted = partner.reshape(items)
    owner = wanted // blocks
    order = jnp.arange(items, dtype=jnp.int32)
    earlier = (owner[None, :] == owner[:, None]) & (order[None, :] < order[:, None])
    slot = owner * cap + jnp.sum(earlier.astype(jnp.int32), axis=1)
    code = wanted % blocks * heads + order // rand % heads
    hit = slot[None, :] == jnp.arange(count, dtype=jnp.int32)[:, None]
    asked = jnp.sum(jnp.where(hit, code[None, :] + 1, 0), axis=1) - 1
    asked = lax.all_to_all(
        asked.reshape(peers, cap), "seq", split_axis=0, concat_axis=0, tiled=True
    ).reshape(count)
    full = pl.BlockSpec(memory_space=VMEM)
    outgoing = pl.pallas_call(
        functools.partial(gather_kernel, block, dim, heads, cap),
        out_shape=jax.ShapeDtypeStruct((count, block, 2 * dim), BF16),
        grid_spec=pltpu.PrefetchScalarGridSpec(
            num_scalar_prefetch=1,
            grid=(peers,),
            in_specs=[pl.BlockSpec((tokens, width), lambda i, *_: (0, 0))] * 2,
            out_specs=pl.BlockSpec((cap, block, 2 * dim), lambda i, *_: (i, 0, 0)),
        ),
        compiler_params=pltpu.CompilerParams(vmem_limit_bytes=LIMIT),
    )(asked, key_rows, value_rows)
    fetched = lax.all_to_all(
        outgoing.reshape(peers, cap, block, 2 * dim), "seq", split_axis=0, concat_axis=0, tiled=True
    ).reshape(count, block, 2 * dim)
    up = shifted(jnp.stack([key_rows[tokens - block:], value_rows[tokens - block:]]), "seq", 1)
    down = shifted(jnp.stack([key_rows[:block], value_rows[:block]]), "seq", -1)
    edge = jnp.stack([(me > 0), (me < peers - 1)]).astype(jnp.int32)
    step = next(n for n in (4, 3, 2, 1) if heads % n == 0)
    wide = pl.BlockSpec((tokens, step * dim), lambda i, *_: (0, i))
    side = pl.BlockSpec((2, block, step * dim), lambda i, *_: (0, 0, i))
    thin = pl.BlockSpec((block, step * dim), lambda i, *_: (0, i))
    far = pl.BlockSpec((count, block, 2 * dim), lambda i, *_: (0, 0, 0))
    half = jax.ShapeDtypeStruct((block, width), BF16)
    whole = jax.ShapeDtypeStruct((tokens, width), F32)
    dq, dk, dv, tok, tov, tnk, tnv, outbound = pl.pallas_call(
        functools.partial(attend_kernel, blocks, block, dim, heads, rand, step, scale),
        out_shape=[
            jax.ShapeDtypeStruct((tokens, width), BF16), whole, whole, half, half, half, half,
            jax.ShapeDtypeStruct((count, block, 2 * dim), BF16),
        ],
        grid_spec=pltpu.PrefetchScalarGridSpec(
            num_scalar_prefetch=2,
            grid=(heads // step,),
            in_specs=[wide, wide, wide, wide, side, side, far],
            out_specs=[wide, wide, wide, thin, thin, thin, thin, far],
        ),
        compiler_params=pltpu.CompilerParams(vmem_limit_bytes=LIMIT),
    )(slot, edge, queries, key_rows, value_rows, out_grad, up, down, fetched)
    inbound = lax.all_to_all(
        outbound.reshape(peers, cap, block, 2 * dim), "seq", split_axis=0, concat_axis=0, tiled=True
    ).reshape(count, block, 2 * dim)
    below_k, below_v = shifted(tok, "seq", -1), shifted(tov, "seq", -1)
    above_k, above_v = shifted(tnk, "seq", 1), shifted(tnv, "seq", 1)
    rows = jax.ShapeDtypeStruct((tokens, width), BF16)
    smem = pl.BlockSpec(memory_space=pltpu.SMEM)
    k_rows, v_rows = pl.pallas_call(
        functools.partial(collect_kernel, blocks, block, dim, heads, count),
        out_shape=[rows, rows],
        in_specs=[smem] + [full] * 7,
        out_specs=[full, full],
        scratch_shapes=[VMEM((tokens, width), F32), VMEM((tokens, width), F32)],
        compiler_params=pltpu.CompilerParams(vmem_limit_bytes=LIMIT),
    )(asked, dk, dv, above_k, above_v, below_k, below_v, inbound)
    return tuple(
        lax.all_to_all(x, "head", split_axis=0, concat_axis=1, tiled=True)
        for x in (dq, k_rows, v_rows)
    )


def solution(mesh):
    placed = (P("seq", "head"),) * 4 + (P("seq", "head", None),)
    return jax.shard_map(
        local,
        mesh=mesh,
        in_specs=placed,
        out_specs=(P(("seq", "head"), None),) * 3,
        check_vma=False,
    )
```

time: 412 us -> 333 us (0.81)
  local copies, waits for them, and re-layouts: 101 us -> 10.4 us
  other arithmetic: 57.3 us -> 2.96 us
  Pallas kernels: 0 us -> 51.4 us
  waiting for transfers between devices: 181 us -> 206 us
  matrix products: 15.8 us -> 0 us
  blocking collectives: 11.4 us -> 20.7 us
    ppermute x2 -> x0, waiting for transfers between devices: 103 us -> none  [the longest x1 101 us: padded(): after = lax.ppermute(first, axis, down)]
    all_to_all x5 -> x4, waiting for transfers between devices: 6.75 us -> 98.3 us  [the longest x1 93.3 us: local(): lax.all_to_all(outbound.reshape(peers, cap, block, 2 * dim), 'seq', split...]
    pallas_call x0 -> x3, Pallas kernels: none -> 51.4 us  [the longest x1 36.2 us: local(): pl.pallas_call(functools.partial(attend_kernel, blocks, block, dim, heads...]
    ppermute x2 -> x6, waiting for transfers between devices: 71.6 us -> 107 us  [shifted(): lax.ppermute(value, axis, [(source, source + steps) for source in range(f...]
    scatter-add x3 -> x0, other arithmetic: 23.2 us -> none  [the longest x1 19.1 us: local(): jax.ops.segment_sum(inbound, segment_ids, num_segments=block_count * head...]
    scatter x2 -> x0, local copies, waits for them, and re-layouts: 18.6 us -> none  [the longest x1 17.8 us: local(): outbound = jnp.zeros((slot_count, block_size, 2 * head_size), jnp.float32...]
    reshape x7 -> x2, local copies, waits for them, and re-layouts: 16.6 us -> 0.2 us  [the longest x1 0.12 us: local(): wanted = partner.reshape(items)]
    dot_general x12 -> x0, matrix products: 15.8 us -> none  [the longest x1 3.29 us: local(): jnp.einsum('bqhd,bkhd->bhqk', grad_blocks, window_values, preferred_eleme...]
  transfers between devices with their start and end apart: 9 -> 10, of which waited for: 5 -> 4; matrix products, arithmetic and copies ran while one was open for 24% -> 2% of each run, Pallas kernels for 0% -> 2%
where the time goes in v1:
time: 333 us; the launch traced here: 328 us
  waiting for transfers between devices  206 us (62%)
  Pallas kernels  51.4 us (15%)
  starting transfers between devices  36.5 us (11%)
  blocking collectives  20.7 us (6%)
  local copies, waits for them, and re-layouts  10.4 us (3%)
    ppermute x6, waiting for transfers between devices, shifted(): lax.ppermute(value, axis, [(source, source + steps) for source in range(f...  107 us
    all_to_all x1, waiting for transfers between devices, local(): lax.all_to_all(outbound.reshape(peers, cap, block, 2 * dim), 'seq', split...  93.3 us
    pallas_call x1, Pallas kernels, local(): pl.pallas_call(functools.partial(attend_kernel, blocks, block, dim, heads...  36.2 us
    ppermute x6, starting transfers between devices, shifted(): lax.ppermute(value, axis, [(source, source + steps) for source in range(f...  17.2 us
    all_to_all x1, blocking collectives, local(): lax.all_to_all(x, 'head', split_axis=0, concat_axis=1, tiled=True)  10.6 us
    all_to_all x1, blocking collectives, local(): lax.all_to_all(asked.reshape(peers, cap), 'seq', split_axis=0, concat_axi...  10.1 us
    pallas_call x1, Pallas kernels, local(): pl.pallas_call(functools.partial(collect_kernel, blocks, block, dim, head...  8.15 us
    all_to_all x2, starting transfers between devices, local(): lax.all_to_all(x, 'head', split_axis=0, concat_axis=1, tiled=True)  7.84 us
  transfers between devices with their start and end apart: 10, of which 4 were waited for; matrix products, arithmetic and copies ran while one was open for 2% of the time, Pallas kernels for 2%

profile of v1, /device:TPU:16, one launch (start us, length us, event | category | flops | bytes accessed | tf_op | source)
XLA Modules:
  0.0 328.5 jit_solution(2946819005413485434)
XLA Ops:
  0.6 0.8 copy.21
  1.4 0.1 reshape.163
  1.5 0.2 convert_reduce_fusion
  1.7 0.1 select_reduce_fusion
  1.9 0.1 sub.19
  1.9 10.1 %all_to_all.73 = s32[16,1,9]{2,1,0:T(1,128)S(1)} all-to-all(s32[16,1,9]{2,1,0:T(1,128)S(1)} %bitcast.35), channel_id=1, replica_groups=mesh['seq'=16,'head'=2] {'seq'}, dimensions={0} | all-to-all | bytes 1152 | tf_op jit(solution)/shard_map/all_to_all | solution.py:141
  12.0 0.5 broadcast.194
  12.5 0.7 reduce.3
  13.2 0.1 reshape.164.codes
  13.3 0.0 copy-start
  13.3 1.1 copy-done
  14.4 0.0 copy-start.2
  14.4 1.1 copy-done.2
  15.6 7.1 %shard_map.76 = bf16[144,64,256]{2,1,0:T(8,128)(2,1)} custom-call(s32[144]{0:T(256)S(1)} %reshape.164.codes, bf16[128,3072]{1,0:T(8,128)(2,1)S(1)} %copy-done, bf16[128,3072]{1,0:T(8,128)(2,1)S(1)} %copy-done.2), custom_call_target="tpu_custom_call" | custom-call | tf_op jit(solution)/shard_map/pallas_call | solution.py:145
  22.7 0.0 copy-start.1
  22.7 0.0 copy-start.3
  22.7 6.9 %all-to-all-start.1 = ((bf16[16,9,64,256]{3,2,1,0:T(8,128)(2,1)}), bf16[16,9,64,256]{3,2,1,0:T(8,128)(2,1)}, u32[]{:S(2)}, u32[]{:S(2)}) async-start(bf16[16,9,64,256]{3,2,1,0:T(8,128)(2,1)} %bitcast.28), calls=%async_computation.1 | async-start | bytes 9437184 | tf_op jit(solution)/shard_map/all_to_all | solution.py:156
  29.6 0.0 copy-done.1
  29.6 0.0 copy-done.3
  29.6 0.0 copy-start.5
  29.6 0.0 copy-start.6
  29.6 0.1 slice_bitcast_fusion
  29.7 0.9 pad_maximum_fusion
  30.7 2.0 collective-permute-start
  32.7 0.9 pad_maximum_fusion.1
  33.7 4.4 %collective-permute-start.1 = (bf16[2,64,3072]{2,1,0:T(8,128)(2,1)}, bf16[2,64,3072]{2,1,0:T(8,128)(2,1)}, u32[]{:S(2)}, u32[]{:S(2)}) collective-permute-start(bf16[2,64,3072]{2,1,0:T(8,128)(2,1)} %pad_maximum_fusion.1), channel_id=1, source_target_pairs={{2,0},{4,2},{6,4},{8,6},{10,8},{12,10},{14,12},{16,14},{18,16},{20... | collective-permute-start | bytes 2359304 | tf_op jit(solution)/shard_map/ppermute | solution.py:119
  38.1 0.1 add_convert_fusion.edge
  38.2 103.8 %collective-permute-done.up_ref = bf16[2,64,3072]{2,1,0:T(8,128)(2,1)} collective-permute-done((bf16[2,64,3072]{2,1,0:T(8,128)(2,1)}, bf16[2,64,3072]{2,1,0:T(8,128)(2,1)}, u32[]{:S(2)}, u32[]{:S(2)}) %collective-permute-start) | collective-permute-done | bytes 786464 | tf_op jit(solution)/shard_map/ppermute | solution.py:119
  141.9 0.0 collective-permute-done.1.down_ref
  141.9 0.0 all-to-all-done.1
  141.9 0.0 copy-done.5
  141.9 0.0 copy-done.6
  142.0 36.2 %shard_map.77 = (bf16[128,3072]{1,0:T(8,128)(2,1)}, f32[128,3072]{1,0:T(8,128)}, f32[128,3072]{1,0:T(8,128)}, bf16[64,3072]{1,0:T(8,128)(2,1)}, bf16[64,3072]{1,...) custom-call(s32[96]{0:T(128)S(1)} %multiply_add_fusion.slots, ...), custom_call_target="tpu_custom_call" | custom-call | tf_op jit(solution)/shard_map/pallas_call | solution.py:169
  178.1 0.0 copy-start.9
  178.1 0.8 copy-done.9
  178.9 0.0 copy-start.10
  178.9 0.0 copy-start.4
  178.9 4.6 %all-to-all-start.3 = ((bf16[16,9,64,256]{3,2,1,0:T(8,128)(2,1)}), bf16[16,9,64,256]{3,2,1,0:T(8,128)(2,1)}, u32[]{:S(2)}, u32[]{:S(2)}) async-start(bf16[16,9,64,256]{3,2,1,0:T(8,128)(2,1)} %bitcast.29), calls=%async_computation.3 | async-start | bytes 9437184 | tf_op jit(solution)/shard_map/all_to_all | solution.py:183
  183.5 1.9 collective-permute-start.2
  185.4 3.2 collective-permute-start.3
  188.6 3.2 collective-permute-start.4
  191.9 0.0 copy-done.10
  191.9 2.4 collective-permute-start.5
  194.3 93.3 %all-to-all-done.3 = bf16[16,9,64,256]{3,2,1,0:T(8,128)(2,1)} async-done(((bf16[16,9,64,256]{3,2,1,0:T(8,128)(2,1)}), bf16[16,9,64,256]{3,2,1,0:T(8,128)(2,1)}, u32[]{:S(2)}, u32[]{:S(2)}) %all-to-all-start.3) | async-done | bytes 4718624 | tf_op jit(solution)/shard_map/all_to_all | solution.py:183
  287.6 4.3 %all-to-all-start.2 = ((bf16[2,64,3072]{2,1,0:T(8,128)(2,1)}), bf16[2,64,3072]{2,1,0:T(8,128)(2,1)}, u32[]{:S(2)}, u32[]{:S(2)}) async-start(bf16[2,64,3072]{2,1,0:T(8,128)(2,1)} %bitcast.9), calls=%async_computation.2 | async-start | bytes 1572864 | tf_op jit(solution)/shard_map/all_to_all | solution.py:199
  292.0 0.0 collective-permute-done.2.ak_ref
  292.0 3.5 %collective-permute-done.3.av_ref = bf16[64,3072]{1,0:T(8,128)(2,1)S(1)} collective-permute-done((bf16[64,3072]{1,0:T(8,128)(2,1)}, bf16[64,3072]{1,0:T(8,128)(2,1)S(1)}, u32[]{:S(2)}, u32[]{:S(2)}) %collective-permute-start.3) | collective-permute-done | bytes 393248 | tf_op jit(solution)/shard_map/ppermute | solution.py:119
  295.5 0.0 collective-permute-done.4.bk_ref
  295.5 0.0 collective-permute-done.5.bv_ref
  295.5 0.0 copy-start.7
  295.5 0.7 copy-done.7
  296.3 0.0 copy-done.4
  296.3 0.0 copy-start.8
  296.3 1.0 copy-done.8
  297.3 8.1 %shard_map.78 = (bf16[128,3072]{1,0:T(8,128)(2,1)}, bf16[128,3072]{1,0:T(8,128)(2,1)S(1)}) custom-call(s32[144]{0:T(256)S(1)} %reshape.164.codes, f32[128,3072]{1,0:T(8,128)S(1)} %copy-done.4, f32[128,3072]{1,0:T(8,128)} %get-tuple-element.15.dv_ref, bf16[64,3072]{1,0:T(8,128)(2,1)S(1)} %collective-permute-done.2.ak_ref, ...), custom_call_target="tpu_custom_call" | custom-call | tf_op jit(solution)/shard_map/pallas_call | solution.py:190
  305.4 0.0 all-to-all-done.2
  305.4 10.6 %all_to_all.74 = bf16[2,64,3072]{2,1,0:T(8,128)(2,1)S(1)} all-to-all(bf16[2,64,3072]{2,1,0:T(8,128)(2,1)S(1)} %bitcast.27), channel_id=1, replica_groups=mesh['seq'=16,'head'=2] {'head'}, dimensions={0} | all-to-all | bytes 1572864 | tf_op jit(solution)/shard_map/all_to_all | solution.py:199
  316.0 3.5 %all-to-all-start.4 = ((bf16[2,64,3072]{2,1,0:T(8,128)(2,1)}), bf16[2,64,3072]{2,1,0:T(8,128)(2,1)S(1)}, u32[]{:S(2)}, u32[]{:S(2)}) async-start(bf16[2,64,3072]{2,1,0:T(8,128)(2,1)} %bitcast.13), calls=%async_computation.4 | async-start | bytes 1572864 | tf_op jit(solution)/shard_map/all_to_all | solution.py:199
  319.6 2.1 copy.26
  321.7 0.9 copy.28
  322.6 5.0 %all-to-all-done.4 = bf16[2,64,3072]{2,1,0:T(8,128)(2,1)S(1)} async-done(((bf16[2,64,3072]{2,1,0:T(8,128)(2,1)}), bf16[2,64,3072]{2,1,0:T(8,128)(2,1)S(1)}, u32[]{:S(2)}, u32[]{:S(2)}) %all-to-all-start.4) | async-done | bytes 786464 | tf_op jit(solution)/shard_map/all_to_all | solution.py:199
  327.6 0.9 copy.27
  (3 shorter events, 0.0 us)
Async XLA Ops:
  13.3 1.1 copy-start
  14.4 1.1 copy-start.2
  22.7 6.9 %copy-start.1 = (bf16[128,3072]{1,0:T(8,128)(2,1)S(1)}, bf16[128,3072]{1,0:T(8,128)(2,1)}, u32[]{:S(2)}) copy-start(bf16[128,3072]{1,0:T(8,128)(2,1)} %k_ref.3) | copy-start | bytes 2359300
  22.7 6.9 %copy-start.3 = (bf16[128,3072]{1,0:T(8,128)(2,1)S(1)}, bf16[128,3072]{1,0:T(8,128)(2,1)}, u32[]{:S(2)}) copy-start(bf16[128,3072]{1,0:T(8,128)(2,1)} %v_ref.3) | copy-start | bytes 2359300
  22.7 119.2 %all-to-all-start.1 = ((bf16[16,9,64,256]{3,2,1,0:T(8,128)(2,1)}), bf16[16,9,64,256]{3,2,1,0:T(8,128)(2,1)}, u32[]{:S(2)}, u32[]{:S(2)}) async-start(bf16[16,9,64,256]{3,2,1,0:T(8,128)(2,1)} %bitcast.28), calls=%async_computation.1 | async-start | bytes 9437184 | tf_op jit(solution)/shard_map/all_to_all | solution.py:156
  29.6 112.3 %copy-start.5 = (bf16[128,3072]{1,0:T(8,128)(2,1)S(1)}, bf16[128,3072]{1,0:T(8,128)(2,1)}, u32[]{:S(2)}) copy-start(bf16[128,3072]{1,0:T(8,128)(2,1)} %q_ref.1) | copy-start | bytes 2359300
  29.6 112.3 %copy-start.6 = (bf16[128,3072]{1,0:T(8,128)(2,1)S(1)}, bf16[128,3072]{1,0:T(8,128)(2,1)}, u32[]{:S(2)}) copy-start(bf16[128,3072]{1,0:T(8,128)(2,1)} %g_ref.1) | copy-start | bytes 2359300
  30.7 111.2 %collective-permute-start = (bf16[2,64,3072]{2,1,0:T(8,128)(2,1)}, bf16[2,64,3072]{2,1,0:T(8,128)(2,1)}, u32[]{:S(2)}, u32[]{:S(2)}) collective-permute-start(bf16[2,64,3072]{2,1,0:T(8,128)(2,1)} %pad_maximum_fusion), channel_id=1, source_target_pairs={{0,2},{2,4},{4,6},{6,8},{8,10},{10,12},{12,14},{14,16},{16,18},{18... | collective-permute-start | bytes 2359304 | tf_op jit(solution)/shard_map/ppermute | solution.py:119
  33.7 108.2 %collective-permute-start.1 = (bf16[2,64,3072]{2,1,0:T(8,128)(2,1)}, bf16[2,64,3072]{2,1,0:T(8,128)(2,1)}, u32[]{:S(2)}, u32[]{:S(2)}) collective-permute-start(bf16[2,64,3072]{2,1,0:T(8,128)(2,1)} %pad_maximum_fusion.1), channel_id=1, source_target_pairs={{2,0},{4,2},{6,4},{8,6},{10,8},{12,10},{14,12},{16,14},{18,16},{20... | collective-permute-start | bytes 2359304 | tf_op jit(solution)/shard_map/ppermute | solution.py:119
  178.1 0.8 copy-start.9
  178.9 13.0 %copy-start.10 = (bf16[64,3072]{1,0:T(8,128)(2,1)S(1)}, bf16[64,3072]{1,0:T(8,128)(2,1)}, u32[]{:S(2)}) copy-start(bf16[64,3072]{1,0:T(8,128)(2,1)} %copy-done.9) | copy-start | bytes 1179652
  178.9 117.4 %copy-start.4 = (f32[128,3072]{1,0:T(8,128)S(1)}, f32[128,3072]{1,0:T(8,128)}, u32[]{:S(2)}) copy-start(f32[128,3072]{1,0:T(8,128)} %get-tuple-element.14.dk_ref) | copy-start | bytes 4718596
  178.9 108.7 %all-to-all-start.3 = ((bf16[16,9,64,256]{3,2,1,0:T(8,128)(2,1)}), bf16[16,9,64,256]{3,2,1,0:T(8,128)(2,1)}, u32[]{:S(2)}, u32[]{:S(2)}) async-start(bf16[16,9,64,256]{3,2,1,0:T(8,128)(2,1)} %bitcast.29), calls=%async_computation.3 | async-start | bytes 9437184 | tf_op jit(solution)/shard_map/all_to_all | solution.py:183
  183.5 108.5 %collective-permute-start.2 = (bf16[64,3072]{1,0:T(8,128)(2,1)}, bf16[64,3072]{1,0:T(8,128)(2,1)S(1)}, u32[]{:S(2)}, u32[]{:S(2)}) collective-permute-start(bf16[64,3072]{1,0:T(8,128)(2,1)} %get-tuple-element.16), channel_id=1, source_target_pairs={{0,2},{2,4},{4,6},{6,8},{8,10},{10,12},{12,14},{14,16},{16,18},{18... | collective-permute-start | bytes 1179656 | tf_op jit(solution)/shard_map/ppermute | solution.py:119
  185.4 110.1 %collective-permute-start.3 = (bf16[64,3072]{1,0:T(8,128)(2,1)}, bf16[64,3072]{1,0:T(8,128)(2,1)S(1)}, u32[]{:S(2)}, u32[]{:S(2)}) collective-permute-start(bf16[64,3072]{1,0:T(8,128)(2,1)} %get-tuple-element.17), channel_id=1, source_target_pairs={{0,2},{2,4},{4,6},{6,8},{8,10},{10,12},{12,14},{14,16},{16,18},{18... | collective-permute-start | bytes 1179656 | tf_op jit(solution)/shard_map/ppermute | solution.py:119
  188.6 106.9 %collective-permute-start.4 = (bf16[64,3072]{1,0:T(8,128)(2,1)}, bf16[64,3072]{1,0:T(8,128)(2,1)S(1)}, u32[]{:S(2)}, u32[]{:S(2)}) collective-permute-start(bf16[64,3072]{1,0:T(8,128)(2,1)} %get-tuple-element.18), channel_id=1, source_target_pairs={{2,0},{4,2},{6,4},{8,6},{10,8},{12,10},{14,12},{16,14},{18,16},{20... | collective-permute-start | bytes 1179656 | tf_op jit(solution)/shard_map/ppermute | solution.py:119
  191.9 103.6 %collective-permute-start.5 = (bf16[64,3072]{1,0:T(8,128)(2,1)S(1)}, bf16[64,3072]{1,0:T(8,128)(2,1)S(1)}, u32[]{:S(2)}, u32[]{:S(2)}) collective-permute-start(bf16[64,3072]{1,0:T(8,128)(2,1)S(1)} %copy-done.10), channel_id=1, source_target_pairs={{2,0},{4,2},{6,4},{8,6},{10,8},{12,10},{14,12},{16,14},{18,16},{20... | collective-permute-start | bytes 1179656 | tf_op jit(solution)/shard_map/ppermute | solution.py:119
  287.6 17.8 %all-to-all-start.2 = ((bf16[2,64,3072]{2,1,0:T(8,128)(2,1)}), bf16[2,64,3072]{2,1,0:T(8,128)(2,1)}, u32[]{:S(2)}, u32[]{:S(2)}) async-start(bf16[2,64,3072]{2,1,0:T(8,128)(2,1)} %bitcast.9), calls=%async_computation.2 | async-start | bytes 1572864 | tf_op jit(solution)/shard_map/all_to_all | solution.py:199
  295.5 0.7 copy-start.7
  296.3 1.0 copy-start.8
  316.0 11.5 %all-to-all-start.4 = ((bf16[2,64,3072]{2,1,0:T(8,128)(2,1)}), bf16[2,64,3072]{2,1,0:T(8,128)(2,1)S(1)}, u32[]{:S(2)}, u32[]{:S(2)}) async-start(bf16[2,64,3072]{2,1,0:T(8,128)(2,1)} %bitcast.13), calls=%async_computation.4 | async-start | bytes 1572864 | tf_op jit(solution)/shard_map/all_to_all | solution.py:199

commit v2 on v1

--- a/solution.py
+++ b/solution.py
@@ -28,19 +28,68 @@
         o_ref[j, :, dim:] = v_ref[rows, cols]
 
 
+def column(ref, index, cols, blocks, block, up, down):
+    inner = [ref[b * block:(b + 1) * block, cols] for b in range(blocks)]
+    return [up[index, :, cols]] + inner + [down[index, :, cols]]
+
+
 def attend_kernel(
     blocks, block, dim, heads, rand, step, scale,
     slots, edge, q_ref, k_ref, v_ref, g_ref, up_ref, down_ref, far_ref,
-    dq_ref, dk_ref, dv_ref, tok_ref, tov_ref, tnk_ref, tnv_ref, out_ref,
+    p_ref, ds_ref, out_ref,
+):
+    group = pl.program_id(0)
+    units = [(j, b) for j in range(step) for b in range(blocks)]
+    at, scores, wgrads, vals, qs, gs = [], [], [], [], [], []
+    for j, b in units:
+        cols = slice(j * dim, (j + 1) * dim)
+        rows = slice(b * block, (b + 1) * block)
+        head = group * step + j
+        at.append([slots[(b * heads + head) * rand + r] for r in range(rand)])
+        ks = column(k_ref, 0, cols, blocks, block, up_ref, down_ref)
+        vs = column(v_ref, 1, cols, blocks, block, up_ref, down_ref)
+        keys = jnp.concatenate(ks[b:b + 3] + [far_ref[s, :, :dim] for s in at[-1]], axis=0)
+        vals.append(jnp.concatenate(vs[b:b + 3] + [far_ref[s, :, dim:] for s in at[-1]], axis=0))
+        qs.append(q_ref[rows, cols])
+        gs.append(g_ref[rows, cols])
+        scores.append(scale * dot(qs[-1], keys, 1, 1))
+        wgrads.append(dot(gs[-1], vals[-1], 1, 1))
+    place = lax.broadcasted_iota(jnp.int32, scores[0].shape, 1)
+    for n, (j, b) in enumerate(units):
+        if b == 0:
+            scores[n] = jnp.where((place < block) & (edge[0] == 0), -jnp.inf, scores[n])
+        if b == blocks - 1:
+            off = (place >= 2 * block) & (place < 3 * block) & (edge[1] == 0)
+            scores[n] = jnp.where(off, -jnp.inf, scores[n])
+    tops = [jnp.max(s, axis=1, keepdims=True) for s in scores]
+    es = [jnp.exp(s - t) for s, t in zip(scores, tops)]
+    ws = [e * (1.0 / jnp.sum(e, axis=1, keepdims=True)) for e in es]
+    ps = [w.astype(BF16) for w in ws]
+    outs = [dot(p, v, 1, 0).astype(BF16).astype(F32) for p, v in zip(ps, vals)]
+    deltas = [jnp.sum(o * g.astype(F32), axis=1, keepdims=True) for o, g in zip(outs, gs)]
+    dss = [(w * (wg - d)).astype(BF16) for w, wg, d in zip(ws, wgrads, deltas)]
+    dks = [(scale * dot(ds[:, 3 * block:], q, 0, 0)).astype(BF16) for ds, q in zip(dss, qs)]
+    dvs = [dot(p[:, 3 * block:], g, 0, 0).astype(BF16) for p, g in zip(ps, gs)]
+    for n, (j, b) in enumerate(units):
+        rows = slice(b * block, (b + 1) * block)
+        p_ref[j, rows] = ps[n][:, :3 * block]
+        ds_ref[j, rows] = dss[n]
+        for r in range(rand):
+            part = slice(r * block, (r + 1) * block)
+            out_ref[at[n][r], :, :dim] = dks[n][part]
+            out_ref[at[n][r], :, dim:] = dvs[n][part]
+
+
+def window_kernel(
+    blocks, block, dim, heads, rand, step, scale,
+    slots, q_ref, k_ref, g_ref, up_ref, down_ref, far_ref, p_ref, ds_ref,
+    dq_ref, dk_ref, dv_ref, tok_ref, tov_ref, tnk_ref, tnv_ref,
 ):
     group = pl.program_id(0)
     for j in range(step):
         head = group * step + j
         cols = slice(j * dim, (j + 1) * dim)
-        ks = [up_ref[0, :, cols]] + [k_ref[b * block:(b + 1) * block, cols] for b in range(blocks)]
-        ks.append(down_ref[0, :, cols])
-        vs = [up_ref[1, :, cols]] + [v_ref[b * block:(b + 1) * block, cols] for b in range(blocks)]
-        vs.append(down_ref[1, :, cols])
+        ks = column(k_ref, 0, cols, blocks, block, up_ref, down_ref)
         gk = [None] * (blocks + 2)
         gv = [None] * (blocks + 2)
         for b in range(blocks):
@@ -49,33 +98,14 @@
             g = g_ref[rows, cols]
             at = [slots[(b * heads + head) * rand + r] for r in range(rand)]
             keys = jnp.concatenate(ks[b:b + 3] + [far_ref[s, :, :dim] for s in at], axis=0)
-            vals = jnp.concatenate(vs[b:b + 3] + [far_ref[s, :, dim:] for s in at], axis=0)
-            s = scale * dot(q, keys, 1, 1)
-            place = lax.broadcasted_iota(jnp.int32, s.shape, 1)
-            if b == 0:
-                s = jnp.where((place < block) & (edge[0] == 0), -jnp.inf, s)
-            if b == blocks - 1:
-                s = jnp.where(
-                    (place >= 2 * block) & (place < 3 * block) & (edge[1] == 0), -jnp.inf, s
-                )
-            top = jnp.max(s, axis=1, keepdims=True)
-            e = jnp.exp(s - top)
-            w = e * (1.0 / jnp.sum(e, axis=1, keepdims=True))
-            p = w.astype(BF16)
-            o = dot(p, vals, 1, 0).astype(BF16).astype(F32)
-            delta = jnp.sum(o * g.astype(F32), axis=1, keepdims=True)
-            ds = (w * (dot(g, vals, 1, 1) - delta)).astype(BF16)
+            ds = ds_ref[j, rows]
             dq_ref[rows, cols] = (scale * dot(ds, keys, 1, 0)).astype(BF16)
-            dk = scale * dot(ds, q, 0, 0)
-            dv = dot(p, g, 0, 0)
+            dk = scale * dot(ds[:, :3 * block], q, 0, 0)
+            dv = dot(p_ref[j, rows], g, 0, 0)
             for i in range(3):
                 part = slice(i * block, (i + 1) * block)
                 gk[b + i] = dk[part] if gk[b + i] is None else gk[b + i] + dk[part]
                 gv[b + i] = dv[part] if gv[b + i] is None else gv[b + i] + dv[part]
-            for r in range(rand):
-                part = slice((3 + r) * block, (4 + r) * block)
-                out_ref[at[r], :, :dim] = dk[part].astype(BF16)
-                out_ref[at[r], :, dim:] = dv[part].astype(BF16)
         tok_ref[:, cols] = gk[0].astype(BF16)
         tov_ref[:, cols] = gv[0].astype(BF16)
         tnk_ref[:, cols] = gk[-1].astype(BF16)
@@ -117,6 +147,19 @@
     count = lax.axis_size(axis)
     first, last = (max(0, -steps), min(count, count - steps))
     return lax.ppermute(value, axis, [(source, source + steps) for source in range(first, last)])
+
+
+def exchanged(x, axis):
+    count = lax.axis_size(axis)
+    me = lax.axis_index(axis)
+    rows, width = x.shape[0] // count, x.shape[1]
+    out = jnp.zeros((rows, count * width), x.dtype)
+    for r in range(count):
+        piece = lax.dynamic_slice_in_dim(x, (me + r) % count * rows, rows, 0)
+        if r:
+            piece = lax.ppermute(piece, axis, [(i, (i + r) % count) for i in range(count)])
+        out = lax.dynamic_update_slice_in_dim(out, piece, (me - r) % count * width, 1)
+    return out
 
 
 def local(queries, key_rows, value_rows, out_grad, partner):
@@ -142,6 +185,9 @@
         asked.reshape(peers, cap), "seq", split_axis=0, concat_axis=0, tiled=True
     ).reshape(count)
     full = pl.BlockSpec(memory_space=VMEM)
+    up = shifted(jnp.stack([key_rows[tokens - block:], value_rows[tokens - block:]]), "seq", 1)
+    down = shifted(jnp.stack([key_rows[:block], value_rows[:block]]), "seq", -1)
+    asked, up, down = lax.optimization_barrier((asked, up, down))
     outgoing = pl.pallas_call(
         functools.partial(gather_kernel, block, dim, heads, cap),
         out_shape=jax.ShapeDtypeStruct((count, block, 2 * dim), BF16),
@@ -156,8 +202,6 @@
     fetched = lax.all_to_all(
         outgoing.reshape(peers, cap, block, 2 * dim), "seq", split_axis=0, concat_axis=0, tiled=True
     ).reshape(count, block, 2 * dim)
-    up = shifted(jnp.stack([key_rows[tokens - block:], value_rows[tokens - block:]]), "seq", 1)
-    down = shifted(jnp.stack([key_rows[:block], value_rows[:block]]), "seq", -1)
     edge = jnp.stack([(me > 0), (me < peers - 1)]).astype(jnp.int32)
     step = next(n for n in (4, 3, 2, 1) if heads % n == 0)
     wide = pl.BlockSpec((tokens, step * dim), lambda i, *_: (0, i))
@@ -166,20 +210,41 @@
     far = pl.BlockSpec((count, block, 2 * dim), lambda i, *_: (0, 0, 0))
     half = jax.ShapeDtypeStruct((block, width), BF16)
     whole = jax.ShapeDtypeStruct((tokens, width), F32)
-    dq, dk, dv, tok, tov, tnk, tnv, outbound = pl.pallas_call(
+    span = 3 * block
+    probs = pl.BlockSpec((step, tokens, span), lambda i, *_: (i, 0, 0))
+    grads = pl.BlockSpec((step, tokens, span + rand * block), lambda i, *_: (i, 0, 0))
+    work = heads * tokens * (span + rand * block) * dim
+    cost = pl.CostEstimate(flops=8 * work, bytes_accessed=16 * 2**20, transcendentals=0)
+    p, ds, outbound = pl.pallas_call(
         functools.partial(attend_kernel, blocks, block, dim, heads, rand, step, scale),
         out_shape=[
-            jax.ShapeDtypeStruct((tokens, width), BF16), whole, whole, half, half, half, half,
+            jax.ShapeDtypeStruct((heads, tokens, span), BF16),
+            jax.ShapeDtypeStruct((heads, tokens, span + rand * block), BF16),
             jax.ShapeDtypeStruct((count, block, 2 * dim), BF16),
         ],
         grid_spec=pltpu.PrefetchScalarGridSpec(
             num_scalar_prefetch=2,
             grid=(heads // step,),
             in_specs=[wide, wide, wide, wide, side, side, far],
-            out_specs=[wide, wide, wide, thin, thin, thin, thin, far],
+            out_specs=[probs, grads, far],
         ),
         compiler_params=pltpu.CompilerParams(vmem_limit_bytes=LIMIT),
+        cost_estimate=cost,
     )(slot, edge, queries, key_rows, value_rows, out_grad, up, down, fetched)
+    dq, dk, dv, tok, tov, tnk, tnv = pl.pallas_call(
+        functools.partial(window_kernel, blocks, block, dim, heads, rand, step, scale),
+        out_shape=[
+            jax.ShapeDtypeStruct((tokens, width), BF16), whole, whole, half, half, half, half,
+        ],
+        grid_spec=pltpu.PrefetchScalarGridSpec(
+            num_scalar_prefetch=1,
+            grid=(heads // step,),
+            in_specs=[wide, wide, wide, side, side, far, probs, grads],
+            out_specs=[wide, wide, wide, thin, thin, thin, thin],
+        ),
+        compiler_params=pltpu.CompilerParams(vmem_limit_bytes=LIMIT),
+        cost_estimate=cost,
+    )(slot, queries, key_rows, out_grad, up, down, fetched, p, ds)
     inbound = lax.all_to_all(
         outbound.reshape(peers, cap, block, 2 * dim), "seq", split_axis=0, concat_axis=0, tiled=True
     ).reshape(count, block, 2 * dim)
@@ -195,10 +260,7 @@
         scratch_shapes=[VMEM((tokens, width), F32), VMEM((tokens, width), F32)],
         compiler_params=pltpu.CompilerParams(vmem_limit_bytes=LIMIT),
     )(asked, dk, dv, above_k, above_v, below_k, below_v, inbound)
-    return tuple(
-        lax.all_to_all(x, "head", split_axis=0, concat_axis=1, tiled=True)
-        for x in (dq, k_rows, v_rows)
-    )
+    return exchanged(dq, "head"), exchanged(k_rows, "head"), exchanged(v_rows, "head")
 
 
 def solution(mesh):

time: 333 us -> 302 us (0.907)
  Pallas kernels: 51.4 us -> 38.6 us
  starting transfers between devices: 36.5 us -> 30.2 us
  blocking collectives: 20.7 us -> 15.8 us
  waiting for transfers between devices: 206 us -> 202 us
    all_to_all x1, waiting for transfers between devices: 0.01 us -> 104 us  [local(): lax.all_to_all(outgoing.reshape(peers, cap, block, 2 * dim), 'seq', split...]
    all_to_all x1, waiting for transfers between devices: 93.3 us -> 0.01 us  [local(): lax.all_to_all(outbound.reshape(peers, cap, block, 2 * dim), 'seq', split...]
    pallas_call x1, Pallas kernels: 36.2 us -> 14.8 us  [local(): pl.pallas_call(functools.partial(attend_kernel, blocks, block, dim, heads...]
    ppermute x6, waiting for transfers between devices: 107 us -> 88.5 us  [shifted(): lax.ppermute(value, axis, [(source, source + steps) for source in range(f...]
    all_to_all x1 -> x0, blocking collectives: 10.6 us -> none  [local(): lax.all_to_all(x, 'head', split_axis=0, concat_axis=1, tiled=True)]
    ppermute x0 -> x3, waiting for transfers between devices: none -> 9.68 us  [exchanged(): lax.ppermute(piece, axis, [(i, (i + r) % count) for i in range(count)])]
    pallas_call x0 -> x1, Pallas kernels: none -> 9.19 us  [local(): pl.pallas_call(functools.partial(window_kernel, blocks, block, dim, heads...]
    all_to_all x2 -> x0, starting transfers between devices: 7.84 us -> none  [local(): lax.all_to_all(x, 'head', split_axis=0, concat_axis=1, tiled=True)]
  transfers between devices with their start and end apart: 10 -> 11, of which waited for: 4 -> 5; matrix products, arithmetic and copies ran while one was open for 2% -> 1% of each run, Pallas kernels for 2% -> 6%
where the time goes in v2:
time: 302 us; the launch traced here: 300 us
  waiting for transfers between devices  202 us (67%)
  Pallas kernels  38.6 us (13%)
  starting transfers between devices  30.2 us (10%)
  blocking collectives  15.8 us (5%)
  local copies, waits for them, and re-layouts  9.51 us (3%)
    all_to_all x1, waiting for transfers between devices, local(): lax.all_to_all(outgoing.reshape(peers, cap, block, 2 * dim), 'seq', split...  104 us
    ppermute x6, waiting for transfers between devices, shifted(): lax.ppermute(value, axis, [(source, source + steps) for source in range(f...  88.5 us
    all_to_all x1, blocking collectives, local(): lax.all_to_all(asked.reshape(peers, cap), 'seq', split_axis=0, concat_axi...  15.8 us
    ppermute x6, starting transfers between devices, shifted(): lax.ppermute(value, axis, [(source, source + steps) for source in range(f...  15.4 us
    pallas_call x1, Pallas kernels, local(): pl.pallas_call(functools.partial(attend_kernel, blocks, block, dim, heads...  14.8 us
    ppermute x3, waiting for transfers between devices, exchanged(): lax.ppermute(piece, axis, [(i, (i + r) % count) for i in range(count)])  9.68 us
    pallas_call x1, Pallas kernels, local(): pl.pallas_call(functools.partial(window_kernel, blocks, block, dim, heads...  9.19 us
    pallas_call x1, Pallas kernels, local(): pl.pallas_call(functools.partial(collect_kernel, blocks, block, dim, head...  7.53 us
  transfers between devices with their start and end apart: 11, of which 5 were waited for; matrix products, arithmetic and copies ran while one was open for 1% of the time, Pallas kernels for 6%

profile of v2, /device:TPU:16, one launch (start us, length us, event | category | flops | bytes accessed | tf_op | source)
XLA Modules:
  0.0 300.1 jit_solution(17269251878374442013)
XLA Ops:
  0.6 0.0 copy-start
  0.6 0.0 copy-start.1
  0.7 0.0 copy-start.14
  0.7 1.6 slice_bitcast_fusion
  2.2 0.9 pad_maximum_fusion.1
  3.2 2.7 collective-permute-start.1
  5.9 0.9 pad_maximum_fusion
  6.9 1.9 collective-permute-start
  8.8 0.0 copy-done.14
  8.8 0.1 copy.12
  8.9 0.1 reshape.154
  9.0 0.2 convert_reduce_fusion
  9.2 0.1 select_reduce_fusion
  9.4 0.1 sub.24
  9.5 15.8 %all_to_all.16 = s32[16,1,9]{2,1,0:T(1,128)S(1)} all-to-all(s32[16,1,9]{2,1,0:T(1,128)S(1)} %bitcast.17), channel_id=1, replica_groups=mesh['seq'=16,'head'=2] {'seq'}, dimensions={0} | all-to-all | bytes 1152 | tf_op jit(solution)/shard_map/all_to_all | solution.py:184
  25.3 0.5 broadcast.201
  25.8 0.7 reduce.3
  26.4 0.1 reshape.155.codes
  26.5 0.0 collective-permute-done.1.down_ref
  26.5 0.0 copy-start.4
  26.6 0.0 collective-permute-done.up_ref
  26.6 0.0 copy-done
  26.6 0.0 copy-start.6
  26.6 7.1 %shard_map.76 = bf16[144,64,256]{2,1,0:T(8,128)(2,1)} custom-call(s32[144]{0:T(256)S(1)} %reshape.155.codes, bf16[128,3072]{1,0:T(8,128)(2,1)S(1)} %copy-done, bf16[128,3072]{1,0:T(8,128)(2,1)S(1)} %copy-done.1), custom_call_target="tpu_custom_call" | custom-call | tf_op jit(solution)/shard_map/pallas_call | solution.py:191
  33.7 0.0 copy-done.4
  33.7 6.2 %all-to-all-start.1 = ((bf16[16,9,64,256]{3,2,1,0:T(8,128)(2,1)}), bf16[16,9,64,256]{3,2,1,0:T(8,128)(2,1)}, u32[]{:S(2)}, u32[]{:S(2)}) async-start(bf16[16,9,64,256]{3,2,1,0:T(8,128)(2,1)} %bitcast.15), calls=%async_computation.1 | async-start | bytes 9437184 | tf_op jit(solution)/shard_map/all_to_all | solution.py:202
  40.0 0.1 add_convert_fusion.edge
  40.0 103.9 %all-to-all-done.1 = bf16[16,9,64,256]{3,2,1,0:T(8,128)(2,1)} async-done(((bf16[16,9,64,256]{3,2,1,0:T(8,128)(2,1)}), bf16[16,9,64,256]{3,2,1,0:T(8,128)(2,1)}, u32[]{:S(2)}, u32[]{:S(2)}) %all-to-all-start.1) | async-done | bytes 4718624 | tf_op jit(solution)/shard_map/all_to_all | solution.py:202
  143.9 0.0 copy-done.3
  143.9 1.1 copy-done.5
  145.0 1.1 copy-done.7
  146.2 14.8 %shard_map.77 = (bf16[24,128,192]{2,1,0:T(8,128)(2,1)}, bf16[24,128,320]{2,1,0:T(8,128)(2,1)}, bf16[144,64,256]{2,1,0:T(8,128)(2,1)}) custom-call(s32[96]{0:T(128)S(1)} %multiply_add_fusion.slots, s32[2]{0:T(128)S(1)} %add_convert_fusion.edge, bf16[128,3072]{1,0:T(8,128)(2,1)S(1)} %copy-done.2, bf16[128,3072]{1,0:T(8,128)(2,1)S(1)} %copy-done, ...), custom_call_target="tpu_custom_call" | custom-call | flops 1006632960 | bytes 16777216 | tf_op jit(solution)/shard_map/pallas_call | solution.py:218
  160.9 4.8 %all-to-all-start.2 = ((bf16[16,9,64,256]{3,2,1,0:T(8,128)(2,1)}), bf16[16,9,64,256]{3,2,1,0:T(8,128)(2,1)}, u32[]{:S(2)}, u32[]{:S(2)}) async-start(bf16[16,9,64,256]{3,2,1,0:T(8,128)(2,1)} %bitcast.16), calls=%async_computation.2 | async-start | bytes 9437184 | tf_op jit(solution)/shard_map/all_to_all | solution.py:248
  165.8 9.2 %shard_map.78 = (bf16[128,3072]{1,0:T(8,128)(2,1)S(1)}, f32[128,3072]{1,0:T(8,128)}, f32[128,3072]{1,0:T(8,128)}, bf16[64,3072]{1,0:T(8,128)(2,1)}, bf16[64,3072...) custom-call(s32[96]{0:T(128)S(1)} %multiply_add_fusion.slots, ...), custom_call_target="tpu_custom_call" | custom-call | flops 1006632960 | bytes 16777216 | tf_op jit(solution)/shard_map/pallas_call | solution.py:234
  174.9 0.9 copy-done.10
  175.8 2.0 collective-permute-start.3
  177.9 3.3 %collective-permute-start.4 = (bf16[64,3072]{1,0:T(8,128)(2,1)}, bf16[64,3072]{1,0:T(8,128)(2,1)S(1)}, u32[]{:S(2)}, u32[]{:S(2)}) collective-permute-start(bf16[64,3072]{1,0:T(8,128)(2,1)} %get-tuple-element.27), channel_id=1, source_target_pairs={{0,2},{2,4},{4,6},{6,8},{8,10},{10,12},{12,14},{14,16},{16,18},{18... | collective-permute-start | bytes 1179656 | tf_op jit(solution)/shard_map/ppermute | solution.py:149
  181.2 3.1 %collective-permute-start.5 = (bf16[64,3072]{1,0:T(8,128)(2,1)}, bf16[64,3072]{1,0:T(8,128)(2,1)S(1)}, u32[]{:S(2)}, u32[]{:S(2)}) collective-permute-start(bf16[64,3072]{1,0:T(8,128)(2,1)} %get-tuple-element.28), channel_id=1, source_target_pairs={{2,0},{4,2},{6,4},{8,6},{10,8},{12,10},{14,12},{16,14},{18,16},{20... | collective-permute-start | bytes 1179656 | tf_op jit(solution)/shard_map/ppermute | solution.py:149
  184.4 2.3 collective-permute-start.6
  186.7 0.1 broadcast.179.clone
  186.7 1.2 constant_dynamic-slice_fusion.1
  187.9 1.5 collective-permute-start.2
  189.5 84.3 %collective-permute-done.3.ak_ref = bf16[64,3072]{1,0:T(8,128)(2,1)S(1)} collective-permute-done((bf16[64,3072]{1,0:T(8,128)(2,1)}, bf16[64,3072]{1,0:T(8,128)(2,1)S(1)}, u32[]{:S(2)}, u32[]{:S(2)}) %collective-permute-start.3) | collective-permute-done | bytes 393248 | tf_op jit(solution)/shard_map/ppermute | solution.py:149
  273.8 4.2 %collective-permute-done.4.av_ref = bf16[64,3072]{1,0:T(8,128)(2,1)S(1)} collective-permute-done((bf16[64,3072]{1,0:T(8,128)(2,1)}, bf16[64,3072]{1,0:T(8,128)(2,1)S(1)}, u32[]{:S(2)}, u32[]{:S(2)}) %collective-permute-start.4) | collective-permute-done | bytes 393248 | tf_op jit(solution)/shard_map/ppermute | solution.py:149
  278.0 0.0 collective-permute-done.5.bk_ref
  278.0 0.0 collective-permute-done.6.bv_ref
  278.0 0.0 all-to-all-done.2
  278.0 1.4 copy-done.9
  279.4 7.5 %shard_map.79 = (bf16[128,3072]{1,0:T(8,128)(2,1)S(1)}, bf16[128,3072]{1,0:T(8,128)(2,1)S(1)}) custom-call(s32[144]{0:T(256)S(1)} %reshape.155.codes, f32[128,3072]{1,0:T(8,128)S(1)} %copy-done.9, f32[128,3072]{1,0:T(8,128)} %get-tuple-element.25.dv_ref, bf16[64,3072]{1,0:T(8,128)(2,1)S(1)} %collective-permute-done.3.ak_ref, ...), custom_call_target="tpu_custom_call" | custom-call | tf_op jit(solution)/shard_map/pallas_call | solution.py:255
  287.0 0.1 broadcast.179.clone.2
  287.0 0.1 constant_dynamic-slice_fusion.2
  287.1 1.2 collective-permute-start.8
  288.4 0.1 broadcast.179.clone.1
  288.4 0.1 constant_dynamic-slice_fusion
  288.5 0.9 collective-permute-start.7
  289.4 0.0 collective-permute-done.2
  289.4 0.0 copy-start.12
  289.4 5.5 %collective-permute-done.8 = bf16[64,3072]{1,0:T(8,128)(2,1)S(1)} collective-permute-done((bf16[64,3072]{1,0:T(8,128)(2,1)S(1)}, bf16[64,3072]{1,0:T(8,128)(2,1)S(1)}, u32[]{:S(2)}, u32[]{:S(2)}) %collective-permute-start.8) | collective-permute-done | bytes 393248 | tf_op jit(solution)/shard_map/ppermute | solution.py:160
  295.0 0.0 copy-start.13
  295.0 4.2 %collective-permute-done.7 = bf16[64,3072]{1,0:T(8,128)(2,1)S(1)} collective-permute-done((bf16[64,3072]{1,0:T(8,128)(2,1)S(1)}, bf16[64,3072]{1,0:T(8,128)(2,1)S(1)}, u32[]{:S(2)}, u32[]{:S(2)}) %collective-permute-start.7) | collective-permute-done | bytes 393248 | tf_op jit(solution)/shard_map/ppermute | solution.py:160
  299.2 0.0 copy-done.12
  299.2 0.0 copy-done.13
  299.2 0.0 copy-start.11
  299.2 0.9 copy-done.11
  (17 shorter events, 0.1 us)
Async XLA Ops:
  0.6 25.9 %copy-start = (bf16[128,3072]{1,0:T(8,128)(2,1)S(1)}, bf16[128,3072]{1,0:T(8,128)(2,1)}, u32[]{:S(2)}) copy-start(bf16[128,3072]{1,0:T(8,128)(2,1)} %k_ref.5) | copy-start | bytes 2359300
  0.6 25.9 %copy-start.1 = (bf16[128,3072]{1,0:T(8,128)(2,1)S(1)}, bf16[128,3072]{1,0:T(8,128)(2,1)}, u32[]{:S(2)}) copy-start(bf16[128,3072]{1,0:T(8,128)(2,1)} %v_ref.3) | copy-start | bytes 2359300
  0.7 8.2 %copy-start.14 = (s32[2,24,2]{1,2,0:T(2,128)S(1)}, s32[2,24,2]{1,2,0:T(2,128)}, u32[]{:S(2)}) copy-start(s32[2,24,2]{1,2,0:T(2,128)} %param.9) | copy-start | bytes 1156
  3.2 23.3 %collective-permute-start.1 = (bf16[2,64,3072]{2,1,0:T(8,128)(2,1)}, bf16[2,64,3072]{2,1,0:T(8,128)(2,1)S(1)}, u32[]{:S(2)}, u32[]{:S(2)}) collective-permute-start(bf16[2,64,3072]{2,1,0:T(8,128)(2,1)} %pad_maximum_fusion.1), channel_id=1, source_target_pairs={{2,0},{4,2},{6,4},{8,6},{10,8},{12,10},{14,12},{16,14},{18,16},{20... | collective-permute-start | bytes 2359304 | tf_op jit(solution)/shard_map/ppermute | solution.py:149
  6.9 19.7 %collective-permute-start = (bf16[2,64,3072]{2,1,0:T(8,128)(2,1)}, bf16[2,64,3072]{2,1,0:T(8,128)(2,1)S(1)}, u32[]{:S(2)}, u32[]{:S(2)}) collective-permute-start(bf16[2,64,3072]{2,1,0:T(8,128)(2,1)} %pad_maximum_fusion), channel_id=1, source_target_pairs={{0,2},{2,4},{4,6},{6,8},{8,10},{10,12},{12,14},{14,16},{16,18},{18... | collective-permute-start | bytes 2359304 | tf_op jit(solution)/shard_map/ppermute | solution.py:149
  26.5 7.2 %copy-start.4 = (bf16[2,64,3072]{2,1,0:T(8,128)(2,1)}, bf16[2,64,3072]{2,1,0:T(8,128)(2,1)S(1)}, u32[]{:S(2)}) copy-start(bf16[2,64,3072]{2,1,0:T(8,128)(2,1)S(1)} %collective-permute-done.1.down_ref) | copy-start | bytes 2359300
  26.6 7.1 %copy-start.6 = (bf16[2,64,3072]{2,1,0:T(8,128)(2,1)}, bf16[2,64,3072]{2,1,0:T(8,128)(2,1)S(1)}, u32[]{:S(2)}) copy-start(bf16[2,64,3072]{2,1,0:T(8,128)(2,1)S(1)} %collective-permute-done.up_ref) | copy-start | bytes 2359300
  33.7 110.2 %copy-start.2 = (bf16[128,3072]{1,0:T(8,128)(2,1)S(1)}, bf16[128,3072]{1,0:T(8,128)(2,1)}, u32[]{:S(2)}) copy-start(bf16[128,3072]{1,0:T(8,128)(2,1)} %q_ref.3) | copy-start | bytes 2359300
  33.7 110.2 %copy-start.3 = (bf16[128,3072]{1,0:T(8,128)(2,1)S(1)}, bf16[128,3072]{1,0:T(8,128)(2,1)}, u32[]{:S(2)}) copy-start(bf16[128,3072]{1,0:T(8,128)(2,1)} %g_ref.3) | copy-start | bytes 2359300
  33.7 110.2 %all-to-all-start.1 = ((bf16[16,9,64,256]{3,2,1,0:T(8,128)(2,1)}), bf16[16,9,64,256]{3,2,1,0:T(8,128)(2,1)}, u32[]{:S(2)}, u32[]{:S(2)}) async-start(bf16[16,9,64,256]{3,2,1,0:T(8,128)(2,1)} %bitcast.15), calls=%async_computation.1 | async-start | bytes 9437184 | tf_op jit(solution)/shard_map/all_to_all | solution.py:202
  143.9 1.1 copy-start.5
  145.0 1.1 copy-start.7
  160.9 4.8 %copy-start.8 = (bf16[2,64,3072]{2,1,0:T(8,128)(2,1)S(1)}, bf16[2,64,3072]{2,1,0:T(8,128)(2,1)}, u32[]{:S(2)}) copy-start(bf16[2,64,3072]{2,1,0:T(8,128)(2,1)} %copy-done.6) | copy-start | bytes 2359300
  160.9 117.1 %all-to-all-start.2 = ((bf16[16,9,64,256]{3,2,1,0:T(8,128)(2,1)}), bf16[16,9,64,256]{3,2,1,0:T(8,128)(2,1)}, u32[]{:S(2)}, u32[]{:S(2)}) async-start(bf16[16,9,64,256]{3,2,1,0:T(8,128)(2,1)} %bitcast.16), calls=%async_computation.2 | async-start | bytes 9437184 | tf_op jit(solution)/shard_map/all_to_all | solution.py:248
  174.9 0.9 copy-start.10
  175.8 98.0 %collective-permute-start.3 = (bf16[64,3072]{1,0:T(8,128)(2,1)}, bf16[64,3072]{1,0:T(8,128)(2,1)S(1)}, u32[]{:S(2)}, u32[]{:S(2)}) collective-permute-start(bf16[64,3072]{1,0:T(8,128)(2,1)} %get-tuple-element.26), channel_id=1, source_target_pairs={{0,2},{2,4},{4,6},{6,8},{8,10},{10,12},{12,14},{14,16},{16,18},{18... | collective-permute-start | bytes 1179656 | tf_op jit(solution)/shard_map/ppermute | solution.py:149
  177.9 100.1 %collective-permute-start.4 = (bf16[64,3072]{1,0:T(8,128)(2,1)}, bf16[64,3072]{1,0:T(8,128)(2,1)S(1)}, u32[]{:S(2)}, u32[]{:S(2)}) collective-permute-start(bf16[64,3072]{1,0:T(8,128)(2,1)} %get-tuple-element.27), channel_id=1, source_target_pairs={{0,2},{2,4},{4,6},{6,8},{8,10},{10,12},{12,14},{14,16},{16,18},{18... | collective-permute-start | bytes 1179656 | tf_op jit(solution)/shard_map/ppermute | solution.py:149
  181.2 96.8 %collective-permute-start.5 = (bf16[64,3072]{1,0:T(8,128)(2,1)}, bf16[64,3072]{1,0:T(8,128)(2,1)S(1)}, u32[]{:S(2)}, u32[]{:S(2)}) collective-permute-start(bf16[64,3072]{1,0:T(8,128)(2,1)} %get-tuple-element.28), channel_id=1, source_target_pairs={{2,0},{4,2},{6,4},{8,6},{10,8},{12,10},{14,12},{16,14},{18,16},{20... | collective-permute-start | bytes 1179656 | tf_op jit(solution)/shard_map/ppermute | solution.py:149
  184.4 93.7 %collective-permute-start.6 = (bf16[64,3072]{1,0:T(8,128)(2,1)S(1)}, bf16[64,3072]{1,0:T(8,128)(2,1)S(1)}, u32[]{:S(2)}, u32[]{:S(2)}) collective-permute-start(bf16[64,3072]{1,0:T(8,128)(2,1)S(1)} %get-tuple-element.29), channel_id=1, source_target_pairs={{2,0},{4,2},{6,4},{8,6},{10,8},{12,10},{14,12},{16,14},{18,16},{20... | collective-permute-start | bytes 1179656 | tf_op jit(solution)/shard_map/ppermute | solution.py:149
  187.9 101.4 %collective-permute-start.2 = (bf16[64,3072]{1,0:T(8,128)(2,1)S(1)}, bf16[64,3072]{1,0:T(8,128)(2,1)S(1)}, u32[]{:S(2)}, u32[]{:S(2)}) collective-permute-start(bf16[64,3072]{1,0:T(8,128)(2,1)S(1)} %get-tuple-element.37), channel_id=1, source_target_pairs={{0,1},{1,0},{2,3},{3,2},{4,5},{5,4},{6,7},{7,6},{8,9},{9,8},{10,11... | collective-permute-start | bytes 1179656 | tf_op jit(solution)/shard_map/ppermute | solution.py:160
  278.0 1.4 copy-start.9
  287.1 7.8 %collective-permute-start.8 = (bf16[64,3072]{1,0:T(8,128)(2,1)S(1)}, bf16[64,3072]{1,0:T(8,128)(2,1)S(1)}, u32[]{:S(2)}, u32[]{:S(2)}) collective-permute-start(bf16[64,3072]{1,0:T(8,128)(2,1)S(1)} %get-tuple-element.33), channel_id=1, source_target_pairs={{0,1},{1,0},{2,3},{3,2},{4,5},{5,4},{6,7},{7,6},{8,9},{9,8},{10,11... | collective-permute-start | bytes 1179656 | tf_op jit(solution)/shard_map/ppermute | solution.py:160
  288.5 10.7 %collective-permute-start.7 = (bf16[64,3072]{1,0:T(8,128)(2,1)S(1)}, bf16[64,3072]{1,0:T(8,128)(2,1)S(1)}, u32[]{:S(2)}, u32[]{:S(2)}) collective-permute-start(bf16[64,3072]{1,0:T(8,128)(2,1)S(1)} %get-tuple-element.35), channel_id=1, source_target_pairs={{0,1},{1,0},{2,3},{3,2},{4,5},{5,4},{6,7},{7,6},{8,9},{9,8},{10,11... | collective-permute-start | bytes 1179656 | tf_op jit(solution)/shard_map/ppermute | solution.py:160
  289.4 9.8 %copy-start.12 = (bf16[64,6144]{1,0:T(8,128)(2,1)}, bf16[64,6144]{1,0:T(8,128)(2,1)S(1)}, u32[]{:S(2)}) copy-start(bf16[64,6144]{1,0:T(8,128)(2,1)S(1)} %constant_dynamic-update-slice_fusion.2) | copy-start | bytes 2359300
  295.0 4.2 %copy-start.13 = (bf16[64,6144]{1,0:T(8,128)(2,1)}, bf16[64,6144]{1,0:T(8,128)(2,1)S(1)}, u32[]{:S(2)}) copy-start(bf16[64,6144]{1,0:T(8,128)(2,1)S(1)} %constant_dynamic-update-slice_fusion.1) | copy-start | bytes 2359300
  299.2 0.9 copy-start.11

commit v3 on v2

--- a/solution.py
+++ b/solution.py
@@ -36,7 +36,7 @@
 def attend_kernel(
     blocks, block, dim, heads, rand, step, scale,
     slots, edge, q_ref, k_ref, v_ref, g_ref, up_ref, down_ref, far_ref,
-    p_ref, ds_ref, out_ref,
+    p_ref, ds_ref, outk_ref, outv_ref,
 ):
     group = pl.program_id(0)
     units = [(j, b) for j in range(step) for b in range(blocks)]
@@ -76,8 +76,8 @@
         ds_ref[j, rows] = dss[n]
         for r in range(rand):
             part = slice(r * block, (r + 1) * block)
-            out_ref[at[n][r], :, :dim] = dks[n][part]
-            out_ref[at[n][r], :, dim:] = dvs[n][part]
+            outk_ref[at[n][r]] = dks[n][part]
+            outv_ref[at[n][r]] = dvs[n][part]
 
 
 def window_kernel(
@@ -117,16 +117,12 @@
 
 
 def collect_kernel(
-    blocks, block, dim, heads, count, codes, dk_ref, dv_ref, ak_ref, av_ref, bk_ref, bv_ref,
-    in_ref, ok_ref, ov_ref, k_acc, v_acc,
+    blocks, block, dim, heads, count, codes, own_ref, above_ref, below_ref, in_ref, out_ref, acc,
 ):
     last = slice((blocks - 1) * block, blocks * block)
-    k_acc[...] = dk_ref[...]
-    v_acc[...] = dv_ref[...]
-    k_acc[:block] += ak_ref[...].astype(F32)
-    v_acc[:block] += av_ref[...].astype(F32)
-    k_acc[last] += bk_ref[...].astype(F32)
-    v_acc[last] += bv_ref[...].astype(F32)
+    acc[...] = own_ref[...]
+    acc[:block] += above_ref[...].astype(F32)
+    acc[last] += below_ref[...].astype(F32)
 
     @pl.loop(0, count)
     def _(s):
@@ -136,11 +132,9 @@
         def _():
             rows = pl.ds(pl.multiple_of(code // heads * block, block), block)
             cols = pl.ds(pl.multiple_of(code % heads * dim, dim), dim)
-            k_acc[rows, cols] += in_ref[s, :, :dim].astype(F32)
-            v_acc[rows, cols] += in_ref[s, :, dim:].astype(F32)
-
-    ok_ref[...] = k_acc[...].astype(BF16)
-    ov_ref[...] = v_acc[...].astype(BF16)
+            acc[rows, cols] += in_ref[s].astype(F32)
+
+    out_ref[...] = acc[...].astype(BF16)
 
 
 def shifted(value, axis, steps):
@@ -211,22 +205,24 @@
     half = jax.ShapeDtypeStruct((block, width), BF16)
     whole = jax.ShapeDtypeStruct((tokens, width), F32)
     span = 3 * block
+    back = pl.BlockSpec((count, block, dim), lambda i, *_: (0, 0, 0))
     probs = pl.BlockSpec((step, tokens, span), lambda i, *_: (i, 0, 0))
     grads = pl.BlockSpec((step, tokens, span + rand * block), lambda i, *_: (i, 0, 0))
     work = heads * tokens * (span + rand * block) * dim
     cost = pl.CostEstimate(flops=8 * work, bytes_accessed=16 * 2**20, transcendentals=0)
-    p, ds, outbound = pl.pallas_call(
+    p, ds, outk, outv = pl.pallas_call(
         functools.partial(attend_kernel, blocks, block, dim, heads, rand, step, scale),
         out_shape=[
             jax.ShapeDtypeStruct((heads, tokens, span), BF16),
             jax.ShapeDtypeStruct((heads, tokens, span + rand * block), BF16),
-            jax.ShapeDtypeStruct((count, block, 2 * dim), BF16),
+            jax.ShapeDtypeStruct((count, block, dim), BF16),
+            jax.ShapeDtypeStruct((count, block, dim), BF16),
         ],
         grid_spec=pltpu.PrefetchScalarGridSpec(
             num_scalar_prefetch=2,
             grid=(heads // step,),
             in_specs=[wide, wide, wide, wide, side, side, far],
-            out_specs=[probs, grads, far],
+            out_specs=[probs, grads, back, back],
         ),
         compiler_params=pltpu.CompilerParams(vmem_limit_bytes=LIMIT),
         cost_estimate=cost,
@@ -245,21 +241,33 @@
         compiler_params=pltpu.CompilerParams(vmem_limit_bytes=LIMIT),
         cost_estimate=cost,
     )(slot, queries, key_rows, out_grad, up, down, fetched, p, ds)
-    inbound = lax.all_to_all(
-        outbound.reshape(peers, cap, block, 2 * dim), "seq", split_axis=0, concat_axis=0, tiled=True
-    ).reshape(count, block, 2 * dim)
-    below_k, below_v = shifted(tok, "seq", -1), shifted(tov, "seq", -1)
-    above_k, above_v = shifted(tnk, "seq", 1), shifted(tnv, "seq", 1)
-    rows = jax.ShapeDtypeStruct((tokens, width), BF16)
     smem = pl.BlockSpec(memory_space=pltpu.SMEM)
-    k_rows, v_rows = pl.pallas_call(
-        functools.partial(collect_kernel, blocks, block, dim, heads, count),
-        out_shape=[rows, rows],
-        in_specs=[smem] + [full] * 7,
-        out_specs=[full, full],
-        scratch_shapes=[VMEM((tokens, width), F32), VMEM((tokens, width), F32)],
-        compiler_params=pltpu.CompilerParams(vmem_limit_bytes=LIMIT),
-    )(asked, dk, dv, above_k, above_v, below_k, below_v, inbound)
+
+    def returned(terms):
+        return lax.all_to_all(
+            terms.reshape(peers, cap, block, dim), "seq", split_axis=0, concat_axis=0, tiled=True
+        ).reshape(count, block, dim)
+
+    def collected(own, above, below, terms):
+        return pl.pallas_call(
+            functools.partial(collect_kernel, blocks, block, dim, heads, count),
+            out_shape=jax.ShapeDtypeStruct((tokens, width), BF16),
+            in_specs=[smem] + [full] * 4,
+            out_specs=full,
+            scratch_shapes=[VMEM((tokens, width), F32)],
+            compiler_params=pltpu.CompilerParams(vmem_limit_bytes=LIMIT),
+            cost_estimate=pl.CostEstimate(
+                flops=0, bytes_accessed=8 * 2**20, transcendentals=0
+            ),
+        )(asked, own, above, below, terms)
+
+    back_v = returned(outv)
+    above_v, below_v = shifted(tnv, "seq", 1), shifted(tov, "seq", -1)
+    above_k, below_k = shifted(tnk, "seq", 1), shifted(tok, "seq", -1)
+    (outk, back_v) = lax.optimization_barrier((outk, back_v))
+    back_k = returned(outk)
+    v_rows = collected(dv, above_v, below_v, back_v)
+    k_rows = collected(dk, above_k, below_k, back_k)
     return exchanged(dq, "head"), exchanged(k_rows, "head"), exchanged(v_rows, "head")
 
 

time: 302 us -> 307 us (1.017)
  waiting for transfers between devices: 202 us -> 134 us
  blocking collectives: 15.8 us -> 73.8 us
  local copies, waits for them, and re-layouts: 9.51 us -> 21.6 us
    ppermute x6, waiting for transfers between devices: 88.5 us -> 26 us  [shifted(): lax.ppermute(value, axis, [(source, source + steps) for source in range(f...]
    all_to_all x0 -> x1, blocking collectives: none -> 58 us  [returned(): lax.all_to_all(terms.reshape(peers, cap, block, dim), 'seq', split_axis=0...]
    unnamed x31 -> x51, local copies, waits for them, and re-layouts: 5.56 us -> 14 us
    ppermute x3, waiting for transfers between devices: 9.68 us -> 4.5 us  [exchanged(): lax.ppermute(piece, axis, [(i, (i + r) % count) for i in range(count)])]
    pallas_call x1 -> x2, Pallas kernels: 7.53 us -> 8.46 us  [collected(): pl.pallas_call(functools.partial(collect_kernel, blocks, block, dim, head...]
  transfers between devices with their start and end apart: 11 -> 11, of which waited for: 5 -> 3; matrix products, arithmetic and copies ran while one was open for 1% -> 3% of each run, Pallas kernels for 6% -> 6%
where the time goes in v3:
time: 307 us; the launch traced here: 306 us
  waiting for transfers between devices  134 us (44%)
  blocking collectives  73.8 us (24%)
  Pallas kernels  39.6 us (13%)
  starting transfers between devices  32.4 us (11%)
  local copies, waits for them, and re-layouts  21.6 us (7%)
    all_to_all x1, waiting for transfers between devices, local(): lax.all_to_all(outgoing.reshape(peers, cap, block, 2 * dim), 'seq', split...  104 us
    all_to_all x1, blocking collectives, returned(): lax.all_to_all(terms.reshape(peers, cap, block, dim), 'seq', split_axis=0...  58 us
    ppermute x6, waiting for transfers between devices, shifted(): lax.ppermute(value, axis, [(source, source + steps) for source in range(f...  26 us
    ppermute x6, starting transfers between devices, shifted(): lax.ppermute(value, axis, [(source, source + steps) for source in range(f...  17.7 us
    all_to_all x1, blocking collectives, local(): lax.all_to_all(asked.reshape(peers, cap), 'seq', split_axis=0, concat_axi...  15.8 us
    pallas_call x1, Pallas kernels, local(): pl.pallas_call(functools.partial(attend_kernel, blocks, block, dim, heads...  14.9 us
    unnamed x51, local copies, waits for them, and re-layouts  14 us
    pallas_call x1, Pallas kernels, local(): pl.pallas_call(functools.partial(window_kernel, blocks, block, dim, heads...  9.11 us
  transfers between devices with their start and end apart: 11, of which 3 were waited for; matrix products, arithmetic and copies ran while one was open for 3% of the time, Pallas kernels for 6%

profile of v3, /device:TPU:16, one launch (start us, length us, event | category | flops | bytes accessed | tf_op | source)
XLA Modules:
  0.0 305.8 jit_solution(10625938850771973058)
XLA Ops:
  0.6 1.5 slice_bitcast_fusion
  2.1 0.0 copy-start.24
  2.1 0.0 copy-start
  2.1 0.0 copy-start.2
  2.1 0.9 pad_maximum_fusion.1
  3.1 2.7 collective-permute-start.1
  5.8 0.9 pad_maximum_fusion
  6.8 1.9 collective-permute-start
  8.7 0.1 copy.12
  8.8 0.1 reshape.160
  8.9 0.2 convert_reduce_fusion
  9.1 0.1 select_reduce_fusion
  9.3 0.1 sub.24
  9.3 15.8 %all_to_all.21 = s32[16,1,9]{2,1,0:T(1,128)S(1)} all-to-all(s32[16,1,9]{2,1,0:T(1,128)S(1)} %bitcast.22), channel_id=1, replica_groups=mesh['seq'=16,'head'=2] {'seq'}, dimensions={0} | all-to-all | bytes 1152 | tf_op jit(solution)/shard_map/all_to_all | solution.py:178
  25.1 0.5 broadcast.201
  25.7 0.7 reduce.3
  26.3 0.1 reshape.161.codes
  26.4 0.0 copy-start.7
  26.5 0.0 copy-start.9
  26.5 7.2 %shard_map.76 = bf16[144,64,256]{2,1,0:T(8,128)(2,1)} custom-call(s32[144]{0:T(256)S(1)} %reshape.161.codes, bf16[128,3072]{1,0:T(8,128)(2,1)S(1)} %copy-done, bf16[128,3072]{1,0:T(8,128)(2,1)S(1)} %copy-done.2), custom_call_target="tpu_custom_call" | custom-call | tf_op jit(solution)/shard_map/pallas_call | solution.py:185
  33.7 6.2 %all-to-all-start.1 = ((bf16[16,9,64,256]{3,2,1,0:T(8,128)(2,1)}), bf16[16,9,64,256]{3,2,1,0:T(8,128)(2,1)}, u32[]{:S(2)}, u32[]{:S(2)}) async-start(bf16[16,9,64,256]{3,2,1,0:T(8,128)(2,1)} %bitcast.19), calls=%async_computation.1 | async-start | bytes 9437184 | tf_op jit(solution)/shard_map/all_to_all | solution.py:196
  39.9 0.1 add_convert_fusion.edge
  40.0 103.9 %all-to-all-done.1 = bf16[16,9,64,256]{3,2,1,0:T(8,128)(2,1)} async-done(((bf16[16,9,64,256]{3,2,1,0:T(8,128)(2,1)}), bf16[16,9,64,256]{3,2,1,0:T(8,128)(2,1)}, u32[]{:S(2)}, u32[]{:S(2)}) %all-to-all-start.1) | async-done | bytes 4718624 | tf_op jit(solution)/shard_map/all_to_all | solution.py:196
  143.8 1.1 copy-done.8
  145.0 1.1 copy-done.10
  146.1 14.9 %shard_map.77 = (bf16[24,128,192]{2,1,0:T(8,128)(2,1)}, bf16[24,128,320]{2,1,0:T(8,128)(2,1)}, bf16[144,64,128]{2,1,0:T(8,128)(2,1)}, bf16[144,64,128]{2,1,0:T(8,128)(2,1)}) custom-call(s32[96]{0:T(128)S(1)} %multiply_add_fusion.slots, s32[2]{0:T(128)S(1)} %add_convert_fusion.edge, bf16[128,3072]{1,0:T(8,128)(2,1)S(1)} %copy-done.3, ...), custom_call_target="tpu_custom_call" | custom-call | flops 1006632960 | bytes 16777216 | tf_op jit(solution)/shard_map/pallas_call | solution.py:213
  161.0 58.0 %all_to_all.22 = bf16[16,9,64,128]{3,2,1,0:T(8,128)(2,1)} all-to-all(bf16[16,9,64,128]{3,2,1,0:T(8,128)(2,1)} %bitcast.21), channel_id=1, replica_groups=mesh['seq'=16,'head'=2] {'seq'}, dimensions={0} | all-to-all | bytes 4718592 | tf_op jit(solution)/shard_map/all_to_all | solution.py:247
  219.0 4.8 %all-to-all-start.3 = ((bf16[16,9,64,128]{3,2,1,0:T(8,128)(2,1)}), bf16[16,9,64,128]{3,2,1,0:T(8,128)(2,1)S(1)}, u32[]{:S(2)}, u32[]{:S(2)}) async-start(bf16[16,9,64,128]{3,2,1,0:T(8,128)(2,1)} %bitcast.20), calls=%async_computation.3 | async-start | bytes 4718592 | tf_op jit(solution)/shard_map/all_to_all | solution.py:247
  223.8 1.1 copy-done.4
  225.0 1.1 copy-done.6
  226.1 1.1 copy-done.11
  227.2 9.1 %shard_map.78 = (bf16[128,3072]{1,0:T(8,128)(2,1)S(1)}, f32[128,3072]{1,0:T(8,128)}, f32[128,3072]{1,0:T(8,128)}, bf16[64,3072]{1,0:T(8,128)(2,1)S(1)}, bf16[64,...) custom-call(s32[96]{0:T(128)S(1)} %multiply_add_fusion.slots, ...), custom_call_target="tpu_custom_call" | custom-call | flops 1006632960 | bytes 16777216 | tf_op jit(solution)/shard_map/pallas_call | solution.py:230
  236.3 0.9 copy-done.14
  237.2 0.8 copy-done.17
  238.0 0.7 copy-done.18
  238.7 2.0 collective-permute-start.6
  240.8 4.4 %collective-permute-start.7 = (bf16[64,3072]{1,0:T(8,128)(2,1)}, bf16[64,3072]{1,0:T(8,128)(2,1)S(1)}, u32[]{:S(2)}, u32[]{:S(2)}) collective-permute-start(bf16[64,3072]{1,0:T(8,128)(2,1)} %get-tuple-element.33), channel_id=1, source_target_pairs={{2,0},{4,2},{6,4},{8,6},{10,8},{12,10},{14,12},{16,14},{18,16},{20... | collective-permute-start | bytes 1179656 | tf_op jit(solution)/shard_map/ppermute | solution.py:143
  245.3 2.1 collective-permute-start.3
  247.3 4.5 %collective-permute-start.4 = (bf16[64,3072]{1,0:T(8,128)(2,1)}, bf16[64,3072]{1,0:T(8,128)(2,1)S(1)}, u32[]{:S(2)}, u32[]{:S(2)}) collective-permute-start(bf16[64,3072]{1,0:T(8,128)(2,1)} %copy-done.17), channel_id=1, source_target_pairs={{2,0},{4,2},{6,4},{8,6},{10,8},{12,10},{14,12},{16,14},{18,16},{20... | collective-permute-start | bytes 1179656 | tf_op jit(solution)/shard_map/ppermute | solution.py:143
  251.9 0.1 broadcast.179.clone
  251.9 1.9 constant_dynamic-slice_fusion.1
  253.9 1.5 collective-permute-start.2
  255.4 26.0 %collective-permute-done.6.above_ref = bf16[64,3072]{1,0:T(8,128)(2,1)S(1)} collective-permute-done((bf16[64,3072]{1,0:T(8,128)(2,1)}, bf16[64,3072]{1,0:T(8,128)(2,1)S(1)}, u32[]{:S(2)}, u32[]{:S(2)}) %collective-permute-start.6) | collective-permute-done | bytes 393248 | tf_op jit(solution)/shard_map/ppermute | solution.py:143
  281.4 1.4 copy-done.13
  282.8 4.2 %shard_map.80 = bf16[128,3072]{1,0:T(8,128)(2,1)S(1)} custom-call(s32[144]{0:T(256)S(1)} %reshape.161.codes, f32[128,3072]{1,0:T(8,128)S(1)} %copy-done.13, bf16[64,3072]{1,0:T(8,128)(2,1)S(1)} %collective-permute-done.6.above_ref, bf16[64,3072]{1,0:T(8,128)(2,1)S(1)} %collective-permute-done.7.below_ref, bf16[144,64,128]{2,1,0:T(8,128)(2,1)S(1)} %bitcast.18), custom_call_target="tpu_custom_call" | custom-call | bytes 8388608 | tf_op jit(solution)/shard_map/pallas_call | solution.py:252
  287.0 0.1 broadcast.179.clone.2
  287.1 0.8 constant_dynamic-slice_fusion.2
  287.9 1.6 collective-permute-start.8
  289.5 0.7 copy-done.15
  290.2 1.4 copy-done.12
  291.6 1.0 copy-done.16
  292.6 4.2 %shard_map.79 = bf16[128,3072]{1,0:T(8,128)(2,1)S(1)} custom-call(s32[144]{0:T(256)S(1)} %reshape.161.codes, f32[128,3072]{1,0:T(8,128)S(1)} %copy-done.12, bf16[64,3072]{1,0:T(8,128)(2,1)S(1)} %collective-permute-done.3.above_ref, bf16[64,3072]{1,0:T(8,128)(2,1)S(1)} %copy-done.16, bf16[144,64,128]{2,1,0:T(8,128)(2,1)S(1)} %bitcast.17), custom_call_target="tpu_custom_call" | custom-call | bytes 8388608 | tf_op jit(solution)/shard_map/pallas_call | solution.py:252
  296.9 0.0 copy-start.21
  296.9 0.1 broadcast.179.clone.1
  296.9 0.1 constant_dynamic-slice_fusion
  297.0 0.6 collective-permute-start.5
  297.6 0.4 copy-done.21
  298.0 1.0 constant_dynamic-update-slice_fusion.2
  299.0 0.0 copy-start.22
  299.1 1.3 constant_dynamic-update-slice_fusion.1
  300.4 0.0 copy-start.23
  300.4 4.5 %collective-permute-done.5 = bf16[64,3072]{1,0:T(8,128)(2,1)S(1)} collective-permute-done((bf16[64,3072]{1,0:T(8,128)(2,1)S(1)}, bf16[64,3072]{1,0:T(8,128)(2,1)S(1)}, u32[]{:S(2)}, u32[]{:S(2)}) %collective-permute-start.5) | collective-permute-done | bytes 393248 | tf_op jit(solution)/shard_map/ppermute | solution.py:154
  304.9 0.0 copy-start.19
  304.9 0.9 copy-done.19
  (39 shorter events, 0.1 us)
Async XLA Ops:
  2.1 6.6 %copy-start.24 = (s32[2,24,2]{1,2,0:T(2,128)S(1)}, s32[2,24,2]{1,2,0:T(2,128)}, u32[]{:S(2)}) copy-start(s32[2,24,2]{1,2,0:T(2,128)} %param.9) | copy-start | bytes 1156
  2.1 24.4 %copy-start = (bf16[128,3072]{1,0:T(8,128)(2,1)S(1)}, bf16[128,3072]{1,0:T(8,128)(2,1)}, u32[]{:S(2)}) copy-start(bf16[128,3072]{1,0:T(8,128)(2,1)} %k_ref.5) | copy-start | bytes 2359300
  2.1 24.4 %copy-start.2 = (bf16[128,3072]{1,0:T(8,128)(2,1)S(1)}, bf16[128,3072]{1,0:T(8,128)(2,1)}, u32[]{:S(2)}) copy-start(bf16[128,3072]{1,0:T(8,128)(2,1)} %v_ref.3) | copy-start | bytes 2359300
  3.1 23.3 %collective-permute-start.1 = (bf16[2,64,3072]{2,1,0:T(8,128)(2,1)}, bf16[2,64,3072]{2,1,0:T(8,128)(2,1)S(1)}, u32[]{:S(2)}, u32[]{:S(2)}) collective-permute-start(bf16[2,64,3072]{2,1,0:T(8,128)(2,1)} %pad_maximum_fusion.1), channel_id=1, source_target_pairs={{2,0},{4,2},{6,4},{8,6},{10,8},{12,10},{14,12},{16,14},{18,16},{20... | collective-permute-start | bytes 2359304 | tf_op jit(solution)/shard_map/ppermute | solution.py:143
  6.8 19.7 %collective-permute-start = (bf16[2,64,3072]{2,1,0:T(8,128)(2,1)}, bf16[2,64,3072]{2,1,0:T(8,128)(2,1)S(1)}, u32[]{:S(2)}, u32[]{:S(2)}) collective-permute-start(bf16[2,64,3072]{2,1,0:T(8,128)(2,1)} %pad_maximum_fusion), channel_id=1, source_target_pairs={{0,2},{2,4},{4,6},{6,8},{8,10},{10,12},{12,14},{14,16},{16,18},{18... | collective-permute-start | bytes 2359304 | tf_op jit(solution)/shard_map/ppermute | solution.py:143
  26.4 7.2 %copy-start.7 = (bf16[2,64,3072]{2,1,0:T(8,128)(2,1)}, bf16[2,64,3072]{2,1,0:T(8,128)(2,1)S(1)}, u32[]{:S(2)}) copy-start(bf16[2,64,3072]{2,1,0:T(8,128)(2,1)S(1)} %collective-permute-done.1.down_ref) | copy-start | bytes 2359300
  26.5 7.2 %copy-start.9 = (bf16[2,64,3072]{2,1,0:T(8,128)(2,1)}, bf16[2,64,3072]{2,1,0:T(8,128)(2,1)S(1)}, u32[]{:S(2)}) copy-start(bf16[2,64,3072]{2,1,0:T(8,128)(2,1)S(1)} %collective-permute-done.up_ref) | copy-start | bytes 2359300
  33.6 110.2 %copy-start.3 = (bf16[128,3072]{1,0:T(8,128)(2,1)S(1)}, bf16[128,3072]{1,0:T(8,128)(2,1)}, u32[]{:S(2)}) copy-start(bf16[128,3072]{1,0:T(8,128)(2,1)} %q_ref.3) | copy-start | bytes 2359300
  33.7 110.2 %copy-start.5 = (bf16[128,3072]{1,0:T(8,128)(2,1)S(1)}, bf16[128,3072]{1,0:T(8,128)(2,1)}, u32[]{:S(2)}) copy-start(bf16[128,3072]{1,0:T(8,128)(2,1)} %g_ref.3) | copy-start | bytes 2359300
  33.7 110.2 %all-to-all-start.1 = ((bf16[16,9,64,256]{3,2,1,0:T(8,128)(2,1)}), bf16[16,9,64,256]{3,2,1,0:T(8,128)(2,1)}, u32[]{:S(2)}, u32[]{:S(2)}) async-start(bf16[16,9,64,256]{3,2,1,0:T(8,128)(2,1)} %bitcast.19), calls=%async_computation.1 | async-start | bytes 9437184 | tf_op jit(solution)/shard_map/all_to_all | solution.py:196
  143.8 1.1 copy-start.8
  145.0 1.1 copy-start.10
  219.0 71.2 %all-to-all-start.3 = ((bf16[16,9,64,128]{3,2,1,0:T(8,128)(2,1)}), bf16[16,9,64,128]{3,2,1,0:T(8,128)(2,1)S(1)}, u32[]{:S(2)}, u32[]{:S(2)}) async-start(bf16[16,9,64,128]{3,2,1,0:T(8,128)(2,1)} %bitcast.20), calls=%async_computation.3 | async-start | bytes 4718592 | tf_op jit(solution)/shard_map/all_to_all | solution.py:247
  223.8 1.1 copy-start.4
  224.9 1.1 copy-start.6
  226.1 1.1 copy-start.11
  236.3 0.9 copy-start.14
  237.2 0.8 copy-start.17
  238.0 0.7 copy-start.18
  238.7 42.6 %collective-permute-start.6 = (bf16[64,3072]{1,0:T(8,128)(2,1)}, bf16[64,3072]{1,0:T(8,128)(2,1)S(1)}, u32[]{:S(2)}, u32[]{:S(2)}) collective-permute-start(bf16[64,3072]{1,0:T(8,128)(2,1)} %get-tuple-element.32), channel_id=1, source_target_pairs={{0,2},{2,4},{4,6},{6,8},{8,10},{10,12},{12,14},{14,16},{16,18},{18... | collective-permute-start | bytes 1179656 | tf_op jit(solution)/shard_map/ppermute | solution.py:143
  240.8 40.6 %collective-permute-start.7 = (bf16[64,3072]{1,0:T(8,128)(2,1)}, bf16[64,3072]{1,0:T(8,128)(2,1)S(1)}, u32[]{:S(2)}, u32[]{:S(2)}) collective-permute-start(bf16[64,3072]{1,0:T(8,128)(2,1)} %get-tuple-element.33), channel_id=1, source_target_pairs={{2,0},{4,2},{6,4},{8,6},{10,8},{12,10},{14,12},{16,14},{18,16},{20... | collective-permute-start | bytes 1179656 | tf_op jit(solution)/shard_map/ppermute | solution.py:143
  245.2 36.1 %copy-start.1 = (bf16[16,9,64,128]{3,2,1,0:T(8,128)(2,1)S(1)}, bf16[16,9,64,128]{3,2,1,0:T(8,128)(2,1)}, u32[]{:S(2)}) copy-start(bf16[16,9,64,128]{3,2,1,0:T(8,128)(2,1)} %all_to_all.22) | copy-start | bytes 7077892
  245.3 44.2 %collective-permute-start.3 = (bf16[64,3072]{1,0:T(8,128)(2,1)}, bf16[64,3072]{1,0:T(8,128)(2,1)S(1)}, u32[]{:S(2)}, u32[]{:S(2)}) collective-permute-start(bf16[64,3072]{1,0:T(8,128)(2,1)} %copy-done.18), channel_id=1, source_target_pairs={{0,2},{2,4},{4,6},{6,8},{8,10},{10,12},{12,14},{14,16},{16,18},{18... | collective-permute-start | bytes 1179656 | tf_op jit(solution)/shard_map/ppermute | solution.py:143
  247.3 42.2 %collective-permute-start.4 = (bf16[64,3072]{1,0:T(8,128)(2,1)}, bf16[64,3072]{1,0:T(8,128)(2,1)S(1)}, u32[]{:S(2)}, u32[]{:S(2)}) collective-permute-start(bf16[64,3072]{1,0:T(8,128)(2,1)} %copy-done.17), channel_id=1, source_target_pairs={{2,0},{4,2},{6,4},{8,6},{10,8},{12,10},{14,12},{16,14},{18,16},{20... | collective-permute-start | bytes 1179656 | tf_op jit(solution)/shard_map/ppermute | solution.py:143
  253.9 27.5 %copy-start.20 = (bf16[64,6144]{1,0:T(8,128)(2,1)}, bf16[64,6144]{1,0:T(8,128)(2,1)S(1)}, u32[]{:S(2)}) copy-start(bf16[64,6144]{1,0:T(8,128)(2,1)S(1)} %get-tuple-element.40) | copy-start | bytes 2359300
  253.9 43.8 %collective-permute-start.2 = (bf16[64,3072]{1,0:T(8,128)(2,1)}, bf16[64,3072]{1,0:T(8,128)(2,1)}, u32[]{:S(2)}, u32[]{:S(2)}) collective-permute-start(bf16[64,3072]{1,0:T(8,128)(2,1)} %get-tuple-element.39), channel_id=1, source_target_pairs={{0,1},{1,0},{2,3},{3,2},{4,5},{5,4},{6,7},{7,6},{8,9},{9,8},{10,11... | collective-permute-start | bytes 1179656 | tf_op jit(solution)/shard_map/ppermute | solution.py:154
  281.4 1.4 copy-start.13
  287.9 11.2 %collective-permute-start.8 = (bf16[64,3072]{1,0:T(8,128)(2,1)}, bf16[64,3072]{1,0:T(8,128)(2,1)}, u32[]{:S(2)}, u32[]{:S(2)}) collective-permute-start(bf16[64,3072]{1,0:T(8,128)(2,1)} %get-tuple-element.35), channel_id=1, source_target_pairs={{0,1},{1,0},{2,3},{3,2},{4,5},{5,4},{6,7},{7,6},{8,9},{9,8},{10,11... | collective-permute-start | bytes 1179656 | tf_op jit(solution)/shard_map/ppermute | solution.py:154
  289.5 0.7 copy-start.15
  290.2 1.4 copy-start.12
  291.6 1.0 copy-start.16
  296.9 1.1 copy-start.21
  297.0 7.8 %collective-permute-start.5 = (bf16[64,3072]{1,0:T(8,128)(2,1)S(1)}, bf16[64,3072]{1,0:T(8,128)(2,1)S(1)}, u32[]{:S(2)}, u32[]{:S(2)}) collective-permute-start(bf16[64,3072]{1,0:T(8,128)(2,1)S(1)} %get-tuple-element.37), channel_id=1, source_target_pairs={{0,1},{1,0},{2,3},{3,2},{4,5},{5,4},{6,7},{7,6},{8,9},{9,8},{10,11... | collective-permute-start | bytes 1179656 | tf_op jit(solution)/shard_map/ppermute | solution.py:154
  299.0 5.9 %copy-start.22 = (bf16[64,6144]{1,0:T(8,128)(2,1)}, bf16[64,6144]{1,0:T(8,128)(2,1)S(1)}, u32[]{:S(2)}) copy-start(bf16[64,6144]{1,0:T(8,128)(2,1)S(1)} %constant_dynamic-update-slice_fusion.2) | copy-start | bytes 2359300
  300.4 4.5 %copy-start.23 = (bf16[64,6144]{1,0:T(8,128)(2,1)}, bf16[64,6144]{1,0:T(8,128)(2,1)S(1)}, u32[]{:S(2)}) copy-start(bf16[64,6144]{1,0:T(8,128)(2,1)S(1)} %constant_dynamic-update-slice_fusion.1) | copy-start | bytes 2359300
  304.9 0.9 copy-start.19

commit v4 on v3

--- a/solution.py
+++ b/solution.py
@@ -36,7 +36,7 @@
 def attend_kernel(
     blocks, block, dim, heads, rand, step, scale,
     slots, edge, q_ref, k_ref, v_ref, g_ref, up_ref, down_ref, far_ref,
-    p_ref, ds_ref, outk_ref, outv_ref,
+    p_ref, ds_ref, out_ref,
 ):
     group = pl.program_id(0)
     units = [(j, b) for j in range(step) for b in range(blocks)]
@@ -76,8 +76,8 @@
         ds_ref[j, rows] = dss[n]
         for r in range(rand):
             part = slice(r * block, (r + 1) * block)
-            outk_ref[at[n][r]] = dks[n][part]
-            outv_ref[at[n][r]] = dvs[n][part]
+            out_ref[at[n][r], :, :dim] = dks[n][part]
+            out_ref[at[n][r], :, dim:] = dvs[n][part]
 
 
 def window_kernel(
@@ -117,7 +117,7 @@
 
 
 def collect_kernel(
-    blocks, block, dim, heads, count, codes, own_ref, above_ref, below_ref, in_ref, out_ref, acc,
+    blocks, block, dim, heads, count, first, codes, own_ref, above_ref, below_ref, in_ref, out_ref, acc,
 ):
     last = slice((blocks - 1) * block, blocks * block)
     acc[...] = own_ref[...]
@@ -132,7 +132,7 @@
         def _():
             rows = pl.ds(pl.multiple_of(code // heads * block, block), block)
             cols = pl.ds(pl.multiple_of(code % heads * dim, dim), dim)
-            acc[rows, cols] += in_ref[s].astype(F32)
+            acc[rows, cols] += in_ref[s, :, first:first + dim].astype(F32)
 
     out_ref[...] = acc[...].astype(BF16)
 
@@ -178,10 +178,10 @@
     asked = lax.all_to_all(
         asked.reshape(peers, cap), "seq", split_axis=0, concat_axis=0, tiled=True
     ).reshape(count)
+    asked, own_k, own_v = lax.optimization_barrier((asked, key_rows, value_rows))
+    up = shifted(jnp.stack([own_k[tokens - block:], own_v[tokens - block:]]), "seq", 1)
+    down = shifted(jnp.stack([own_k[:block], own_v[:block]]), "seq", -1)
     full = pl.BlockSpec(memory_space=VMEM)
-    up = shifted(jnp.stack([key_rows[tokens - block:], value_rows[tokens - block:]]), "seq", 1)
-    down = shifted(jnp.stack([key_rows[:block], value_rows[:block]]), "seq", -1)
-    asked, up, down = lax.optimization_barrier((asked, up, down))
     outgoing = pl.pallas_call(
         functools.partial(gather_kernel, block, dim, heads, cap),
         out_shape=jax.ShapeDtypeStruct((count, block, 2 * dim), BF16),
@@ -192,7 +192,9 @@
             out_specs=pl.BlockSpec((cap, block, 2 * dim), lambda i, *_: (i, 0, 0)),
         ),
         compiler_params=pltpu.CompilerParams(vmem_limit_bytes=LIMIT),
-    )(asked, key_rows, value_rows)
+        cost_estimate=pl.CostEstimate(flops=0, bytes_accessed=16 * 2**20, transcendentals=0),
+    )(asked, own_k, own_v)
+    outgoing, up, down = lax.optimization_barrier((outgoing, up, down))
     fetched = lax.all_to_all(
         outgoing.reshape(peers, cap, block, 2 * dim), "seq", split_axis=0, concat_axis=0, tiled=True
     ).reshape(count, block, 2 * dim)
@@ -205,24 +207,22 @@
     half = jax.ShapeDtypeStruct((block, width), BF16)
     whole = jax.ShapeDtypeStruct((tokens, width), F32)
     span = 3 * block
-    back = pl.BlockSpec((count, block, dim), lambda i, *_: (0, 0, 0))
     probs = pl.BlockSpec((step, tokens, span), lambda i, *_: (i, 0, 0))
     grads = pl.BlockSpec((step, tokens, span + rand * block), lambda i, *_: (i, 0, 0))
     work = heads * tokens * (span + rand * block) * dim
     cost = pl.CostEstimate(flops=8 * work, bytes_accessed=16 * 2**20, transcendentals=0)
-    p, ds, outk, outv = pl.pallas_call(
+    p, ds, outbound = pl.pallas_call(
         functools.partial(attend_kernel, blocks, block, dim, heads, rand, step, scale),
         out_shape=[
             jax.ShapeDtypeStruct((heads, tokens, span), BF16),
             jax.ShapeDtypeStruct((heads, tokens, span + rand * block), BF16),
-            jax.ShapeDtypeStruct((count, block, dim), BF16),
-            jax.ShapeDtypeStruct((count, block, dim), BF16),
+            jax.ShapeDtypeStruct((count, block, 2 * dim), BF16),
         ],
         grid_spec=pltpu.PrefetchScalarGridSpec(
             num_scalar_prefetch=2,
             grid=(heads // step,),
             in_specs=[wide, wide, wide, wide, side, side, far],
-            out_specs=[probs, grads, back, back],
+            out_specs=[probs, grads, far],
         ),
         compiler_params=pltpu.CompilerParams(vmem_limit_bytes=LIMIT),
         cost_estimate=cost,
@@ -241,16 +241,14 @@
         compiler_params=pltpu.CompilerParams(vmem_limit_bytes=LIMIT),
         cost_estimate=cost,
     )(slot, queries, key_rows, out_grad, up, down, fetched, p, ds)
+    inbound = lax.all_to_all(
+        outbound.reshape(peers, cap, block, 2 * dim), "seq", split_axis=0, concat_axis=0, tiled=True
+    ).reshape(count, block, 2 * dim)
     smem = pl.BlockSpec(memory_space=pltpu.SMEM)
 
-    def returned(terms):
-        return lax.all_to_all(
-            terms.reshape(peers, cap, block, dim), "seq", split_axis=0, concat_axis=0, tiled=True
-        ).reshape(count, block, dim)
-
-    def collected(own, above, below, terms):
+    def collected(own, above, below, first):
         return pl.pallas_call(
-            functools.partial(collect_kernel, blocks, block, dim, heads, count),
+            functools.partial(collect_kernel, blocks, block, dim, heads, count, first),
             out_shape=jax.ShapeDtypeStruct((tokens, width), BF16),
             in_specs=[smem] + [full] * 4,
             out_specs=full,
@@ -259,15 +257,10 @@
             cost_estimate=pl.CostEstimate(
                 flops=0, bytes_accessed=8 * 2**20, transcendentals=0
             ),
-        )(asked, own, above, below, terms)
-
-    back_v = returned(outv)
-    above_v, below_v = shifted(tnv, "seq", 1), shifted(tov, "seq", -1)
-    above_k, below_k = shifted(tnk, "seq", 1), shifted(tok, "seq", -1)
-    (outk, back_v) = lax.optimization_barrier((outk, back_v))
-    back_k = returned(outk)
-    v_rows = collected(dv, above_v, below_v, back_v)
-    k_rows = collected(dk, above_k, below_k, back_k)
+        )(asked, own, shifted(above, "seq", 1), shifted(below, "seq", -1), inbound)
+
+    k_rows = collected(dk, tnk, tok, 0)
+    v_rows = collected(dv, tnv, tov, dim)
     return exchanged(dq, "head"), exchanged(k_rows, "head"), exchanged(v_rows, "head")
 
 

time: 307 us -> 305 us (level)
  blocking collectives: 73.8 us -> 10.1 us
  waiting for transfers between devices: 134 us -> 195 us
  local copies, waits for them, and re-layouts: 21.6 us -> 12.7 us
  starting transfers between devices: 32.4 us -> 39.6 us
  Pallas kernels: 39.6 us -> 43.5 us
    all_to_all x1 -> x0, blocking collectives: 58 us -> none  [returned(): lax.all_to_all(terms.reshape(peers, cap, block, dim), 'seq', split_axis=0...]
    ppermute x6, waiting for transfers between devices: 26 us -> 83 us  [shifted(): lax.ppermute(value, axis, [(source, source + steps) for source in range(f...]
    all_to_all x1, blocking collectives: 15.8 us -> 10.1 us  [local(): lax.all_to_all(asked.reshape(peers, cap), 'seq', split_axis=0, concat_axi...]
    unnamed x51 -> x33, local copies, waits for them, and re-layouts: 14 us -> 8.85 us
    all_to_all x1, starting transfers between devices: 6.23 us -> 10.9 us  [local(): lax.all_to_all(outgoing.reshape(peers, cap, block, 2 * dim), 'seq', split...]
    pallas_call x2, Pallas kernels: 8.46 us -> 12.5 us  [collected(): pl.pallas_call(functools.partial(collect_kernel, blocks, block, dim, head...]
    ppermute x3, waiting for transfers between devices: 4.5 us -> 7.84 us  [exchanged(): lax.ppermute(piece, axis, [(i, (i + r) % count) for i in range(count)])]
  transfers between devices with their start and end apart: 11 -> 11, of which waited for: 3 -> 6; matrix products, arithmetic and copies ran while one was open for 3% -> 1% of each run, Pallas kernels for 6% -> 9%
where the time goes in v4:
time: 305 us; the launch traced here: 303 us
  waiting for transfers between devices  195 us (64%)
  Pallas kernels  43.5 us (14%)
  starting transfers between devices  39.6 us (13%)
  local copies, waits for them, and re-layouts  12.7 us (4%)
  blocking collectives  10.1 us (3%)
    all_to_all x1, waiting for transfers between devices, local(): lax.all_to_all(outgoing.reshape(peers, cap, block, 2 * dim), 'seq', split...  104 us
    ppermute x6, waiting for transfers between devices, shifted(): lax.ppermute(value, axis, [(source, source + steps) for source in range(f...  83 us
    ppermute x6, starting transfers between devices, shifted(): lax.ppermute(value, axis, [(source, source + steps) for source in range(f...  19.4 us
    pallas_call x1, Pallas kernels, local(): pl.pallas_call(functools.partial(attend_kernel, blocks, block, dim, heads...  14.8 us
    pallas_call x2, Pallas kernels, collected(): pl.pallas_call(functools.partial(collect_kernel, blocks, block, dim, head...  12.5 us
    all_to_all x1, starting transfers between devices, local(): lax.all_to_all(outgoing.reshape(peers, cap, block, 2 * dim), 'seq', split...  10.9 us
    all_to_all x1, blocking collectives, local(): lax.all_to_all(asked.reshape(peers, cap), 'seq', split_axis=0, concat_axi...  10.1 us
    pallas_call x1, Pallas kernels, local(): pl.pallas_call(functools.partial(window_kernel, blocks, block, dim, heads...  9.12 us
  transfers between devices with their start and end apart: 11, of which 6 were waited for; matrix products, arithmetic and copies ran while one was open for 1% of the time, Pallas kernels for 9%

profile of v4, /device:TPU:16, one launch (start us, length us, event | category | flops | bytes accessed | tf_op | source)
XLA Modules:
  0.0 302.7 jit_solution(10427385049252561410)
XLA Ops:
  0.6 0.0 copy-start
  0.6 0.0 copy-start.1
  0.7 0.9 copy.12
  1.5 0.1 reshape.154
  1.7 0.2 convert_reduce_fusion
  1.9 0.1 select_reduce_fusion
  2.0 0.1 sub.24
  2.1 10.1 %all_to_all.16 = s32[16,1,9]{2,1,0:T(1,128)S(1)} all-to-all(s32[16,1,9]{2,1,0:T(1,128)S(1)} %bitcast.17), channel_id=1, replica_groups=mesh['seq'=16,'head'=2] {'seq'}, dimensions={0} | all-to-all | bytes 1152 | tf_op jit(solution)/shard_map/all_to_all | solution.py:178
  12.2 0.5 broadcast.201
  12.7 0.7 reduce.3
  13.3 0.1 reshape.155.codes
  13.4 1.5 slice_bitcast_fusion
  14.9 0.1 pad_maximum_fusion
  15.0 1.9 collective-permute-start
  16.9 0.1 pad_maximum_fusion.1
  17.0 4.5 %collective-permute-start.1 = (bf16[2,64,3072]{2,1,0:T(8,128)(2,1)S(1)}, bf16[2,64,3072]{2,1,0:T(8,128)(2,1)S(1)}, u32[]{:S(2)}, u32[]{:S(2)}) collective-permute-start(bf16[2,64,3072]{2,1,0:T(8,128)(2,1)S(1)} %pad_maximum_fusion.1), channel_id=1, source_target_pairs={{2,0},{4,2},{6,4},{8,6},{10,8},{12,10},{14,12},{16,14},{18,16},{20... | collective-permute-start | bytes 2359304 | tf_op jit(solution)/shard_map/ppermute | solution.py:143
  21.5 0.0 copy-done
  21.6 0.0 copy-done.1
  21.6 7.1 %shard_map.76 = bf16[144,64,256]{2,1,0:T(8,128)(2,1)} custom-call(s32[144]{0:T(256)S(1)} %reshape.155.codes, bf16[128,3072]{1,0:T(8,128)(2,1)S(1)} %copy-done, bf16[128,3072]{1,0:T(8,128)(2,1)S(1)} %copy-done.1), custom_call_target="tpu_custom_call" | custom-call | bytes 16777216 | tf_op jit(solution)/shard_map/pallas_call | solution.py:185
  28.7 0.6 collective-permute-done.up_ref
  29.3 0.9 copy-done.4
  30.2 0.9 collective-permute-done.1.down_ref
  31.1 0.9 copy-done.7
  32.0 10.9 %all-to-all-start.1 = ((bf16[16,9,64,256]{3,2,1,0:T(8,128)(2,1)}), bf16[16,9,64,256]{3,2,1,0:T(8,128)(2,1)}, u32[]{:S(2)}, u32[]{:S(2)}) async-start(bf16[16,9,64,256]{3,2,1,0:T(8,128)(2,1)} %bitcast.15), calls=%async_computation.1 | async-start | bytes 9437184 | tf_op jit(solution)/shard_map/all_to_all | solution.py:198
  42.8 0.1 add_convert_fusion.edge
  42.9 103.8 %all-to-all-done.1 = bf16[16,9,64,256]{3,2,1,0:T(8,128)(2,1)} async-done(((bf16[16,9,64,256]{3,2,1,0:T(8,128)(2,1)}), bf16[16,9,64,256]{3,2,1,0:T(8,128)(2,1)}, u32[]{:S(2)}, u32[]{:S(2)}) %all-to-all-start.1) | async-done | bytes 4718624 | tf_op jit(solution)/shard_map/all_to_all | solution.py:198
  146.8 0.0 copy-done.2
  146.8 0.0 copy-done.3
  146.8 1.1 copy-done.5
  147.9 1.1 copy-done.8
  149.0 14.8 %shard_map.77 = (bf16[24,128,192]{2,1,0:T(8,128)(2,1)}, bf16[24,128,320]{2,1,0:T(8,128)(2,1)}, bf16[144,64,256]{2,1,0:T(8,128)(2,1)}) custom-call(s32[96]{0:T(128)S(1)} %multiply_add_fusion.slots, s32[2]{0:T(128)S(1)} %add_convert_fusion.edge, bf16[128,3072]{1,0:T(8,128)(2,1)S(1)} %copy-done.2, bf16[128,3072]{1,0:T(8,128)(2,1)S(1)} %copy-done, ...), custom_call_target="tpu_custom_call" | custom-call | flops 1006632960 | bytes 16777216 | tf_op jit(solution)/shard_map/pallas_call | solution.py:214
  163.8 5.8 %all-to-all-start.2 = ((bf16[16,9,64,256]{3,2,1,0:T(8,128)(2,1)}), bf16[16,9,64,256]{3,2,1,0:T(8,128)(2,1)}, u32[]{:S(2)}, u32[]{:S(2)}) async-start(bf16[16,9,64,256]{3,2,1,0:T(8,128)(2,1)} %bitcast.16), calls=%async_computation.2 | async-start | bytes 9437184 | tf_op jit(solution)/shard_map/all_to_all | solution.py:244
  169.6 0.0 copy-done.6
  169.6 9.1 %shard_map.78 = (bf16[128,3072]{1,0:T(8,128)(2,1)S(1)}, f32[128,3072]{1,0:T(8,128)}, f32[128,3072]{1,0:T(8,128)}, bf16[64,3072]{1,0:T(8,128)(2,1)S(1)}, bf16[64,...) custom-call(s32[96]{0:T(128)S(1)} %multiply_add_fusion.slots, ...), custom_call_target="tpu_custom_call" | custom-call | flops 1006632960 | bytes 16777216 | tf_op jit(solution)/shard_map/pallas_call | solution.py:230
  178.8 0.9 copy-done.11
  179.6 0.7 copy-done.12
  180.4 2.0 collective-permute-start.6
  182.4 4.4 %collective-permute-start.7 = (bf16[64,3072]{1,0:T(8,128)(2,1)}, bf16[64,3072]{1,0:T(8,128)(2,1)S(1)}, u32[]{:S(2)}, u32[]{:S(2)}) collective-permute-start(bf16[64,3072]{1,0:T(8,128)(2,1)} %get-tuple-element.34), channel_id=1, source_target_pairs={{2,0},{4,2},{6,4},{8,6},{10,8},{12,10},{14,12},{16,14},{18,16},{20... | collective-permute-start | bytes 1179656 | tf_op jit(solution)/shard_map/ppermute | solution.py:143
  186.9 1.9 collective-permute-start.3
  188.8 4.5 %collective-permute-start.4 = (bf16[64,3072]{1,0:T(8,128)(2,1)S(1)}, bf16[64,3072]{1,0:T(8,128)(2,1)S(1)}, u32[]{:S(2)}, u32[]{:S(2)}) collective-permute-start(bf16[64,3072]{1,0:T(8,128)(2,1)S(1)} %get-tuple-element.30), channel_id=1, source_target_pairs={{2,0},{4,2},{6,4},{8,6},{10,8},{12,10},{14,12},{16,14},{18,16},{20... | collective-permute-start | bytes 1179656 | tf_op jit(solution)/shard_map/ppermute | solution.py:143
  193.4 0.1 broadcast.179.clone
  193.4 1.2 constant_dynamic-slice_fusion.1
  194.6 1.6 collective-permute-start.2
  196.2 81.5 %collective-permute-done.6.above_ref = bf16[64,3072]{1,0:T(8,128)(2,1)S(1)} collective-permute-done((bf16[64,3072]{1,0:T(8,128)(2,1)}, bf16[64,3072]{1,0:T(8,128)(2,1)S(1)}, u32[]{:S(2)}, u32[]{:S(2)}) %collective-permute-start.6) | collective-permute-done | bytes 393248 | tf_op jit(solution)/shard_map/ppermute | solution.py:143
  277.7 0.0 collective-permute-done.7.below_ref
  277.7 0.0 all-to-all-done.2
  277.7 1.4 copy-done.10
  279.1 6.3 %shard_map.80 = bf16[128,3072]{1,0:T(8,128)(2,1)S(1)} custom-call(s32[144]{0:T(256)S(1)} %reshape.155.codes, f32[128,3072]{1,0:T(8,128)S(1)} %copy-done.10, bf16[64,3072]{1,0:T(8,128)(2,1)S(1)} %collective-permute-done.6.above_ref, bf16[64,3072]{1,0:T(8,128)(2,1)S(1)} %collective-permute-done.7.below_ref, bf16[144,64,256]{2,1,0:T(8,128)(2,1)} %bitcast.10.in_ref), custom_call_target="tpu_custom_call" | custom-call | bytes 8388608 | tf_op jit(solution)/shard_map/pallas_call | solution.py:250
  285.4 0.1 broadcast.179.clone.2
  285.5 0.1 constant_dynamic-slice_fusion.2
  285.5 1.4 collective-permute-start.8
  286.9 0.0 collective-permute-done.3.above_ref
  286.9 0.0 collective-permute-done.4.below_ref
  286.9 6.2 %shard_map.79 = bf16[128,3072]{1,0:T(8,128)(2,1)S(1)} custom-call(s32[144]{0:T(256)S(1)} %reshape.155.codes, f32[128,3072]{1,0:T(8,128)S(1)} %copy-done.9, bf16[64,3072]{1,0:T(8,128)(2,1)S(1)} %collective-permute-done.3.above_ref, bf16[64,3072]{1,0:T(8,128)(2,1)S(1)} %collective-permute-done.4.below_ref, bf16[144,64,256]{2,1,0:T(8,128)(2,1)} %bitcast.10.in_ref), custom_call_target="tpu_custom_call" | custom-call | bytes 8388608 | tf_op jit(solution)/shard_map/pallas_call | solution.py:250
  293.1 0.1 broadcast.179.clone.1
  293.2 0.1 constant_dynamic-slice_fusion
  293.3 0.6 collective-permute-start.5
  293.9 0.0 collective-permute-done.2
  293.9 0.0 copy-start.14
  293.9 1.6 collective-permute-done.8
  295.5 0.0 copy-start.15
  295.6 6.3 %collective-permute-done.5 = bf16[64,3072]{1,0:T(8,128)(2,1)S(1)} collective-permute-done((bf16[64,3072]{1,0:T(8,128)(2,1)S(1)}, bf16[64,3072]{1,0:T(8,128)(2,1)S(1)}, u32[]{:S(2)}, u32[]{:S(2)}) %collective-permute-start.5) | collective-permute-done | bytes 393248 | tf_op jit(solution)/shard_map/ppermute | solution.py:154
  301.9 0.0 copy-start.13
  301.9 0.9 copy-done.13
  (20 shorter events, 0.1 us)
Async XLA Ops:
  0.6 20.9 %copy-start = (bf16[128,3072]{1,0:T(8,128)(2,1)S(1)}, bf16[128,3072]{1,0:T(8,128)(2,1)}, u32[]{:S(2)}) copy-start(bf16[128,3072]{1,0:T(8,128)(2,1)} %k_ref.4) | copy-start | bytes 2359300
  0.6 20.9 %copy-start.1 = (bf16[128,3072]{1,0:T(8,128)(2,1)S(1)}, bf16[128,3072]{1,0:T(8,128)(2,1)}, u32[]{:S(2)}) copy-start(bf16[128,3072]{1,0:T(8,128)(2,1)} %v_ref.2) | copy-start | bytes 2359300
  15.0 14.3 %collective-permute-start = (bf16[2,64,3072]{2,1,0:T(8,128)(2,1)S(1)}, bf16[2,64,3072]{2,1,0:T(8,128)(2,1)S(1)}, u32[]{:S(2)}, u32[]{:S(2)}) collective-permute-start(bf16[2,64,3072]{2,1,0:T(8,128)(2,1)S(1)} %pad_maximum_fusion), channel_id=1, source_target_pairs={{0,2},{2,4},{4,6},{6,8},{8,10},{10,12},{12,14},{14,16},{16,18},{18... | collective-permute-start | bytes 2359304 | tf_op jit(solution)/shard_map/ppermute | solution.py:143
  17.0 14.1 %collective-permute-start.1 = (bf16[2,64,3072]{2,1,0:T(8,128)(2,1)S(1)}, bf16[2,64,3072]{2,1,0:T(8,128)(2,1)S(1)}, u32[]{:S(2)}, u32[]{:S(2)}) collective-permute-start(bf16[2,64,3072]{2,1,0:T(8,128)(2,1)S(1)} %pad_maximum_fusion.1), channel_id=1, source_target_pairs={{2,0},{4,2},{6,4},{8,6},{10,8},{12,10},{14,12},{16,14},{18,16},{20... | collective-permute-start | bytes 2359304 | tf_op jit(solution)/shard_map/ppermute | solution.py:143
  29.3 0.9 copy-start.4
  31.1 0.9 copy-start.7
  32.0 114.8 %copy-start.2 = (bf16[128,3072]{1,0:T(8,128)(2,1)S(1)}, bf16[128,3072]{1,0:T(8,128)(2,1)}, u32[]{:S(2)}) copy-start(bf16[128,3072]{1,0:T(8,128)(2,1)} %q_ref.3) | copy-start | bytes 2359300
  32.0 114.8 %copy-start.3 = (bf16[128,3072]{1,0:T(8,128)(2,1)S(1)}, bf16[128,3072]{1,0:T(8,128)(2,1)}, u32[]{:S(2)}) copy-start(bf16[128,3072]{1,0:T(8,128)(2,1)} %g_ref.3) | copy-start | bytes 2359300
  32.0 114.8 %all-to-all-start.1 = ((bf16[16,9,64,256]{3,2,1,0:T(8,128)(2,1)}), bf16[16,9,64,256]{3,2,1,0:T(8,128)(2,1)}, u32[]{:S(2)}, u32[]{:S(2)}) async-start(bf16[16,9,64,256]{3,2,1,0:T(8,128)(2,1)} %bitcast.15), calls=%async_computation.1 | async-start | bytes 9437184 | tf_op jit(solution)/shard_map/all_to_all | solution.py:198
  146.8 1.1 copy-start.5
  147.9 1.1 copy-start.8
  163.8 5.8 %copy-start.6 = (bf16[2,64,3072]{2,1,0:T(8,128)(2,1)S(1)}, bf16[2,64,3072]{2,1,0:T(8,128)(2,1)}, u32[]{:S(2)}) copy-start(bf16[2,64,3072]{2,1,0:T(8,128)(2,1)} %copy-done.4) | copy-start | bytes 2359300
  163.8 113.9 %all-to-all-start.2 = ((bf16[16,9,64,256]{3,2,1,0:T(8,128)(2,1)}), bf16[16,9,64,256]{3,2,1,0:T(8,128)(2,1)}, u32[]{:S(2)}, u32[]{:S(2)}) async-start(bf16[16,9,64,256]{3,2,1,0:T(8,128)(2,1)} %bitcast.16), calls=%async_computation.2 | async-start | bytes 9437184 | tf_op jit(solution)/shard_map/all_to_all | solution.py:244
  178.8 0.9 copy-start.11
  179.6 0.7 copy-start.12
  180.4 97.3 %collective-permute-start.6 = (bf16[64,3072]{1,0:T(8,128)(2,1)}, bf16[64,3072]{1,0:T(8,128)(2,1)S(1)}, u32[]{:S(2)}, u32[]{:S(2)}) collective-permute-start(bf16[64,3072]{1,0:T(8,128)(2,1)} %get-tuple-element.33), channel_id=1, source_target_pairs={{0,2},{2,4},{4,6},{6,8},{8,10},{10,12},{12,14},{14,16},{16,18},{18... | collective-permute-start | bytes 1179656 | tf_op jit(solution)/shard_map/ppermute | solution.py:143
  182.4 95.2 %collective-permute-start.7 = (bf16[64,3072]{1,0:T(8,128)(2,1)}, bf16[64,3072]{1,0:T(8,128)(2,1)S(1)}, u32[]{:S(2)}, u32[]{:S(2)}) collective-permute-start(bf16[64,3072]{1,0:T(8,128)(2,1)} %get-tuple-element.34), channel_id=1, source_target_pairs={{2,0},{4,2},{6,4},{8,6},{10,8},{12,10},{14,12},{16,14},{18,16},{20... | collective-permute-start | bytes 1179656 | tf_op jit(solution)/shard_map/ppermute | solution.py:143
  186.9 100.0 %collective-permute-start.3 = (bf16[64,3072]{1,0:T(8,128)(2,1)}, bf16[64,3072]{1,0:T(8,128)(2,1)S(1)}, u32[]{:S(2)}, u32[]{:S(2)}) collective-permute-start(bf16[64,3072]{1,0:T(8,128)(2,1)} %copy-done.12), channel_id=1, source_target_pairs={{0,2},{2,4},{4,6},{6,8},{8,10},{10,12},{12,14},{14,16},{16,18},{18... | collective-permute-start | bytes 1179656 | tf_op jit(solution)/shard_map/ppermute | solution.py:143
  188.8 98.1 %collective-permute-start.4 = (bf16[64,3072]{1,0:T(8,128)(2,1)S(1)}, bf16[64,3072]{1,0:T(8,128)(2,1)S(1)}, u32[]{:S(2)}, u32[]{:S(2)}) collective-permute-start(bf16[64,3072]{1,0:T(8,128)(2,1)S(1)} %get-tuple-element.30), channel_id=1, source_target_pairs={{2,0},{4,2},{6,4},{8,6},{10,8},{12,10},{14,12},{16,14},{18,16},{20... | collective-permute-start | bytes 1179656 | tf_op jit(solution)/shard_map/ppermute | solution.py:143
  194.6 99.2 %collective-permute-start.2 = (bf16[64,3072]{1,0:T(8,128)(2,1)S(1)}, bf16[64,3072]{1,0:T(8,128)(2,1)S(1)}, u32[]{:S(2)}, u32[]{:S(2)}) collective-permute-start(bf16[64,3072]{1,0:T(8,128)(2,1)S(1)} %get-tuple-element.39), channel_id=1, source_target_pairs={{0,1},{1,0},{2,3},{3,2},{4,5},{5,4},{6,7},{7,6},{8,9},{9,8},{10,11... | collective-permute-start | bytes 1179656 | tf_op jit(solution)/shard_map/ppermute | solution.py:154
  277.7 1.4 copy-start.10
  279.1 7.8 %copy-start.9 = (f32[128,3072]{1,0:T(8,128)S(1)}, f32[128,3072]{1,0:T(8,128)}, u32[]{:S(2)}) copy-start(f32[128,3072]{1,0:T(8,128)} %get-tuple-element.28.own_ref) | copy-start | bytes 4718596
  285.5 10.0 %collective-permute-start.8 = (bf16[64,3072]{1,0:T(8,128)(2,1)S(1)}, bf16[64,3072]{1,0:T(8,128)(2,1)S(1)}, u32[]{:S(2)}, u32[]{:S(2)}) collective-permute-start(bf16[64,3072]{1,0:T(8,128)(2,1)S(1)} %get-tuple-element.35), channel_id=1, source_target_pairs={{0,1},{1,0},{2,3},{3,2},{4,5},{5,4},{6,7},{7,6},{8,9},{9,8},{10,11... | collective-permute-start | bytes 1179656 | tf_op jit(solution)/shard_map/ppermute | solution.py:154
  293.3 8.5 %collective-permute-start.5 = (bf16[64,3072]{1,0:T(8,128)(2,1)S(1)}, bf16[64,3072]{1,0:T(8,128)(2,1)S(1)}, u32[]{:S(2)}, u32[]{:S(2)}) collective-permute-start(bf16[64,3072]{1,0:T(8,128)(2,1)S(1)} %get-tuple-element.37), channel_id=1, source_target_pairs={{0,1},{1,0},{2,3},{3,2},{4,5},{5,4},{6,7},{7,6},{8,9},{9,8},{10,11... | collective-permute-start | bytes 1179656 | tf_op jit(solution)/shard_map/ppermute | solution.py:154
  293.9 7.9 %copy-start.14 = (bf16[64,6144]{1,0:T(8,128)(2,1)}, bf16[64,6144]{1,0:T(8,128)(2,1)S(1)}, u32[]{:S(2)}) copy-start(bf16[64,6144]{1,0:T(8,128)(2,1)S(1)} %constant_dynamic-update-slice_fusion.2) | copy-start | bytes 2359300
  295.5 6.3 %copy-start.15 = (bf16[64,6144]{1,0:T(8,128)(2,1)}, bf16[64,6144]{1,0:T(8,128)(2,1)S(1)}, u32[]{:S(2)}) copy-start(bf16[64,6144]{1,0:T(8,128)(2,1)S(1)} %constant_dynamic-update-slice_fusion.1) | copy-start | bytes 2359300
  301.9 0.9 copy-start.13

commit v5 on v4

--- a/solution.py
+++ b/solution.py
@@ -124,15 +124,18 @@
     acc[:block] += above_ref[...].astype(F32)
     acc[last] += below_ref[...].astype(F32)
 
-    @pl.loop(0, count)
-    def _(s):
-        code = codes[s]
-
-        @pl.when(code >= 0)
-        def _():
+    batch = next(n for n in (8, 4, 2, 1) if count % n == 0)
+
+    @pl.loop(0, count // batch)
+    def _(i):
+        for j in range(batch):
+            code = codes[i * batch + j]
+            term = in_ref[i * batch + j, :, first:first + dim].astype(F32)
+            term = jnp.where(code >= 0, term, 0.0)
+            code = jnp.maximum(code, 0)
             rows = pl.ds(pl.multiple_of(code // heads * block, block), block)
             cols = pl.ds(pl.multiple_of(code % heads * dim, dim), dim)
-            acc[rows, cols] += in_ref[s, :, first:first + dim].astype(F32)
+            acc[rows, cols] += term
 
     out_ref[...] = acc[...].astype(BF16)
 
@@ -182,6 +185,9 @@
     up = shifted(jnp.stack([own_k[tokens - block:], own_v[tokens - block:]]), "seq", 1)
     down = shifted(jnp.stack([own_k[:block], own_v[:block]]), "seq", -1)
     full = pl.BlockSpec(memory_space=VMEM)
+    up = shifted(jnp.stack([key_rows[tokens - block:], value_rows[tokens - block:]]), "seq", 1)
+    down = shifted(jnp.stack([key_rows[:block], value_rows[:block]]), "seq", -1)
+    asked, up, down = lax.optimization_barrier((asked, up, down))
     outgoing = pl.pallas_call(
         functools.partial(gather_kernel, block, dim, heads, cap),
         out_shape=jax.ShapeDtypeStruct((count, block, 2 * dim), BF16),
@@ -192,9 +198,7 @@
             out_specs=pl.BlockSpec((cap, block, 2 * dim), lambda i, *_: (i, 0, 0)),
         ),
         compiler_params=pltpu.CompilerParams(vmem_limit_bytes=LIMIT),
-        cost_estimate=pl.CostEstimate(flops=0, bytes_accessed=16 * 2**20, transcendentals=0),
-    )(asked, own_k, own_v)
-    outgoing, up, down = lax.optimization_barrier((outgoing, up, down))
+    )(asked, key_rows, value_rows)
     fetched = lax.all_to_all(
         outgoing.reshape(peers, cap, block, 2 * dim), "seq", split_axis=0, concat_axis=0, tiled=True
     ).reshape(count, block, 2 * dim)

time: 305 us -> 299 us (0.980)
  starting transfers between devices: 39.6 us -> 32.3 us
  blocking collectives: 10.1 us -> 15.8 us
  Pallas kernels: 43.5 us -> 39.3 us
    all_to_all x1, blocking collectives: 10.1 us -> 15.8 us  [local(): lax.all_to_all(asked.reshape(peers, cap), 'seq', split_axis=0, concat_axi...]
    all_to_all x1, starting transfers between devices: 10.9 us -> 6.23 us  [local(): lax.all_to_all(outgoing.reshape(peers, cap, block, 2 * dim), 'seq', split...]
    pallas_call x2, Pallas kernels: 12.5 us -> 8.3 us  [collected(): pl.pallas_call(functools.partial(collect_kernel, blocks, block, dim, head...]
    unnamed x33 -> x35, local copies, waits for them, and re-layouts: 8.85 us -> 6.31 us
  transfers between devices with their start and end apart: 11 -> 11, of which waited for: 6 -> 4; matrix products, arithmetic and copies ran while one was open for 1% -> 2% of each run, Pallas kernels for 9% -> 6%
where the time goes in v5:
time: 299 us; the launch traced here: 297 us
  waiting for transfers between devices  195 us (65%)
  Pallas kernels  39.3 us (13%)
  starting transfers between devices  32.3 us (11%)
  blocking collectives  15.8 us (5%)
  local copies, waits for them, and re-layouts  10.3 us (3%)
    all_to_all x1, waiting for transfers between devices, local(): lax.all_to_all(outgoing.reshape(peers, cap, block, 2 * dim), 'seq', split...  104 us
    ppermute x6, waiting for transfers between devices, shifted(): lax.ppermute(value, axis, [(source, source + steps) for source in range(f...  81.5 us
    ppermute x6, starting transfers between devices, shifted(): lax.ppermute(value, axis, [(source, source + steps) for source in range(f...  17.6 us
    all_to_all x1, blocking collectives, local(): lax.all_to_all(asked.reshape(peers, cap), 'seq', split_axis=0, concat_axi...  15.8 us
    pallas_call x1, Pallas kernels, local(): pl.pallas_call(functools.partial(attend_kernel, blocks, block, dim, heads...  14.8 us
    ppermute x3, waiting for transfers between devices, exchanged(): lax.ppermute(piece, axis, [(i, (i + r) % count) for i in range(count)])  9.76 us
    pallas_call x1, Pallas kernels, local(): pl.pallas_call(functools.partial(window_kernel, blocks, block, dim, heads...  9.11 us
    pallas_call x2, Pallas kernels, collected(): pl.pallas_call(functools.partial(collect_kernel, blocks, block, dim, head...  8.3 us
  transfers between devices with their start and end apart: 11, of which 4 were waited for; matrix products, arithmetic and copies ran while one was open for 2% of the time, Pallas kernels for 6%

profile of v5, /device:TPU:16, one launch (start us, length us, event | category | flops | bytes accessed | tf_op | source)
XLA Modules:
  0.0 296.8 jit_solution(6769788247730561923)
XLA Ops:
  0.6 0.0 copy-start
  0.6 0.0 copy-start.1
  0.7 0.0 copy-start.16
  0.7 1.6 slice_bitcast_fusion
  2.2 0.9 pad_maximum_fusion.1
  3.2 2.7 collective-permute-start.1
  5.9 0.9 pad_maximum_fusion
  6.9 1.9 collective-permute-start
  8.8 0.0 copy-done.16
  8.8 0.1 copy.12
  8.9 0.1 reshape.154
  9.0 0.2 convert_reduce_fusion
  9.2 0.1 select_reduce_fusion
  9.4 0.1 sub.24
  9.5 15.8 %all_to_all.16 = s32[16,1,9]{2,1,0:T(1,128)S(1)} all-to-all(s32[16,1,9]{2,1,0:T(1,128)S(1)} %bitcast.17), channel_id=1, replica_groups=mesh['seq'=16,'head'=2] {'seq'}, dimensions={0} | all-to-all | bytes 1152 | tf_op jit(solution)/shard_map/all_to_all | solution.py:181
  25.3 0.5 broadcast.201
  25.8 0.7 reduce.3
  26.4 0.1 reshape.155.codes
  26.5 0.0 collective-permute-done.1.down_ref
  26.5 0.0 copy-start.4
  26.6 0.0 collective-permute-done.up_ref
  26.6 0.0 copy-done
  26.6 0.0 copy-start.6
  26.6 7.1 %shard_map.76 = bf16[144,64,256]{2,1,0:T(8,128)(2,1)} custom-call(s32[144]{0:T(256)S(1)} %reshape.155.codes, bf16[128,3072]{1,0:T(8,128)(2,1)S(1)} %copy-done, bf16[128,3072]{1,0:T(8,128)(2,1)S(1)} %copy-done.1), custom_call_target="tpu_custom_call" | custom-call | tf_op jit(solution)/shard_map/pallas_call | solution.py:191
  33.7 0.0 copy-done.4
  33.7 6.2 %all-to-all-start.1 = ((bf16[16,9,64,256]{3,2,1,0:T(8,128)(2,1)}), bf16[16,9,64,256]{3,2,1,0:T(8,128)(2,1)}, u32[]{:S(2)}, u32[]{:S(2)}) async-start(bf16[16,9,64,256]{3,2,1,0:T(8,128)(2,1)} %bitcast.15), calls=%async_computation.1 | async-start | bytes 9437184 | tf_op jit(solution)/shard_map/all_to_all | solution.py:202
  40.0 0.1 add_convert_fusion.edge
  40.0 103.9 %all-to-all-done.1 = bf16[16,9,64,256]{3,2,1,0:T(8,128)(2,1)} async-done(((bf16[16,9,64,256]{3,2,1,0:T(8,128)(2,1)}), bf16[16,9,64,256]{3,2,1,0:T(8,128)(2,1)}, u32[]{:S(2)}, u32[]{:S(2)}) %all-to-all-start.1) | async-done | bytes 4718624 | tf_op jit(solution)/shard_map/all_to_all | solution.py:202
  143.9 0.0 copy-done.3
  143.9 1.1 copy-done.5
  145.0 1.1 copy-done.7
  146.2 14.8 %shard_map.77 = (bf16[24,128,192]{2,1,0:T(8,128)(2,1)}, bf16[24,128,320]{2,1,0:T(8,128)(2,1)}, bf16[144,64,256]{2,1,0:T(8,128)(2,1)}) custom-call(s32[96]{0:T(128)S(1)} %multiply_add_fusion.slots, s32[2]{0:T(128)S(1)} %add_convert_fusion.edge, bf16[128,3072]{1,0:T(8,128)(2,1)S(1)} %copy-done.2, bf16[128,3072]{1,0:T(8,128)(2,1)S(1)} %copy-done, ...), custom_call_target="tpu_custom_call" | custom-call | flops 1006632960 | bytes 16777216 | tf_op jit(solution)/shard_map/pallas_call | solution.py:218
  161.0 4.8 %all-to-all-start.2 = ((bf16[16,9,64,256]{3,2,1,0:T(8,128)(2,1)}), bf16[16,9,64,256]{3,2,1,0:T(8,128)(2,1)}, u32[]{:S(2)}, u32[]{:S(2)}) async-start(bf16[16,9,64,256]{3,2,1,0:T(8,128)(2,1)} %bitcast.16), calls=%async_computation.2 | async-start | bytes 9437184 | tf_op jit(solution)/shard_map/all_to_all | solution.py:248
  165.8 9.1 %shard_map.78 = (bf16[128,3072]{1,0:T(8,128)(2,1)S(1)}, f32[128,3072]{1,0:T(8,128)}, f32[128,3072]{1,0:T(8,128)}, bf16[64,3072]{1,0:T(8,128)(2,1)S(1)}, bf16[64,...) custom-call(s32[96]{0:T(128)S(1)} %multiply_add_fusion.slots, ...), custom_call_target="tpu_custom_call" | custom-call | flops 1006632960 | bytes 16777216 | tf_op jit(solution)/shard_map/pallas_call | solution.py:234
  174.9 0.9 copy-done.11
  175.8 0.7 copy-done.12
  176.5 2.0 collective-permute-start.6
  178.6 4.4 %collective-permute-start.7 = (bf16[64,3072]{1,0:T(8,128)(2,1)}, bf16[64,3072]{1,0:T(8,128)(2,1)S(1)}, u32[]{:S(2)}, u32[]{:S(2)}) collective-permute-start(bf16[64,3072]{1,0:T(8,128)(2,1)} %get-tuple-element.30), channel_id=1, source_target_pairs={{2,0},{4,2},{6,4},{8,6},{10,8},{12,10},{14,12},{16,14},{18,16},{20... | collective-permute-start | bytes 1179656 | tf_op jit(solution)/shard_map/ppermute | solution.py:146
  183.0 1.9 collective-permute-start.3
  185.0 4.5 %collective-permute-start.4 = (bf16[64,3072]{1,0:T(8,128)(2,1)S(1)}, bf16[64,3072]{1,0:T(8,128)(2,1)S(1)}, u32[]{:S(2)}, u32[]{:S(2)}) collective-permute-start(bf16[64,3072]{1,0:T(8,128)(2,1)S(1)} %get-tuple-element.26), channel_id=1, source_target_pairs={{2,0},{4,2},{6,4},{8,6},{10,8},{12,10},{14,12},{16,14},{18,16},{20... | collective-permute-start | bytes 1179656 | tf_op jit(solution)/shard_map/ppermute | solution.py:146
  189.5 0.1 broadcast.179.clone
  189.6 1.2 constant_dynamic-slice_fusion.1
  190.8 1.6 collective-permute-start.2
  192.3 81.5 %collective-permute-done.6.above_ref = bf16[64,3072]{1,0:T(8,128)(2,1)S(1)} collective-permute-done((bf16[64,3072]{1,0:T(8,128)(2,1)}, bf16[64,3072]{1,0:T(8,128)(2,1)S(1)}, u32[]{:S(2)}, u32[]{:S(2)}) %collective-permute-start.6) | collective-permute-done | bytes 393248 | tf_op jit(solution)/shard_map/ppermute | solution.py:146
  273.8 0.0 collective-permute-done.7.below_ref
  273.8 0.0 all-to-all-done.2
  273.8 1.4 copy-done.10
  275.2 4.2 %shard_map.80 = bf16[128,3072]{1,0:T(8,128)(2,1)S(1)} custom-call(s32[144]{0:T(256)S(1)} %reshape.155.codes, f32[128,3072]{1,0:T(8,128)S(1)} %copy-done.10, bf16[64,3072]{1,0:T(8,128)(2,1)S(1)} %collective-permute-done.6.above_ref, bf16[64,3072]{1,0:T(8,128)(2,1)S(1)} %collective-permute-done.7.below_ref, bf16[144,64,256]{2,1,0:T(8,128)(2,1)} %bitcast.10.in_ref), custom_call_target="tpu_custom_call" | custom-call | bytes 8388608 | tf_op jit(solution)/shard_map/pallas_call | solution.py:254
  279.5 0.1 broadcast.179.clone.2
  279.5 0.1 constant_dynamic-slice_fusion.2
  279.6 1.6 collective-permute-start.8
  281.2 0.0 collective-permute-done.3.above_ref
  281.2 0.0 collective-permute-done.4.below_ref
  281.2 4.1 %shard_map.79 = bf16[128,3072]{1,0:T(8,128)(2,1)S(1)} custom-call(s32[144]{0:T(256)S(1)} %reshape.155.codes, f32[128,3072]{1,0:T(8,128)S(1)} %copy-done.9, bf16[64,3072]{1,0:T(8,128)(2,1)S(1)} %collective-permute-done.3.above_ref, bf16[64,3072]{1,0:T(8,128)(2,1)S(1)} %collective-permute-done.4.below_ref, bf16[144,64,256]{2,1,0:T(8,128)(2,1)} %bitcast.10.in_ref), custom_call_target="tpu_custom_call" | custom-call | bytes 8388608 | tf_op jit(solution)/shard_map/pallas_call | solution.py:254
  285.3 0.1 broadcast.179.clone.1
  285.3 0.1 constant_dynamic-slice_fusion
  285.4 0.6 collective-permute-start.5
  286.0 0.0 collective-permute-done.2
  286.1 0.0 copy-start.14
  286.1 5.5 %collective-permute-done.8 = bf16[64,3072]{1,0:T(8,128)(2,1)S(1)} collective-permute-done((bf16[64,3072]{1,0:T(8,128)(2,1)S(1)}, bf16[64,3072]{1,0:T(8,128)(2,1)S(1)}, u32[]{:S(2)}, u32[]{:S(2)}) %collective-permute-start.8) | collective-permute-done | bytes 393248 | tf_op jit(solution)/shard_map/ppermute | solution.py:157
  291.6 0.0 copy-start.15
  291.6 4.3 %collective-permute-done.5 = bf16[64,3072]{1,0:T(8,128)(2,1)S(1)} collective-permute-done((bf16[64,3072]{1,0:T(8,128)(2,1)S(1)}, bf16[64,3072]{1,0:T(8,128)(2,1)S(1)}, u32[]{:S(2)}, u32[]{:S(2)}) %collective-permute-start.5) | collective-permute-done | bytes 393248 | tf_op jit(solution)/shard_map/ppermute | solution.py:157
  295.9 0.0 copy-start.13
  295.9 0.9 copy-done.13
  (22 shorter events, 0.1 us)
Async XLA Ops:
  0.6 25.9 %copy-start = (bf16[128,3072]{1,0:T(8,128)(2,1)S(1)}, bf16[128,3072]{1,0:T(8,128)(2,1)}, u32[]{:S(2)}) copy-start(bf16[128,3072]{1,0:T(8,128)(2,1)} %k_ref.5) | copy-start | bytes 2359300
  0.6 25.9 %copy-start.1 = (bf16[128,3072]{1,0:T(8,128)(2,1)S(1)}, bf16[128,3072]{1,0:T(8,128)(2,1)}, u32[]{:S(2)}) copy-start(bf16[128,3072]{1,0:T(8,128)(2,1)} %v_ref.3) | copy-start | bytes 2359300
  0.7 8.2 %copy-start.16 = (s32[2,24,2]{1,2,0:T(2,128)S(1)}, s32[2,24,2]{1,2,0:T(2,128)}, u32[]{:S(2)}) copy-start(s32[2,24,2]{1,2,0:T(2,128)} %param.9) | copy-start | bytes 1156
  3.2 23.3 %collective-permute-start.1 = (bf16[2,64,3072]{2,1,0:T(8,128)(2,1)}, bf16[2,64,3072]{2,1,0:T(8,128)(2,1)S(1)}, u32[]{:S(2)}, u32[]{:S(2)}) collective-permute-start(bf16[2,64,3072]{2,1,0:T(8,128)(2,1)} %pad_maximum_fusion.1), channel_id=1, source_target_pairs={{2,0},{4,2},{6,4},{8,6},{10,8},{12,10},{14,12},{16,14},{18,16},{20... | collective-permute-start | bytes 2359304 | tf_op jit(solution)/shard_map/ppermute | solution.py:146
  6.9 19.7 %collective-permute-start = (bf16[2,64,3072]{2,1,0:T(8,128)(2,1)}, bf16[2,64,3072]{2,1,0:T(8,128)(2,1)S(1)}, u32[]{:S(2)}, u32[]{:S(2)}) collective-permute-start(bf16[2,64,3072]{2,1,0:T(8,128)(2,1)} %pad_maximum_fusion), channel_id=1, source_target_pairs={{0,2},{2,4},{4,6},{6,8},{8,10},{10,12},{12,14},{14,16},{16,18},{18... | collective-permute-start | bytes 2359304 | tf_op jit(solution)/shard_map/ppermute | solution.py:146
  26.5 7.2 %copy-start.4 = (bf16[2,64,3072]{2,1,0:T(8,128)(2,1)}, bf16[2,64,3072]{2,1,0:T(8,128)(2,1)S(1)}, u32[]{:S(2)}) copy-start(bf16[2,64,3072]{2,1,0:T(8,128)(2,1)S(1)} %collective-permute-done.1.down_ref) | copy-start | bytes 2359300
  26.6 7.1 %copy-start.6 = (bf16[2,64,3072]{2,1,0:T(8,128)(2,1)}, bf16[2,64,3072]{2,1,0:T(8,128)(2,1)S(1)}, u32[]{:S(2)}) copy-start(bf16[2,64,3072]{2,1,0:T(8,128)(2,1)S(1)} %collective-permute-done.up_ref) | copy-start | bytes 2359300
  33.7 110.2 %copy-start.2 = (bf16[128,3072]{1,0:T(8,128)(2,1)S(1)}, bf16[128,3072]{1,0:T(8,128)(2,1)}, u32[]{:S(2)}) copy-start(bf16[128,3072]{1,0:T(8,128)(2,1)} %q_ref.3) | copy-start | bytes 2359300
  33.7 110.2 %copy-start.3 = (bf16[128,3072]{1,0:T(8,128)(2,1)S(1)}, bf16[128,3072]{1,0:T(8,128)(2,1)}, u32[]{:S(2)}) copy-start(bf16[128,3072]{1,0:T(8,128)(2,1)} %g_ref.3) | copy-start | bytes 2359300
  33.7 110.2 %all-to-all-start.1 = ((bf16[16,9,64,256]{3,2,1,0:T(8,128)(2,1)}), bf16[16,9,64,256]{3,2,1,0:T(8,128)(2,1)}, u32[]{:S(2)}, u32[]{:S(2)}) async-start(bf16[16,9,64,256]{3,2,1,0:T(8,128)(2,1)} %bitcast.15), calls=%async_computation.1 | async-start | bytes 9437184 | tf_op jit(solution)/shard_map/all_to_all | solution.py:202
  143.9 1.1 copy-start.5
  145.0 1.1 copy-start.7
  161.0 4.8 %copy-start.8 = (bf16[2,64,3072]{2,1,0:T(8,128)(2,1)S(1)}, bf16[2,64,3072]{2,1,0:T(8,128)(2,1)}, u32[]{:S(2)}) copy-start(bf16[2,64,3072]{2,1,0:T(8,128)(2,1)} %copy-done.6) | copy-start | bytes 2359300
  161.0 112.9 %all-to-all-start.2 = ((bf16[16,9,64,256]{3,2,1,0:T(8,128)(2,1)}), bf16[16,9,64,256]{3,2,1,0:T(8,128)(2,1)}, u32[]{:S(2)}, u32[]{:S(2)}) async-start(bf16[16,9,64,256]{3,2,1,0:T(8,128)(2,1)} %bitcast.16), calls=%async_computation.2 | async-start | bytes 9437184 | tf_op jit(solution)/shard_map/all_to_all | solution.py:248
  174.9 0.9 copy-start.11
  175.8 0.7 copy-start.12
  176.5 97.3 %collective-permute-start.6 = (bf16[64,3072]{1,0:T(8,128)(2,1)}, bf16[64,3072]{1,0:T(8,128)(2,1)S(1)}, u32[]{:S(2)}, u32[]{:S(2)}) collective-permute-start(bf16[64,3072]{1,0:T(8,128)(2,1)} %get-tuple-element.29), channel_id=1, source_target_pairs={{0,2},{2,4},{4,6},{6,8},{8,10},{10,12},{12,14},{14,16},{16,18},{18... | collective-permute-start | bytes 1179656 | tf_op jit(solution)/shard_map/ppermute | solution.py:146
  178.6 95.2 %collective-permute-start.7 = (bf16[64,3072]{1,0:T(8,128)(2,1)}, bf16[64,3072]{1,0:T(8,128)(2,1)S(1)}, u32[]{:S(2)}, u32[]{:S(2)}) collective-permute-start(bf16[64,3072]{1,0:T(8,128)(2,1)} %get-tuple-element.30), channel_id=1, source_target_pairs={{2,0},{4,2},{6,4},{8,6},{10,8},{12,10},{14,12},{16,14},{18,16},{20... | collective-permute-start | bytes 1179656 | tf_op jit(solution)/shard_map/ppermute | solution.py:146
  183.0 98.1 %collective-permute-start.3 = (bf16[64,3072]{1,0:T(8,128)(2,1)}, bf16[64,3072]{1,0:T(8,128)(2,1)S(1)}, u32[]{:S(2)}, u32[]{:S(2)}) collective-permute-start(bf16[64,3072]{1,0:T(8,128)(2,1)} %copy-done.12), channel_id=1, source_target_pairs={{0,2},{2,4},{4,6},{6,8},{8,10},{10,12},{12,14},{14,16},{16,18},{18... | collective-permute-start | bytes 1179656 | tf_op jit(solution)/shard_map/ppermute | solution.py:146
  185.0 96.2 %collective-permute-start.4 = (bf16[64,3072]{1,0:T(8,128)(2,1)S(1)}, bf16[64,3072]{1,0:T(8,128)(2,1)S(1)}, u32[]{:S(2)}, u32[]{:S(2)}) collective-permute-start(bf16[64,3072]{1,0:T(8,128)(2,1)S(1)} %get-tuple-element.26), channel_id=1, source_target_pairs={{2,0},{4,2},{6,4},{8,6},{10,8},{12,10},{14,12},{16,14},{18,16},{20... | collective-permute-start | bytes 1179656 | tf_op jit(solution)/shard_map/ppermute | solution.py:146
  190.8 95.2 %collective-permute-start.2 = (bf16[64,3072]{1,0:T(8,128)(2,1)S(1)}, bf16[64,3072]{1,0:T(8,128)(2,1)S(1)}, u32[]{:S(2)}, u32[]{:S(2)}) collective-permute-start(bf16[64,3072]{1,0:T(8,128)(2,1)S(1)} %get-tuple-element.35), channel_id=1, source_target_pairs={{0,1},{1,0},{2,3},{3,2},{4,5},{5,4},{6,7},{7,6},{8,9},{9,8},{10,11... | collective-permute-start | bytes 1179656 | tf_op jit(solution)/shard_map/ppermute | solution.py:157
  273.8 1.4 copy-start.10
  275.2 5.9 %copy-start.9 = (f32[128,3072]{1,0:T(8,128)S(1)}, f32[128,3072]{1,0:T(8,128)}, u32[]{:S(2)}) copy-start(f32[128,3072]{1,0:T(8,128)} %get-tuple-element.24.own_ref) | copy-start | bytes 4718596
  279.6 12.0 %collective-permute-start.8 = (bf16[64,3072]{1,0:T(8,128)(2,1)S(1)}, bf16[64,3072]{1,0:T(8,128)(2,1)S(1)}, u32[]{:S(2)}, u32[]{:S(2)}) collective-permute-start(bf16[64,3072]{1,0:T(8,128)(2,1)S(1)} %get-tuple-element.31), channel_id=1, source_target_pairs={{0,1},{1,0},{2,3},{3,2},{4,5},{5,4},{6,7},{7,6},{8,9},{9,8},{10,11... | collective-permute-start | bytes 1179656 | tf_op jit(solution)/shard_map/ppermute | solution.py:157
  285.4 10.5 %collective-permute-start.5 = (bf16[64,3072]{1,0:T(8,128)(2,1)S(1)}, bf16[64,3072]{1,0:T(8,128)(2,1)S(1)}, u32[]{:S(2)}, u32[]{:S(2)}) collective-permute-start(bf16[64,3072]{1,0:T(8,128)(2,1)S(1)} %get-tuple-element.33), channel_id=1, source_target_pairs={{0,1},{1,0},{2,3},{3,2},{4,5},{5,4},{6,7},{7,6},{8,9},{9,8},{10,11... | collective-permute-start | bytes 1179656 | tf_op jit(solution)/shard_map/ppermute | solution.py:157
  286.1 9.9 %copy-start.14 = (bf16[64,6144]{1,0:T(8,128)(2,1)}, bf16[64,6144]{1,0:T(8,128)(2,1)S(1)}, u32[]{:S(2)}) copy-start(bf16[64,6144]{1,0:T(8,128)(2,1)S(1)} %constant_dynamic-update-slice_fusion.2) | copy-start | bytes 2359300
  291.6 4.3 %copy-start.15 = (bf16[64,6144]{1,0:T(8,128)(2,1)}, bf16[64,6144]{1,0:T(8,128)(2,1)S(1)}, u32[]{:S(2)}) copy-start(bf16[64,6144]{1,0:T(8,128)(2,1)S(1)} %constant_dynamic-update-slice_fusion.1) | copy-start | bytes 2359300
  295.9 0.9 copy-start.13

commit v6 on v5

--- a/solution.py
+++ b/solution.py
@@ -203,7 +203,7 @@
         outgoing.reshape(peers, cap, block, 2 * dim), "seq", split_axis=0, concat_axis=0, tiled=True
     ).reshape(count, block, 2 * dim)
     edge = jnp.stack([(me > 0), (me < peers - 1)]).astype(jnp.int32)
-    step = next(n for n in (4, 3, 2, 1) if heads % n == 0)
+    step = next(n for n in (6, 4, 3, 2, 1) if heads % n == 0)
     wide = pl.BlockSpec((tokens, step * dim), lambda i, *_: (0, i))
     side = pl.BlockSpec((2, block, step * dim), lambda i, *_: (0, 0, i))
     thin = pl.BlockSpec((block, step * dim), lambda i, *_: (0, i))

time: 299 us -> 298 us (level)
  no operation moved by 1% of the time
where the time goes in v6:
time: 298 us; the launch traced here: 296 us
  waiting for transfers between devices  196 us (66%)
  Pallas kernels  38 us (13%)
  starting transfers between devices  32.3 us (11%)
  blocking collectives  15.8 us (5%)
  local copies, waits for them, and re-layouts  10.3 us (3%)
    all_to_all x1, waiting for transfers between devices, local(): lax.all_to_all(outgoing.reshape(peers, cap, block, 2 * dim), 'seq', split...  104 us
    ppermute x6, waiting for transfers between devices, shifted(): lax.ppermute(value, axis, [(source, source + steps) for source in range(f...  82.4 us
    ppermute x6, starting transfers between devices, shifted(): lax.ppermute(value, axis, [(source, source + steps) for source in range(f...  17.6 us
    all_to_all x1, blocking collectives, local(): lax.all_to_all(asked.reshape(peers, cap), 'seq', split_axis=0, concat_axi...  15.8 us
    pallas_call x1, Pallas kernels, local(): pl.pallas_call(functools.partial(attend_kernel, blocks, block, dim, heads...  14.4 us
    ppermute x3, waiting for transfers between devices, exchanged(): lax.ppermute(piece, axis, [(i, (i + r) % count) for i in range(count)])  9.76 us
    pallas_call x2, Pallas kernels, collected(): pl.pallas_call(functools.partial(collect_kernel, blocks, block, dim, head...  8.3 us
    pallas_call x1, Pallas kernels, local(): pl.pallas_call(functools.partial(window_kernel, blocks, block, dim, heads...  8.21 us
  transfers between devices with their start and end apart: 11, of which 4 were waited for; matrix products, arithmetic and copies ran while one was open for 2% of the time, Pallas kernels for 6%

profile of v6, /device:TPU:16, one launch (start us, length us, event | category | flops | bytes accessed | tf_op | source)
XLA Modules:
  0.0 296.4 jit_solution(5635763981985536024)
XLA Ops:
  0.6 0.0 copy-start
  0.6 0.0 copy-start.1
  0.7 0.0 copy-start.16
  0.7 1.6 slice_bitcast_fusion
  2.2 0.9 pad_maximum_fusion.1
  3.2 2.7 collective-permute-start.1
  5.9 0.9 pad_maximum_fusion
  6.9 1.9 collective-permute-start
  8.8 0.1 copy.12
  8.9 0.1 reshape.154
  9.0 0.2 convert_reduce_fusion
  9.2 0.1 select_reduce_fusion
  9.4 0.1 sub.24
  9.5 15.8 %all_to_all.16 = s32[16,1,9]{2,1,0:T(1,128)S(1)} all-to-all(s32[16,1,9]{2,1,0:T(1,128)S(1)} %bitcast.17), channel_id=1, replica_groups=mesh['seq'=16,'head'=2] {'seq'}, dimensions={0} | all-to-all | bytes 1152 | tf_op jit(solution)/shard_map/all_to_all | solution.py:181
  25.3 0.5 broadcast.201
  25.8 0.7 reduce.3
  26.4 0.1 reshape.155.codes
  26.5 0.0 collective-permute-done.1.down_ref
  26.5 0.0 copy-start.4
  26.6 0.0 collective-permute-done.up_ref
  26.6 0.0 copy-start.6
  26.6 7.1 %shard_map.76 = bf16[144,64,256]{2,1,0:T(8,128)(2,1)} custom-call(s32[144]{0:T(256)S(1)} %reshape.155.codes, bf16[128,3072]{1,0:T(8,128)(2,1)S(1)} %copy-done, bf16[128,3072]{1,0:T(8,128)(2,1)S(1)} %copy-done.1), custom_call_target="tpu_custom_call" | custom-call | tf_op jit(solution)/shard_map/pallas_call | solution.py:191
  33.7 0.0 copy-done.4
  33.7 6.2 %all-to-all-start.1 = ((bf16[16,9,64,256]{3,2,1,0:T(8,128)(2,1)}), bf16[16,9,64,256]{3,2,1,0:T(8,128)(2,1)}, u32[]{:S(2)}, u32[]{:S(2)}) async-start(bf16[16,9,64,256]{3,2,1,0:T(8,128)(2,1)} %bitcast.15), calls=%async_computation.1 | async-start | bytes 9437184 | tf_op jit(solution)/shard_map/all_to_all | solution.py:202
  40.0 0.1 add_convert_fusion.edge
  40.0 103.9 %all-to-all-done.1 = bf16[16,9,64,256]{3,2,1,0:T(8,128)(2,1)} async-done(((bf16[16,9,64,256]{3,2,1,0:T(8,128)(2,1)}), bf16[16,9,64,256]{3,2,1,0:T(8,128)(2,1)}, u32[]{:S(2)}, u32[]{:S(2)}) %all-to-all-start.1) | async-done | bytes 4718624 | tf_op jit(solution)/shard_map/all_to_all | solution.py:202
  143.9 0.0 copy-done.3
  143.9 1.1 copy-done.5
  145.0 1.1 copy-done.7
  146.2 14.4 %shard_map.77 = (bf16[24,128,192]{2,1,0:T(8,128)(2,1)}, bf16[24,128,320]{2,1,0:T(8,128)(2,1)}, bf16[144,64,256]{2,1,0:T(8,128)(2,1)}) custom-call(s32[96]{0:T(128)S(1)} %multiply_add_fusion.slots, s32[2]{0:T(128)S(1)} %add_convert_fusion.edge, bf16[128,3072]{1,0:T(8,128)(2,1)S(1)} %copy-done.2, bf16[128,3072]{1,0:T(8,128)(2,1)S(1)} %copy-done, ...), custom_call_target="tpu_custom_call" | custom-call | flops 1006632960 | bytes 16777216 | tf_op jit(solution)/shard_map/pallas_call | solution.py:218
  160.6 4.8 %all-to-all-start.2 = ((bf16[16,9,64,256]{3,2,1,0:T(8,128)(2,1)}), bf16[16,9,64,256]{3,2,1,0:T(8,128)(2,1)}, u32[]{:S(2)}, u32[]{:S(2)}) async-start(bf16[16,9,64,256]{3,2,1,0:T(8,128)(2,1)} %bitcast.16), calls=%async_computation.2 | async-start | bytes 9437184 | tf_op jit(solution)/shard_map/all_to_all | solution.py:248
  165.4 8.2 %shard_map.78 = (bf16[128,3072]{1,0:T(8,128)(2,1)S(1)}, f32[128,3072]{1,0:T(8,128)}, f32[128,3072]{1,0:T(8,128)}, bf16[64,3072]{1,0:T(8,128)(2,1)S(1)}, bf16[64,...) custom-call(s32[96]{0:T(128)S(1)} %multiply_add_fusion.slots, ...), custom_call_target="tpu_custom_call" | custom-call | flops 1006632960 | bytes 16777216 | tf_op jit(solution)/shard_map/pallas_call | solution.py:234
  173.6 0.9 copy-done.11
  174.5 0.7 copy-done.12
  175.2 2.0 collective-permute-start.6
  177.3 4.4 %collective-permute-start.7 = (bf16[64,3072]{1,0:T(8,128)(2,1)}, bf16[64,3072]{1,0:T(8,128)(2,1)S(1)}, u32[]{:S(2)}, u32[]{:S(2)}) collective-permute-start(bf16[64,3072]{1,0:T(8,128)(2,1)} %get-tuple-element.30), channel_id=1, source_target_pairs={{2,0},{4,2},{6,4},{8,6},{10,8},{12,10},{14,12},{16,14},{18,16},{20... | collective-permute-start | bytes 1179656 | tf_op jit(solution)/shard_map/ppermute | solution.py:146
  181.8 1.9 collective-permute-start.3
  183.7 4.5 %collective-permute-start.4 = (bf16[64,3072]{1,0:T(8,128)(2,1)S(1)}, bf16[64,3072]{1,0:T(8,128)(2,1)S(1)}, u32[]{:S(2)}, u32[]{:S(2)}) collective-permute-start(bf16[64,3072]{1,0:T(8,128)(2,1)S(1)} %get-tuple-element.26), channel_id=1, source_target_pairs={{2,0},{4,2},{6,4},{8,6},{10,8},{12,10},{14,12},{16,14},{18,16},{20... | collective-permute-start | bytes 1179656 | tf_op jit(solution)/shard_map/ppermute | solution.py:146
  188.2 0.1 broadcast.179.clone
  188.3 1.2 constant_dynamic-slice_fusion.1
  189.5 1.6 collective-permute-start.2
  191.1 82.4 %collective-permute-done.6.above_ref = bf16[64,3072]{1,0:T(8,128)(2,1)S(1)} collective-permute-done((bf16[64,3072]{1,0:T(8,128)(2,1)}, bf16[64,3072]{1,0:T(8,128)(2,1)S(1)}, u32[]{:S(2)}, u32[]{:S(2)}) %collective-permute-start.6) | collective-permute-done | bytes 393248 | tf_op jit(solution)/shard_map/ppermute | solution.py:146
  273.4 0.0 collective-permute-done.7.below_ref
  273.5 0.0 all-to-all-done.2
  273.5 1.4 copy-done.10
  274.9 4.2 %shard_map.80 = bf16[128,3072]{1,0:T(8,128)(2,1)S(1)} custom-call(s32[144]{0:T(256)S(1)} %reshape.155.codes, f32[128,3072]{1,0:T(8,128)S(1)} %copy-done.10, bf16[64,3072]{1,0:T(8,128)(2,1)S(1)} %collective-permute-done.6.above_ref, bf16[64,3072]{1,0:T(8,128)(2,1)S(1)} %collective-permute-done.7.below_ref, bf16[144,64,256]{2,1,0:T(8,128)(2,1)} %bitcast.10.in_ref), custom_call_target="tpu_custom_call" | custom-call | bytes 8388608 | tf_op jit(solution)/shard_map/pallas_call | solution.py:254
  279.1 0.1 broadcast.179.clone.2
  279.1 0.1 constant_dynamic-slice_fusion.2
  279.2 1.6 collective-permute-start.8
  280.8 0.0 collective-permute-done.3.above_ref
  280.8 0.0 collective-permute-done.4.below_ref
  280.8 4.1 %shard_map.79 = bf16[128,3072]{1,0:T(8,128)(2,1)S(1)} custom-call(s32[144]{0:T(256)S(1)} %reshape.155.codes, f32[128,3072]{1,0:T(8,128)S(1)} %copy-done.9, bf16[64,3072]{1,0:T(8,128)(2,1)S(1)} %collective-permute-done.3.above_ref, bf16[64,3072]{1,0:T(8,128)(2,1)S(1)} %collective-permute-done.4.below_ref, bf16[144,64,256]{2,1,0:T(8,128)(2,1)} %bitcast.10.in_ref), custom_call_target="tpu_custom_call" | custom-call | bytes 8388608 | tf_op jit(solution)/shard_map/pallas_call | solution.py:254
  284.9 0.1 broadcast.179.clone.1
  285.0 0.1 constant_dynamic-slice_fusion
  285.0 0.6 collective-permute-start.5
  285.6 0.0 collective-permute-done.2
  285.7 0.0 copy-start.14
  285.7 5.5 %collective-permute-done.8 = bf16[64,3072]{1,0:T(8,128)(2,1)S(1)} collective-permute-done((bf16[64,3072]{1,0:T(8,128)(2,1)S(1)}, bf16[64,3072]{1,0:T(8,128)(2,1)S(1)}, u32[]{:S(2)}, u32[]{:S(2)}) %collective-permute-start.8) | collective-permute-done | bytes 393248 | tf_op jit(solution)/shard_map/ppermute | solution.py:157
  291.2 0.0 copy-start.15
  291.2 4.2 %collective-permute-done.5 = bf16[64,3072]{1,0:T(8,128)(2,1)S(1)} collective-permute-done((bf16[64,3072]{1,0:T(8,128)(2,1)S(1)}, bf16[64,3072]{1,0:T(8,128)(2,1)S(1)}, u32[]{:S(2)}, u32[]{:S(2)}) %collective-permute-start.5) | collective-permute-done | bytes 393248 | tf_op jit(solution)/shard_map/ppermute | solution.py:157
  295.5 0.0 copy-done.14
  295.5 0.0 copy-done.15
  295.5 0.0 copy-start.13
  295.6 0.9 copy-done.13
  (22 shorter events, 0.1 us)
Async XLA Ops:
  0.6 25.9 %copy-start = (bf16[128,3072]{1,0:T(8,128)(2,1)S(1)}, bf16[128,3072]{1,0:T(8,128)(2,1)}, u32[]{:S(2)}) copy-start(bf16[128,3072]{1,0:T(8,128)(2,1)} %k_ref.5) | copy-start | bytes 2359300
  0.6 25.9 %copy-start.1 = (bf16[128,3072]{1,0:T(8,128)(2,1)S(1)}, bf16[128,3072]{1,0:T(8,128)(2,1)}, u32[]{:S(2)}) copy-start(bf16[128,3072]{1,0:T(8,128)(2,1)} %v_ref.3) | copy-start | bytes 2359300
  0.7 8.2 %copy-start.16 = (s32[2,24,2]{1,2,0:T(2,128)S(1)}, s32[2,24,2]{1,2,0:T(2,128)}, u32[]{:S(2)}) copy-start(s32[2,24,2]{1,2,0:T(2,128)} %param.9) | copy-start | bytes 1156
  3.2 23.3 %collective-permute-start.1 = (bf16[2,64,3072]{2,1,0:T(8,128)(2,1)}, bf16[2,64,3072]{2,1,0:T(8,128)(2,1)S(1)}, u32[]{:S(2)}, u32[]{:S(2)}) collective-permute-start(bf16[2,64,3072]{2,1,0:T(8,128)(2,1)} %pad_maximum_fusion.1), channel_id=1, source_target_pairs={{2,0},{4,2},{6,4},{8,6},{10,8},{12,10},{14,12},{16,14},{18,16},{20... | collective-permute-start | bytes 2359304 | tf_op jit(solution)/shard_map/ppermute | solution.py:146
  6.9 19.7 %collective-permute-start = (bf16[2,64,3072]{2,1,0:T(8,128)(2,1)}, bf16[2,64,3072]{2,1,0:T(8,128)(2,1)S(1)}, u32[]{:S(2)}, u32[]{:S(2)}) collective-permute-start(bf16[2,64,3072]{2,1,0:T(8,128)(2,1)} %pad_maximum_fusion), channel_id=1, source_target_pairs={{0,2},{2,4},{4,6},{6,8},{8,10},{10,12},{12,14},{14,16},{16,18},{18... | collective-permute-start | bytes 2359304 | tf_op jit(solution)/shard_map/ppermute | solution.py:146
  26.5 7.2 %copy-start.4 = (bf16[2,64,3072]{2,1,0:T(8,128)(2,1)}, bf16[2,64,3072]{2,1,0:T(8,128)(2,1)S(1)}, u32[]{:S(2)}) copy-start(bf16[2,64,3072]{2,1,0:T(8,128)(2,1)S(1)} %collective-permute-done.1.down_ref) | copy-start | bytes 2359300
  26.6 7.1 %copy-start.6 = (bf16[2,64,3072]{2,1,0:T(8,128)(2,1)}, bf16[2,64,3072]{2,1,0:T(8,128)(2,1)S(1)}, u32[]{:S(2)}) copy-start(bf16[2,64,3072]{2,1,0:T(8,128)(2,1)S(1)} %collective-permute-done.up_ref) | copy-start | bytes 2359300
  33.7 110.2 %copy-start.2 = (bf16[128,3072]{1,0:T(8,128)(2,1)S(1)}, bf16[128,3072]{1,0:T(8,128)(2,1)}, u32[]{:S(2)}) copy-start(bf16[128,3072]{1,0:T(8,128)(2,1)} %q_ref.3) | copy-start | bytes 2359300
  33.7 110.2 %copy-start.3 = (bf16[128,3072]{1,0:T(8,128)(2,1)S(1)}, bf16[128,3072]{1,0:T(8,128)(2,1)}, u32[]{:S(2)}) copy-start(bf16[128,3072]{1,0:T(8,128)(2,1)} %g_ref.3) | copy-start | bytes 2359300
  33.7 110.2 %all-to-all-start.1 = ((bf16[16,9,64,256]{3,2,1,0:T(8,128)(2,1)}), bf16[16,9,64,256]{3,2,1,0:T(8,128)(2,1)}, u32[]{:S(2)}, u32[]{:S(2)}) async-start(bf16[16,9,64,256]{3,2,1,0:T(8,128)(2,1)} %bitcast.15), calls=%async_computation.1 | async-start | bytes 9437184 | tf_op jit(solution)/shard_map/all_to_all | solution.py:202
  143.9 1.1 copy-start.5
  145.0 1.1 copy-start.7
  160.6 4.8 %copy-start.8 = (bf16[2,64,3072]{2,1,0:T(8,128)(2,1)S(1)}, bf16[2,64,3072]{2,1,0:T(8,128)(2,1)}, u32[]{:S(2)}) copy-start(bf16[2,64,3072]{2,1,0:T(8,128)(2,1)} %copy-done.6) | copy-start | bytes 2359300
  160.6 112.9 %all-to-all-start.2 = ((bf16[16,9,64,256]{3,2,1,0:T(8,128)(2,1)}), bf16[16,9,64,256]{3,2,1,0:T(8,128)(2,1)}, u32[]{:S(2)}, u32[]{:S(2)}) async-start(bf16[16,9,64,256]{3,2,1,0:T(8,128)(2,1)} %bitcast.16), calls=%async_computation.2 | async-start | bytes 9437184 | tf_op jit(solution)/shard_map/all_to_all | solution.py:248
  173.6 0.9 copy-start.11
  174.5 0.7 copy-start.12
  175.2 98.2 %collective-permute-start.6 = (bf16[64,3072]{1,0:T(8,128)(2,1)}, bf16[64,3072]{1,0:T(8,128)(2,1)S(1)}, u32[]{:S(2)}, u32[]{:S(2)}) collective-permute-start(bf16[64,3072]{1,0:T(8,128)(2,1)} %get-tuple-element.29), channel_id=1, source_target_pairs={{0,2},{2,4},{4,6},{6,8},{8,10},{10,12},{12,14},{14,16},{16,18},{18... | collective-permute-start | bytes 1179656 | tf_op jit(solution)/shard_map/ppermute | solution.py:146
  177.3 96.2 %collective-permute-start.7 = (bf16[64,3072]{1,0:T(8,128)(2,1)}, bf16[64,3072]{1,0:T(8,128)(2,1)S(1)}, u32[]{:S(2)}, u32[]{:S(2)}) collective-permute-start(bf16[64,3072]{1,0:T(8,128)(2,1)} %get-tuple-element.30), channel_id=1, source_target_pairs={{2,0},{4,2},{6,4},{8,6},{10,8},{12,10},{14,12},{16,14},{18,16},{20... | collective-permute-start | bytes 1179656 | tf_op jit(solution)/shard_map/ppermute | solution.py:146
  181.8 99.0 %collective-permute-start.3 = (bf16[64,3072]{1,0:T(8,128)(2,1)}, bf16[64,3072]{1,0:T(8,128)(2,1)S(1)}, u32[]{:S(2)}, u32[]{:S(2)}) collective-permute-start(bf16[64,3072]{1,0:T(8,128)(2,1)} %copy-done.12), channel_id=1, source_target_pairs={{0,2},{2,4},{4,6},{6,8},{8,10},{10,12},{12,14},{14,16},{16,18},{18... | collective-permute-start | bytes 1179656 | tf_op jit(solution)/shard_map/ppermute | solution.py:146
  183.7 97.1 %collective-permute-start.4 = (bf16[64,3072]{1,0:T(8,128)(2,1)S(1)}, bf16[64,3072]{1,0:T(8,128)(2,1)S(1)}, u32[]{:S(2)}, u32[]{:S(2)}) collective-permute-start(bf16[64,3072]{1,0:T(8,128)(2,1)S(1)} %get-tuple-element.26), channel_id=1, source_target_pairs={{2,0},{4,2},{6,4},{8,6},{10,8},{12,10},{14,12},{16,14},{18,16},{20... | collective-permute-start | bytes 1179656 | tf_op jit(solution)/shard_map/ppermute | solution.py:146
  189.5 96.1 %collective-permute-start.2 = (bf16[64,3072]{1,0:T(8,128)(2,1)S(1)}, bf16[64,3072]{1,0:T(8,128)(2,1)S(1)}, u32[]{:S(2)}, u32[]{:S(2)}) collective-permute-start(bf16[64,3072]{1,0:T(8,128)(2,1)S(1)} %get-tuple-element.35), channel_id=1, source_target_pairs={{0,1},{1,0},{2,3},{3,2},{4,5},{5,4},{6,7},{7,6},{8,9},{9,8},{10,11... | collective-permute-start | bytes 1179656 | tf_op jit(solution)/shard_map/ppermute | solution.py:157
  273.5 1.4 copy-start.10
  274.9 5.9 %copy-start.9 = (f32[128,3072]{1,0:T(8,128)S(1)}, f32[128,3072]{1,0:T(8,128)}, u32[]{:S(2)}) copy-start(f32[128,3072]{1,0:T(8,128)} %get-tuple-element.24.own_ref) | copy-start | bytes 4718596
  279.2 12.0 %collective-permute-start.8 = (bf16[64,3072]{1,0:T(8,128)(2,1)S(1)}, bf16[64,3072]{1,0:T(8,128)(2,1)S(1)}, u32[]{:S(2)}, u32[]{:S(2)}) collective-permute-start(bf16[64,3072]{1,0:T(8,128)(2,1)S(1)} %get-tuple-element.31), channel_id=1, source_target_pairs={{0,1},{1,0},{2,3},{3,2},{4,5},{5,4},{6,7},{7,6},{8,9},{9,8},{10,11... | collective-permute-start | bytes 1179656 | tf_op jit(solution)/shard_map/ppermute | solution.py:157
  285.0 10.4 %collective-permute-start.5 = (bf16[64,3072]{1,0:T(8,128)(2,1)S(1)}, bf16[64,3072]{1,0:T(8,128)(2,1)S(1)}, u32[]{:S(2)}, u32[]{:S(2)}) collective-permute-start(bf16[64,3072]{1,0:T(8,128)(2,1)S(1)} %get-tuple-element.33), channel_id=1, source_target_pairs={{0,1},{1,0},{2,3},{3,2},{4,5},{5,4},{6,7},{7,6},{8,9},{9,8},{10,11... | collective-permute-start | bytes 1179656 | tf_op jit(solution)/shard_map/ppermute | solution.py:157
  285.7 9.9 %copy-start.14 = (bf16[64,6144]{1,0:T(8,128)(2,1)}, bf16[64,6144]{1,0:T(8,128)(2,1)S(1)}, u32[]{:S(2)}) copy-start(bf16[64,6144]{1,0:T(8,128)(2,1)S(1)} %constant_dynamic-update-slice_fusion.2) | copy-start | bytes 2359300
  291.2 4.3 %copy-start.15 = (bf16[64,6144]{1,0:T(8,128)(2,1)}, bf16[64,6144]{1,0:T(8,128)(2,1)S(1)}, u32[]{:S(2)}) copy-start(bf16[64,6144]{1,0:T(8,128)(2,1)S(1)} %constant_dynamic-update-slice_fusion.1) | copy-start | bytes 2359300
  295.5 0.9 copy-start.13
